TPU v7x, 32 devices: a whole 2x2x4 slice. The times are simulated.
32 devices in a mesh: dp: 4 (over z), fsdp: 8 (over y, x, core).
Axes of the slice: x: 2, y: 2, z: 4, core: 2. Of those that a mesh axis runs over, the one named last changes fastest.
Arguments:
- tokens: bfloat16 [32, 1024, 1024], P(('dp', 'fsdp')), may hold values from -6 to 6
- lengths: int32 [32], P(('dp', 'fsdp')), may hold values from 64 to 1024, as said below
- cotangent: bfloat16 [32, 1024, 1024], P(('dp', 'fsdp')), may hold values from -6 to 6
- gain_one: float32 [1024], replicated, may hold values from 0.5 to 1.5
- shift_one: float32 [1024], replicated, may hold values from -1 to 1
- gain_two: float32 [1024], replicated, may hold values from 0.5 to 1.5
- shift_two: float32 [1024], replicated, may hold values from -1 to 1
- w_qkv: bfloat16 [1024, 3072], P('fsdp'), may hold values from -0.25 to 0.25
- w_proj: bfloat16 [1024, 1024], P('fsdp'), may hold values from -0.75 to 0.75
- w_fc: bfloat16 [1024, 4096], P('fsdp'), may hold values from -0.1875 to 0.1875
- w_out: bfloat16 [4096, 1024], P('fsdp'), may hold values from -0.125 to 0.125
- query_down_factor: float32 [1024, 4], replicated, may hold values from -0.1875 to 0.1875
- query_up_factor: float32 [4, 1024], replicated, may hold values from -0.3 to 0.3
- value_down_factor: float32 [1024, 4], replicated, may hold values from -0.1875 to 0.1875
- value_up_factor: float32 [4, 1024], replicated, may hold values from -0.3 to 0.3
Outputs:
- block_out: bfloat16 [32, 1024, 1024], P(('dp', 'fsdp'))
- grad_tokens: bfloat16 [32, 1024, 1024], P(('dp', 'fsdp'))
- grad_a_query: float32 [1024, 4], replicated
- query_up_gradient: float32 [4, 1024], replicated
- grad_a_value: float32 [1024, 4], replicated
- value_up_gradient: float32 [4, 1024], replicated
Inputs may be any that keep to these rules, and one draw needn't show every extreme that they name: `lengths`: number of real tokens of each sequence; positions from it up to 1023 are padding.
All inputs are finite; a program needn't handle non-finite values.
Results may differ from a plain program's by a relative error of at most 0.015.
The roundings to bfloat16 on the way count: a program that leaves them out, or rounds other values in their place, can miss the bound.
Values may be sent and summed in bfloat16 or wider, within the bound.
No kernel may reach another device: no remote copies, remote signals or barrier semaphores. Data moves between devices by JAX's collectives and lax.ppermute only.
A program may use at most 256 MiB of HBM per device.

v0:
```python
import math

import jax
import jax.numpy as jnp
from jax import lax
from jax.sharding import PartitionSpec as P

HD = 64


adapter_scale_factor = 8.0
norm_eps = 1e-05
neg_big = -1e30


def layer_norm(values, gain, shift):
    center = values - jnp.mean(values, axis=-1, keepdims=True)
    spread = jnp.mean(center * center, axis=-1, keepdims=True)
    return center * lax.rsqrt(spread + norm_eps) * gain + shift


def gelu_tanh(values):
    return jax.nn.gelu(values, approximate=True)


def block_scores(q_part, k_part, row_start, length, score_scale):
    raw_scores = (
        jnp.einsum("qhd,khd->hqk", q_part, k_part, preferred_element_type=jnp.float32) * score_scale
    )
    q_pos = row_start + jnp.arange(q_part.shape[0], dtype=jnp.int32)[:, None]
    k_pos = jnp.arange(k_part.shape[0], dtype=jnp.int32)[None, :]
    allowed = (k_pos <= q_pos) & (k_pos < length)
    return jnp.where(allowed[None], raw_scores, neg_big)


def attention_forward(q_row, k_row, v_row, length, block_rows, head_group, score_scale):
    seq_len, head_count = (q_row.shape[0], q_row.shape[1])
    out_blocks = []
    lse_blocks = []
    for row_start in range(0, seq_len, block_rows):
        key_len = row_start + block_rows
        head_parts = []
        lse_parts = []
        for head_start in range(0, head_count, head_group):
            head_slice = slice(head_start, head_start + head_group)
            q_part = q_row[row_start:key_len, head_slice]
            k_part = k_row[:key_len, head_slice]
            v_part = v_row[:key_len, head_slice]
            scores = block_scores(q_part, k_part, row_start, length, score_scale)
            row_top = jnp.max(scores, axis=-1, keepdims=True)
            exp_scores = jnp.exp(scores - row_top)
            row_total = jnp.sum(exp_scores, axis=-1, keepdims=True)
            prob_low = (exp_scores / row_total).astype(jnp.bfloat16)
            head_parts.append(
                jnp.einsum("hqk,khd->qhd", prob_low, v_part, preferred_element_type=jnp.float32)
            )
            lse_parts.append(row_top + jnp.log(row_total))
        out_blocks.append(jnp.concatenate(head_parts, axis=1))
        lse_blocks.append(lse_parts)
    return (jnp.concatenate(out_blocks, axis=0), lse_blocks)


def attention_backward(
    q_row, k_row, v_row, grad_row, lse_blocks, length, block_rows, head_group, score_scale
):
    seq_len, head_count = (q_row.shape[0], q_row.shape[1])
    grad_q_blocks = []
    grad_k = jnp.zeros(q_row.shape, jnp.float32)
    grad_v = jnp.zeros(q_row.shape, jnp.float32)
    for block_index, row_start in enumerate(range(0, seq_len, block_rows)):
        key_len = row_start + block_rows
        q_parts = []
        k_parts = []
        v_parts = []
        for group_index, head_start in enumerate(range(0, head_count, head_group)):
            head_slice = slice(head_start, head_start + head_group)
            q_part = q_row[row_start:key_len, head_slice]
            k_part = k_row[:key_len, head_slice]
            v_part = v_row[:key_len, head_slice]
            grad_part = grad_row[row_start:key_len, head_slice]
            scores = block_scores(q_part, k_part, row_start, length, score_scale)
            attn_probs = jnp.exp(scores - lse_blocks[block_index][group_index])
            prob_low = attn_probs.astype(jnp.bfloat16)
            grad_probs = jnp.einsum(
                "qhd,khd->hqk", grad_part, v_part, preferred_element_type=jnp.float32
            )
            row_dot = jnp.sum(attn_probs * grad_probs, axis=-1, keepdims=True)
            grad_scores = (attn_probs * (grad_probs - row_dot)).astype(jnp.bfloat16)
            q_parts.append(
                jnp.einsum("hqk,khd->qhd", grad_scores, k_part, preferred_element_type=jnp.float32)
                * score_scale
            )
            k_parts.append(
                jnp.einsum("hqk,qhd->khd", grad_scores, q_part, preferred_element_type=jnp.float32)
                * score_scale
            )
            v_parts.append(
                jnp.einsum("hqk,qhd->khd", prob_low, grad_part, preferred_element_type=jnp.float32)
            )
        grad_q_blocks.append(jnp.concatenate(q_parts, axis=1))
        grad_k = grad_k.at[:key_len].add(jnp.concatenate(k_parts, axis=1))
        grad_v = grad_v.at[:key_len].add(jnp.concatenate(v_parts, axis=1))
    return (jnp.concatenate(grad_q_blocks, axis=0), grad_k, grad_v)


def local(
    tokens,
    lengths,
    cotangent,
    gain_one,
    shift_one,
    gain_two,
    shift_two,
    w_qkv,
    w_proj,
    w_fc,
    w_out,
    query_down_factor,
    query_up_factor,
    value_down_factor,
    value_up_factor,
):
    rows_here, seq_len, embedding_width = tokens.shape
    head_dim = HD
    head_count = embedding_width // head_dim
    rank_size = query_down_factor.shape[1]
    score_scale = 1.0 / math.sqrt(head_dim)
    block_rows = min(512, seq_len)
    head_group = min(head_count, 8)
    token_count = rows_here * seq_len
    qkv_full, proj_full = (
        lax.all_gather(w_qkv, "fsdp", axis=0, tiled=True),
        lax.all_gather(w_proj, "fsdp", axis=0, tiled=True),
    )

    def norm_one(values):
        return layer_norm(values, gain_one, shift_one)

    def norm_two(values):
        return layer_norm(values, gain_two, shift_two)

    adapter_down_project = jnp.concatenate([query_down_factor, value_down_factor], axis=1).astype(
        jnp.bfloat16
    )
    query_up_low = query_up_factor.astype(jnp.bfloat16)
    value_up_low = value_up_factor.astype(jnp.bfloat16)
    flat_in = tokens.reshape(token_count, embedding_width).astype(jnp.float32)
    normed_one, norm_one_pull = jax.vjp(norm_one, flat_in)
    normalized_narrow_product = normed_one.astype(jnp.bfloat16)
    combined_projection_weight = jnp.dot(
        normalized_narrow_product, qkv_full, preferred_element_type=jnp.float32
    )
    joint_narrow_product = jnp.dot(
        normalized_narrow_product, adapter_down_project, preferred_element_type=jnp.float32
    ).astype(jnp.bfloat16)
    query_narrow_product = joint_narrow_product[:, :rank_size]
    value_narrow_product = joint_narrow_product[:, rank_size:]
    query_rows = combined_projection_weight[:, :embedding_width] + adapter_scale_factor * jnp.dot(
        query_narrow_product, query_up_low, preferred_element_type=jnp.float32
    )
    keys_all = combined_projection_weight[:, embedding_width : 2 * embedding_width]
    value_rows_complete = combined_projection_weight[
        :, 2 * embedding_width :
    ] + adapter_scale_factor * jnp.dot(
        value_narrow_product, value_up_low, preferred_element_type=jnp.float32
    )
    head_shape = (rows_here, seq_len, head_count, head_dim)
    q_low = query_rows.astype(jnp.bfloat16).reshape(head_shape)
    k_low = keys_all.astype(jnp.bfloat16).reshape(head_shape)
    v_low = value_rows_complete.astype(jnp.bfloat16).reshape(head_shape)
    row_index = 0
    row_out, row_lse = attention_forward(
        q_low[row_index],
        k_low[row_index],
        v_low[row_index],
        lengths[row_index],
        block_rows,
        head_group,
        score_scale,
    )
    attended_rows = [row_out]
    lse_rows = [row_lse]
    attended_low = (
        jnp.stack(attended_rows).reshape(token_count, embedding_width).astype(jnp.bfloat16)
    )
    hidden = flat_in + jnp.dot(attended_low, proj_full, preferred_element_type=jnp.float32)
    fc_full, out_full = (
        lax.all_gather(w_fc, "fsdp", axis=0, tiled=True),
        lax.all_gather(w_out, "fsdp", axis=0, tiled=True),
    )
    normed_two, norm_two_pull = jax.vjp(norm_two, hidden)
    normed_two_low = normed_two.astype(jnp.bfloat16)
    pre_act = jnp.dot(normed_two_low, fc_full, preferred_element_type=jnp.float32)
    activated, gelu_pull = jax.vjp(gelu_tanh, pre_act)
    mlp_out = jnp.dot(activated.astype(jnp.bfloat16), out_full, preferred_element_type=jnp.float32)
    positions = jnp.arange(seq_len, dtype=jnp.int32)
    row_mask = (positions[None, :] < lengths[:, None]).astype(jnp.float32).reshape(token_count, 1)
    block_out = (
        (row_mask * (hidden + mlp_out))
        .astype(jnp.bfloat16)
        .reshape(rows_here, seq_len, embedding_width)
    )
    qkv_back, proj_back = (
        lax.all_gather(w_qkv, "fsdp", axis=0, tiled=True),
        lax.all_gather(w_proj, "fsdp", axis=0, tiled=True),
    )
    fc_back, out_back = (
        lax.all_gather(w_fc, "fsdp", axis=0, tiled=True),
        lax.all_gather(w_out, "fsdp", axis=0, tiled=True),
    )
    grad_out = row_mask * cotangent.reshape(token_count, embedding_width).astype(jnp.float32)
    grad_act = jnp.dot(
        grad_out.astype(jnp.bfloat16), out_back.T, preferred_element_type=jnp.float32
    )
    grad_pre = gelu_pull(grad_act)[0].astype(jnp.bfloat16)
    grad_normed_two = jnp.dot(grad_pre, fc_back.T, preferred_element_type=jnp.float32)
    grad_hidden = grad_out + norm_two_pull(grad_normed_two)[0]
    grad_attended = jnp.dot(
        grad_hidden.astype(jnp.bfloat16), proj_back.T, preferred_element_type=jnp.float32
    )
    grad_att_low = grad_attended.astype(jnp.bfloat16).reshape(head_shape)
    row_index = 0
    grad_q_row, grad_k_row, grad_v_row = attention_backward(
        q_low[row_index],
        k_low[row_index],
        v_low[row_index],
        grad_att_low[row_index],
        lse_rows[row_index],
        lengths[row_index],
        block_rows,
        head_group,
        score_scale,
    )
    grad_q_rows = [grad_q_row]
    grad_k_rows = [grad_k_row]
    grad_v_rows = [grad_v_row]
    grad_queries = jnp.stack(grad_q_rows).reshape(token_count, embedding_width).astype(jnp.bfloat16)
    grad_keys = jnp.stack(grad_k_rows).reshape(token_count, embedding_width).astype(jnp.bfloat16)
    grad_values = jnp.stack(grad_v_rows).reshape(token_count, embedding_width).astype(jnp.bfloat16)
    grad_merged = jnp.concatenate([grad_queries, grad_keys, grad_values], axis=1)
    query_narrow_gradient = adapter_scale_factor * jnp.dot(
        grad_queries, query_up_low.T, preferred_element_type=jnp.float32
    )
    value_narrow_gradient = adapter_scale_factor * jnp.dot(
        grad_values, value_up_low.T, preferred_element_type=jnp.float32
    )
    joint_narrow_gradient = jnp.concatenate(
        [query_narrow_gradient, value_narrow_gradient], axis=1
    ).astype(jnp.bfloat16)
    normalized_input_gradient = jnp.dot(grad_merged, qkv_back.T, preferred_element_type=jnp.float32)
    normalized_input_gradient = normalized_input_gradient + jnp.dot(
        joint_narrow_gradient, adapter_down_project.T, preferred_element_type=jnp.float32
    )
    grad_flat = grad_hidden + norm_one_pull(normalized_input_gradient)[0]
    grad_tokens = grad_flat.astype(jnp.bfloat16).reshape(rows_here, seq_len, embedding_width)
    grad_down_both = jnp.dot(
        normalized_narrow_product.T, joint_narrow_gradient, preferred_element_type=jnp.float32
    )
    query_up_gradient = adapter_scale_factor * jnp.dot(
        query_narrow_product.T, grad_queries, preferred_element_type=jnp.float32
    )
    value_up_gradient = adapter_scale_factor * jnp.dot(
        value_narrow_product.T, grad_values, preferred_element_type=jnp.float32
    )
    summed = lax.psum(
        (
            grad_down_both[:, :rank_size],
            query_up_gradient,
            grad_down_both[:, rank_size:],
            value_up_gradient,
        ),
        ("dp", "fsdp"),
    )
    return (block_out, grad_tokens, summed[0], summed[1], summed[2], summed[3])


def solution(mesh):
    return jax.shard_map(
        local,
        mesh=mesh,
        in_specs=(
            P(("dp", "fsdp"), None, None),
            P(("dp", "fsdp")),
            P(("dp", "fsdp"), None, None),
            P(),
            P(),
            P(),
            P(),
            P("fsdp", None),
            P("fsdp", None),
            P("fsdp", None),
            P("fsdp", None),
            P(),
            P(),
            P(),
            P(),
        ),
        out_specs=(
            P(("dp", "fsdp"), None, None),
            P(("dp", "fsdp"), None, None),
            P(),
            P(),
            P(),
            P(),
        ),
        check_vma=False,
    )
```

profile of v0, /device:TPU:1, one launch (start us, length us, event | category | flops | bytes accessed | tf_op | source)
XLA Modules:
  0.0 502.6 jit_solution(17822238097688001023)
XLA Ops:
  23.8 34.2 %all-gather.5.cloned.1.call-done = bf16[1024,3072]{1,0:T(8,128)(2,1)} async-done(((bf16[128,3072]{1,0:T(8,128)(2,1)}), bf16[1024,3072]{1,0:T(8,128)(2,1)}) %all-gather.5.cloned.1.call-update) | async-done | bytes 6291472 | tf_op jit(solution)/shard_map/all_gather | solution.py:132
  57.9 9.7 %fusion.187 = f32[1024,3072]{1,0:T(8,128)S(1)} fusion(bf16[1024,1024]{0,1:T(8,128)(2,1)} %copy-done.5, bf16[1024,3072]{1,0:T(8,128)(2,1)} %all-gather.5.cloned.1.call-done), kind=kOutput, calls=%fused_computation.240 | convolution fusion | flops 6442450944 | bytes 20971520 | tf_op jit(solution)/shard_map/dot_general | solution.py:150
  67.6 4.6 copy-done.15
  82.2 6.4 %fusion.182 = (f32[8,512]{1,0:T(8,128)S(1)}, f32[8,512,512]{1,2,0:T(8,128)}) fusion(bf16[1024,16,64]{0,2,1:T(8,128)(2,1)} %bitcast.150, bf16[1024,16,64]{0,2,1:T(8,128)(2,1)S(1)} %bitcast.136, pred[512,512]{0,1:T(8,128)(4,1)S(1)} %fusion.125), kind=kOutput, calls=%fused_computation.237 | convolution fusion | flops 274722816 | bytes 9715712 | tf_op jit(solution)/shard_map/qhd,khd->hqk/dot_general | solution.py:28
  88.7 4.9 fusion.183
  93.5 8.4 %fusion.180 = (f32[8,512]{1,0:T(8,128)S(1)}, f32[8,512,1024]{2,1,0:T(8,128)}) fusion(bf16[1024,16,64]{0,2,1:T(8,128)(2,1)S(1)} %bitcast.156, bf16[1024,16,64]{0,2,1:T(8,128)(2,1)S(1)} %bitcast.138, pred[512,1024]{1,0:T(8,128)(4,1)S(1)} %fusion.82), kind=kOutput, calls=%fused_computation.235 | convolution fusion | flops 549449728 | bytes 18890752 | tf_op jit(solution)/shard_map/qhd,khd->hqk/dot_general | solution.py:28
  101.9 7.6 %fusion.181 = (f32[8,512]{1,0:T(8,128)S(1)}, f32[8,512,1024]{2,1,0:T(8,128)}) fusion(bf16[1024,16,64]{0,2,1:T(8,128)(2,1)S(1)} %bitcast.157, bf16[1024,16,64]{0,2,1:T(8,128)(2,1)S(1)} %bitcast.139, pred[512,1024]{1,0:T(8,128)(4,1)S(1)} %fusion.82), kind=kOutput, calls=%fused_computation.236 | convolution fusion | flops 549449728 | bytes 18890752 | tf_op jit(solution)/shard_map/qhd,khd->hqk/dot_general | solution.py:28
  115.1 5.6 %fusion.23 = f32[8,512]{1,0:T(8,128)S(1)} fusion(f32[8,512,512]{1,2,0:T(8,128)} %get-tuple-element.95, f32[8,512]{1,0:T(8,128)S(1)} %get-tuple-element.94), kind=kLoop, calls=%fused_computation.47 | loop fusion | flops 4190208 | bytes 8421376 | tf_op jit(solution)/shard_map/reduce_sum | solution.py:52
  120.7 5.2 %fusion.22 = f32[8,512]{1,0:T(8,128)S(1)} fusion(f32[8,512,512]{1,2,0:T(8,128)} %get-tuple-element.97, f32[8,512]{1,0:T(8,128)S(1)} %get-tuple-element.96), kind=kLoop, calls=%fused_computation.46 | loop fusion | flops 4190208 | bytes 8421376 | tf_op jit(solution)/shard_map/reduce_sum | solution.py:52
  125.9 9.9 %fusion.8 = f32[8,512]{1,0:T(8,128)} fusion(f32[8,512,1024]{2,1,0:T(8,128)} %get-tuple-element.91, f32[8,512]{1,0:T(8,128)S(1)} %get-tuple-element.90), kind=kLoop, calls=%fused_computation.23 | loop fusion | flops 8384512 | bytes 16809984 | tf_op jit(solution)/shard_map/reduce_sum | solution.py:52
  144.5 8.0 %fusion.112 = bf16[512,8,64]{0,2,1:T(8,128)(2,1)S(1)} fusion(bf16[1024,16,64]{0,2,1:T(8,128)(2,1)} %bitcast.158, f32[8,512,1024]{2,1,0:T(8,128)} %get-tuple-element.91, f32[8,512]{1,0:T(8,128)} %fusion.8, f32[8,512]{1,0:T(8,128)S(1)} %get-tuple-element.90), kind=kOutput, calls=%fused_computation.144 | convolution fusion | flops 549715968 | bytes 19431424 | tf_op jit(solution)/shard_map/hqk,khd->qhd/dot_general | solution.py:55
  158.2 4.9 fusion.184
  167.4 17.0 %fusion.62 = f32[1024,4096]{1,0:T(8,128)} fusion(bf16[1024,4096]{1,0:T(8,128)(2,1)} %all-gather.9.cloned.1.call-done, f32[1024,1024]{0,1:T(8,128)} %copy-done.10, f32[1024]{0:T(1024)S(1)} %copy-done.58, f32[1024]{0:T(1024)S(1)} %copy-done.56, f32[1024]{0:T(1024)S(1)} %fusion.162, f32[1024]{0:T(1024)S(1)} %broadcast_multiply_fusion), kind=kOutput, calls=%fused_computation.100 | convolution fusion | flops 8595177472 | bytes 29376512 | tf_op jit(solution)/shard_map/dot_general | solution.py:193
  184.4 15.9 %all-gather.11.cloned.1.call-done = bf16[4096,1024]{1,0:T(8,128)(2,1)} async-done(((bf16[512,1024]{1,0:T(8,128)(2,1)}), bf16[4096,1024]{1,0:T(8,128)(2,1)}) %all-gather.11.cloned.1.call-update) | async-done | bytes 8388624 | tf_op jit(solution)/shard_map/all_gather | solution.py:189
  200.3 29.4 %multiply_reduce_fusion.4 = (f32[1024]{0:T(1024)S(1)}, f32[1024,1024]{0,1:T(8,128)}) fusion(f32[1024,1024]{0,1:T(8,128)} %copy-done.10, f32[1024]{0:T(1024)S(1)} %copy-done.56, f32[1024]{0:T(1024)S(1)} %broadcast_multiply_fusion, bf16[1024,4096]{1,0:T(8,128)(2,1)} %all-gather.9.cloned.1.call-done, f32[1024,4096]{1,0:T(8,128)} %fusion.62, ...), kind=kOutput, calls=%fused_computation.92 | convolution fusion | flops 17271095296 | bytes 44056576 | tf_op jit(solution)/shard_map/dot_general | solution.py:216
  229.7 4.7 fusion.178
  234.4 5.8 %fusion.84 = bf16[1024,1024]{0,1:T(8,128)(2,1)S(1)} fusion(bf16[1024,1024]{1,0:T(8,128)(2,1)} %all-gather.7.cloned.1.call-done, f32[1024,1024]{0,1:T(8,128)S(1)} %get-tuple-element.87, bf16[1,1024,1024]{1,2,0:T(8,128)(2,1)S(1)} %copy-done.18, f32[1024]{0:T(1024)S(1)} %negate_multiply_fusion.1, f32[1024]{0:T(1024)S(1)} %copy-done.53), kind=kOutput, calls=%fused_computation.120 | convolution fusion | flops 2153775104 | bytes 10493952 | tf_op jit(solution)/shard_map/dot_general | solution.py:218
  245.9 4.6 fusion.87
  250.5 7.3 %fusion.90 = f32[1024,8,64]{0,2,1:T(8,128)S(1)} fusion(f32[8,512,1024]{2,1,0:T(8,128)} %get-tuple-element.91, f32[8,512]{1,0:T(8,128)S(1)} %copy-done.29, bf16[1024,16,64]{0,2,1:T(8,128)(2,1)S(1)} %bitcast.172), kind=kOutput, calls=%fused_computation.122 | convolution fusion | flops 545259520 | bytes 19415040 | tf_op jit(solution)/shard_map/hqk,qhd->khd/dot_general | solution.py:98
  260.9 6.6 %multiply_reduce_fusion.2 = (f32[8,512]{1,0:T(8,128)S(1)}, f32[8,512,512]{1,2,0:T(8,128)}) fusion(f32[8,512,512]{1,2,0:T(8,128)} %get-tuple-element.95, f32[8,512]{1,0:T(8,128)S(1)} %copy-done.32, bf16[1024,16,64]{0,2,1:T(8,128)(2,1)} %bitcast.159, bf16[1024,16,64]{0,2,1:T(8,128)(2,1)S(1)} %bitcast.173), kind=kOutput, calls=%fused_computation.31 | convolution fusion | flops 274722816 | bytes 17858560 | tf_op jit(solution)/shard_map/qhd,khd->hqk/dot_general | solution.py:84
  267.5 6.8 %multiply_convert_fusion.3 = bf16[8,512,512]{1,2,0:T(8,128)(2,1)S(1)} fusion(f32[8,512,512]{1,2,0:T(8,128)} %get-tuple-element.103, f32[8,512,512]{1,2,0:T(8,128)} %get-tuple-element.95, f32[8,512]{1,0:T(8,128)S(1)} %get-tuple-element.102, f32[8,512]{1,0:T(8,128)S(1)} %copy-done.32), kind=kLoop, calls=%fused_computation.30 | loop fusion | flops 8388608 | bytes 21004288 | tf_op jit(solution)/shard_map/convert_element_type | solution.py:88
  279.9 6.3 %multiply_reduce_fusion.3 = (f32[8,512]{1,0:T(8,128)S(1)}, f32[8,512,512]{1,2,0:T(8,128)}) fusion(f32[8,512,512]{1,2,0:T(8,128)S(1)} %bitcast.131, f32[8,512]{1,0:T(8,128)S(1)} %copy-done.31, bf16[1024,16,64]{0,2,1:T(8,128)(2,1)} %bitcast.160, bf16[1024,16,64]{0,2,1:T(8,128)(2,1)} %bitcast.169), kind=kOutput, calls=%fused_computation.34 | convolution fusion | flops 274722816 | bytes 17858560 | tf_op jit(solution)/shard_map/qhd,khd->hqk/dot_general | solution.py:84
  286.2 4.5 multiply_convert_fusion.4
  296.7 12.3 %multiply_reduce_fusion = (f32[8,512]{1,0:T(8,128)}, f32[8,512,1024]{2,1,0:T(8,128)}) fusion(f32[8,512,1024]{2,1,0:T(8,128)} %get-tuple-element.91, f32[8,512]{1,0:T(8,128)} %log_add_fusion, bf16[1024,16,64]{0,2,1:T(8,128)(2,1)} %bitcast.161, bf16[1024,16,64]{0,2,1:T(8,128)(2,1)} %bitcast.170), kind=kOutput, calls=%fused_computation.10 | convolution fusion | flops 549449728 | bytes 35160064 | tf_op jit(solution)/shard_map/qhd,khd->hqk/dot_general | solution.py:84
  309.1 11.8 %multiply_convert_fusion = bf16[8,512,1024]{2,1,0:T(8,128)(2,1)S(1)} fusion(f32[8,512,1024]{2,1,0:T(8,128)} %get-tuple-element.107, f32[8,512,1024]{2,1,0:T(8,128)} %get-tuple-element.91, f32[8,512]{1,0:T(8,128)} %get-tuple-element.106, f32[8,512]{1,0:T(8,128)} %log_add_fusion), kind=kLoop, calls=%fused_computation.9 | loop fusion | flops 16777216 | bytes 41975808 | tf_op jit(solution)/shard_map/convert_element_type | solution.py:88
  320.9 4.7 fusion.115
  329.5 10.0 %multiply_reduce_fusion.1 = (f32[8,512]{1,0:T(8,128)}, f32[8,512,1024]{2,1,0:T(8,128)}) fusion(f32[8,512,1024]{2,1,0:T(8,128)S(1)} %bitcast.125, f32[8,512]{1,0:T(8,128)} %log_add_fusion.1, bf16[1024,16,64]{0,2,1:T(8,128)(2,1)} %bitcast.162, bf16[1024,16,64]{0,2,1:T(8,128)(2,1)} %bitcast.171), kind=kOutput, calls=%fused_computation.13 | convolution fusion | flops 549449728 | bytes 35160064 | tf_op jit(solution)/shard_map/qhd,khd->hqk/dot_general | solution.py:84
  339.5 7.7 %multiply_convert_fusion.1 = bf16[8,512,1024]{2,1,0:T(8,128)(2,1)S(1)} fusion(f32[8,512,1024]{2,1,0:T(8,128)} %get-tuple-element.109, f32[8,512,1024]{2,1,0:T(8,128)S(1)} %bitcast.125, f32[8,512]{1,0:T(8,128)} %get-tuple-element.108, f32[8,512]{1,0:T(8,128)} %log_add_fusion.1), kind=kLoop, calls=%fused_computation.12 | loop fusion | flops 16777216 | bytes 41975808 | tf_op jit(solution)/shard_map/convert_element_type | solution.py:88
  358.8 6.7 %fusion.26 = f32[1024,1024]{0,1:T(8,128)S(1)} fusion(bf16[1024,3072]{1,0:T(8,128)(2,1)S(1)} %bitcast.177, bf16[1024,1024]{0,1:T(8,128)(2,1)S(1)} %bitcast.149, bf16[1024,1024]{0,1:T(8,128)(2,1)S(1)} %bitcast.175, bf16[1024,1024]{0,1:T(8,128)(2,1)S(1)} %bitcast.146), kind=kOutput, calls=%fused_computation.50 | convolution fusion | flops 6461325312 | bytes 16777216 | tf_op jit(solution)/shard_map/dot_general | solution.py:250
  369.9 17.2 %fusion.63 = bf16[1,1024,1024]{1,2,0:T(8,128)(2,1)} fusion(f32[1024,1024]{0,1:T(8,128)} %copy-done.10, f32[1024]{0:T(1024)S(1)} %copy-done.53, bf16[4096,1024]{1,0:T(8,128)(2,1)} %all-gather.11.cloned.1.call-done, f32[1024,4096]{1,0:T(8,128)} %fusion.62), kind=kOutput, calls=%fused_computation.101 | convolution fusion | flops 8630829056 | bytes 31461376 | tf_op jit(solution)/shard_map/dot_general | solution.py:195
  387.1 7.2 %fusion.64 = bf16[1,1024,1024]{1,2,0:T(8,128)(2,1)} fusion(f32[1024,1024]{0,1:T(8,128)} %copy-done.11, bf16[1,1024,1024]{1,2,0:T(8,128)(2,1)} %copy.57, f32[1024]{0:T(1024)S(1)} %negate_multiply_fusion, f32[1024]{0:T(1024)S(1)} %copy-done.55, f32[1024]{0:T(1024)S(1)} %copy-done.53, f32[1024]{0:T(1024)S(1)} %multiply_multiply_fusion.2, ...), kind=kLoop, calls=%fused_computation.102 | loop fusion | flops 13631488 | bytes 14704640 | tf_op jit(solution)/shard_map/reshape | solution.py:255
  401.0 89.3 %all-reduce.5.cloned.1.call-done = (f32[1024,4]{0,1:T(4,128)}, f32[4,1024]{1,0:T(4,128)}, f32[1024,4]{0,1:T(4,128)}, f32[4,1024]{1,0:T(4,128)}) async-done(((f32[1024,4]{0,1:T(4,128)}, f32[4,1024]{1,0:T(4,128)}, f32[1024,4]{0,1:T(4,128)}, f32[4,1024]{1,0:T(4,128)}), (f32[1024,4]{0,1:T(4,128)}, f32[4,1024]{1,0:T(4,128)}, f32[1024,4]{0,1:T(4,128)}, f32[4,1024]{1,0:T(4,128)})) %all-reduce.5.cloned.1.call-update) | async-done | bytes 65552 | tf_op jit(solution)/shard_map/psum | solution.py:265
  (241 shorter events, 101.6 us)
Async XLA Ops:
  7.2 50.8 %all-gather.5.cloned.1.call-start = ((), (), s32[]{:S(2)}) async-start(), calls=%async_computation | async-start | bytes 7077888 | tf_op jit(solution)/shard_map/all_gather | solution.py:132
  7.9 149.6 %all-gather.7.cloned.1.call-start = ((), (), s32[]{:S(2)}) async-start(), calls=%async_computation.1 | async-start | bytes 2359296 | tf_op jit(solution)/shard_map/all_gather | solution.py:133
  8.6 158.7 %all-gather.9.cloned.1.call-start = ((), (), s32[]{:S(2)}) async-start(), calls=%async_computation.2 | async-start | bytes 9437184 | tf_op jit(solution)/shard_map/all_gather | solution.py:188
  9.4 190.9 %all-gather.11.cloned.1.call-start = ((), (), s32[]{:S(2)}) async-start(), calls=%async_computation.3 | async-start | bytes 9437184 | tf_op jit(solution)/shard_map/all_gather | solution.py:189
  10.0 480.4 %all-reduce.5.cloned.1.call-start = ((), (), s32[]{:S(2)}) async-start(), calls=%async_computation.4 | async-start | bytes 131072 | tf_op jit(solution)/shard_map/psum | solution.py:265
  12.0 10.1 %copy-start.35 = (bf16[1024,4]{0,1:T(4,128)(2,1)}, bf16[1024,4]{0,1:T(4,128)(2,1)S(1)}, u32[]{:S(2)}) copy-start(bf16[1024,4]{0,1:T(4,128)(2,1)S(1)} %convert.52) | copy-start | bytes 24580
  12.7 9.3 %copy-start.37 = (bf16[1024,4]{0,1:T(4,128)(2,1)}, bf16[1024,4]{0,1:T(4,128)(2,1)S(1)}, u32[]{:S(2)}) copy-start(bf16[1024,4]{0,1:T(4,128)(2,1)S(1)} %convert.53) | copy-start | bytes 24580
  23.8 85.8 %copy-start.25 = (bf16[1024,8]{0,1:T(8,128)(2,1)}, bf16[1024,8]{0,1:T(8,128)(2,1)S(1)}, u32[]{:S(2)}) copy-start(bf16[1024,8]{0,1:T(8,128)(2,1)S(1)} %convolution_convert_fusion) | copy-start | bytes 49156
  82.2 19.7 %copy-start.4 = (bf16[1024,1024]{0,1:T(8,128)(2,1)}, bf16[1024,1024]{0,1:T(8,128)(2,1)S(1)}, u32[]{:S(2)}) copy-start(bf16[1024,1024]{0,1:T(8,128)(2,1)S(1)} %copy.52) | copy-start | bytes 6291460
  101.9 7.6 %copy-start.39 = (f32[4,1024]{1,0:T(4,128)S(1)}, f32[4,1024]{1,0:T(4,128)}, u32[]{:S(2)}) copy-start(f32[4,1024]{1,0:T(4,128)} %param.41) | copy-start | bytes 49156
  115.1 20.7 %slice-start = ((s8[16777216]{0:T(1024)(128)(4,1)}), s8[4194304]{0:T(1024)(128)(4,1)S(1)}, s32[]{:S(2)}) async-start(s8[16777216]{0:T(1024)(128)(4,1)} %bitcast.122), calls=%async_computation.5 | async-start | bytes 8388608
  115.1 20.7 %slice-start.1 = ((s8[16777216]{0:T(1024)(128)(4,1)}), s8[4194304]{0:T(1024)(128)(4,1)S(1)}, s32[]{:S(2)}) async-start(s8[16777216]{0:T(1024)(128)(4,1)} %bitcast.122), calls=%async_computation.6 | async-start | bytes 8388608
  120.7 19.3 %copy-start.43 = (f32[8,512]{1,0:T(8,128)}, f32[8,512]{1,0:T(8,128)S(1)}, u32[]{:S(2)}) copy-start(f32[8,512]{1,0:T(8,128)S(1)} %fusion.23) | copy-start | bytes 49156
  120.7 15.1 %slice-start.2 = ((s8[16777216]{0:T(1024)(128)(4,1)}), s8[4194304]{0:T(1024)(128)(4,1)S(1)}, s32[]{:S(2)}) async-start(s8[16777216]{0:T(1024)(128)(4,1)} %bitcast.122), calls=%async_computation.7 | async-start | bytes 8388608
  125.9 9.9 %slice-start.3 = ((s8[16777216]{0:T(1024)(128)(4,1)}), s8[4194304]{0:T(1024)(128)(4,1)S(1)}, s32[]{:S(2)}) async-start(s8[16777216]{0:T(1024)(128)(4,1)} %bitcast.122), calls=%async_computation.8 | async-start | bytes 8388608
  125.9 14.1 %slice-start.14 = ((s8[8388608]{0:T(1024)(128)(4,1)}), s8[4194304]{0:T(1024)(128)(4,1)S(1)}, s32[]{:S(2)}) async-start(s8[8388608]{0:T(1024)(128)(4,1)} %bitcast.132), calls=%async_computation.19 | async-start | bytes 8388608
  144.5 8.0 %copy-start.13 = (bf16[1024,1024]{0,1:T(8,128)(2,1)S(1)}, bf16[1024,1024]{0,1:T(8,128)(2,1)}, u32[]{:S(2)}) copy-start(bf16[1024,1024]{0,1:T(8,128)(2,1)} %copy.50) | copy-start | bytes 6291460
  144.5 8.1 %copy-start.45 = (f32[8,512]{1,0:T(8,128)S(1)}, f32[8,512]{1,0:T(8,128)}, u32[]{:S(2)}) copy-start(f32[8,512]{1,0:T(8,128)} %fusion.7) | copy-start | bytes 49156
  166.1 74.1 %copy-start.30 = (f32[8,512]{1,0:T(8,128)}, f32[8,512]{1,0:T(8,128)S(1)}, u32[]{:S(2)}) copy-start(f32[8,512]{1,0:T(8,128)S(1)} %log_add_fusion.3) | copy-start | bytes 49156
  167.4 32.9 %copy-start.18 = (bf16[1,1024,1024]{1,2,0:T(8,128)(2,1)S(1)}, bf16[1,1024,1024]{1,2,0:T(8,128)(2,1)}, u32[]{:S(2)}) copy-start(bf16[1,1024,1024]{1,2,0:T(8,128)(2,1)} %copy.57) | copy-start | bytes 6291460
  167.4 32.9 %copy-start.53 = (f32[1024]{0:T(1024)S(1)}, f32[1024]{0:T(1024)}, u32[]{:S(2)}) copy-start(f32[1024]{0:T(1024)} %fusion.163) | copy-start | bytes 12292
  229.6 10.6 %slice-start.10 = ((s8[8388608]{0:T(1024)(128)(4,1)}), s8[4194304]{0:T(1024)(128)(4,1)S(1)}, s32[]{:S(2)}) async-start(s8[8388608]{0:T(1024)(128)(4,1)} %bitcast.128), calls=%async_computation.15 | async-start | bytes 8388608
  229.7 12.1 %slice-start.16 = ((s8[8388608]{0:T(1024)(128)(4,1)}), s8[4194304]{0:T(1024)(128)(4,1)S(1)}, s32[]{:S(2)}) async-start(s8[8388608]{0:T(1024)(128)(4,1)} %bitcast.134), calls=%async_computation.21 | async-start | bytes 8388608
  234.4 7.4 %slice-start.17 = ((s8[8388608]{0:T(1024)(128)(4,1)}), s8[4194304]{0:T(1024)(128)(4,1)S(1)}, s32[]{:S(2)}) async-start(s8[8388608]{0:T(1024)(128)(4,1)} %bitcast.134), calls=%async_computation.22 | async-start | bytes 8388608
  234.4 9.6 %slice-start.4 = ((s8[16777216]{0:T(1024)(128)(4,1)}), s8[4194304]{0:T(1024)(128)(4,1)S(1)}, s32[]{:S(2)}) async-start(s8[16777216]{0:T(1024)(128)(4,1)} %bitcast.124), calls=%async_computation.9 | async-start | bytes 8388608
  234.4 9.6 %slice-start.5 = ((s8[16777216]{0:T(1024)(128)(4,1)}), s8[4194304]{0:T(1024)(128)(4,1)S(1)}, s32[]{:S(2)}) async-start(s8[16777216]{0:T(1024)(128)(4,1)} %bitcast.124), calls=%async_computation.10 | async-start | bytes 8388608
  267.5 12.4 %slice-start.12 = ((s8[8388608]{0:T(1024)(128)(4,1)}), s8[4194304]{0:T(1024)(128)(4,1)S(1)}, s32[]{:S(2)}) async-start(s8[8388608]{0:T(1024)(128)(4,1)} %bitcast.130), calls=%async_computation.17 | async-start | bytes 8388608
  267.5 12.4 %slice-start.13 = ((s8[8388608]{0:T(1024)(128)(4,1)}), s8[4194304]{0:T(1024)(128)(4,1)S(1)}, s32[]{:S(2)}) async-start(s8[8388608]{0:T(1024)(128)(4,1)} %bitcast.130), calls=%async_computation.18 | async-start | bytes 8388608
  347.2 10.7 %slice-start.18 = ((s8[6291456]{0:T(1024)(128)(4,1)}), s8[4194304]{0:T(1024)(128)(4,1)S(1)}, s32[]{:S(2)}) async-start(s8[6291456]{0:T(1024)(128)(4,1)} %bitcast.176), calls=%async_computation.23 | async-start | bytes 8388608
  358.7 6.8 %copy-start.38 = (bf16[1024,4]{0,1:T(4,128)(2,1)S(1)}, bf16[1024,4]{0,1:T(4,128)(2,1)}, u32[]{:S(2)}) copy-start(bf16[1024,4]{0,1:T(4,128)(2,1)} %copy-done.37) | copy-start | bytes 24580
  358.8 6.8 %copy-start.52 = (f32[1024]{0:T(1024)S(1)}, f32[1024]{0:T(1024)}, u32[]{:S(2)}) copy-start(f32[1024]{0:T(1024)} %param.30) | copy-start | bytes 12292
  369.9 17.2 %copy-start.55 = (f32[1024]{0:T(1024)S(1)}, f32[1024]{0:T(1024)}, u32[]{:S(2)}) copy-start(f32[1024]{0:T(1024)} %copy-done.54) | copy-start | bytes 12292
  (52 other events, 192.9 us)
Sparse Core Ops, SparseCore 0:
  9.9 48.0 all-gather.4
  59.8 27.8 all-gather.6
  89.7 54.3 all-gather.8
  145.8 54.3 all-gather.10
  370.0 120.2 all-reduce.4
where the time goes:
time: 512 us; the launch traced here: 503 us
  matrix products  223 us (44%)
  waiting for transfers between devices  142 us (28%)
  other arithmetic  78.4 us (15%)
  local copies, waits for them, and re-layouts  43.4 us (8%)
  between operations  16 us (3%)
    psum x1, waiting for transfers between devices, local(): lax.psum((grad_down_both[:, :rank_size], query_up_gradient, grad_down_bot...  89.3 us
    dot_general x4, matrix products, attention_backward(): jnp.einsum('qhd,khd->hqk', grad_part, v_part, preferred_element_type=jnp....  35.3 us
    unnamed x166, local copies, waits for them, and re-layouts  34.4 us
    all_gather x1, waiting for transfers between devices, local(): lax.all_gather(w_qkv, 'fsdp', axis=0, tiled=True)  34.2 us
    convert_element_type x4, other arithmetic, attention_backward(): grad_scores = (attn_probs * (grad_probs - row_dot)).astype(jnp.bfloat16)  30.8 us
    dot_general x1, matrix products, local(): jnp.dot(grad_pre, fc_back.T, preferred_element_type=jnp.float32)  29.4 us
    dot_general x4, matrix products, block_scores(): jnp.einsum('qhd,khd->hqk', q_part, k_part, preferred_element_type=jnp.flo...  27.3 us
    reduce_sum x4, other arithmetic, attention_forward(): row_total = jnp.sum(exp_scores, axis=-1, keepdims=True)  24.8 us
  transfers between devices with their start and end apart: 5, of which 3 were waited for; matrix products, arithmetic and copies ran while one was open for 32% of the time, Pallas kernels for 0%

commit v1 on v0

v1 whole, which is shorter than its diff:
```python
import functools

import jax
import jax.numpy as jnp
from jax import lax
from jax.experimental import pallas as pl
from jax.experimental.pallas import tpu as pltpu
from jax.sharding import PartitionSpec as P

BF = jnp.bfloat16
F32 = jnp.float32
HD = 64
PAIR = 2 * HD
PAD = 128
SCALE = 8.0
EPS = 1e-05
NEG = -1e30
BLOCK = 256
FF_STEP = 512
VMEM_LIMIT = 58 * 2**20
GELU_C = 0.7978845608028654
GELU_A = 0.044715
ANY = pl.BlockSpec(memory_space=pl.ANY)
SMEM = pl.BlockSpec(memory_space=pltpu.SMEM)


def dot(a, b):
    return lax.dot_general(a, b, (((1,), (0,)), ((), ())), preferred_element_type=F32)


def dot_nt(a, b):
    return lax.dot_general(a, b, (((1,), (1,)), ((), ())), preferred_element_type=F32)


def dot_tn(a, b):
    return lax.dot_general(a, b, (((0,), (0,)), ((), ())), preferred_element_type=F32)


def lane(shape):
    return lax.broadcasted_iota(jnp.int32, shape, 1)


def row(shape):
    return lax.broadcasted_iota(jnp.int32, shape, 0)


def split3(x):
    a = x.astype(BF)
    r = x - a.astype(F32)
    b = r.astype(BF)
    c = (r - b.astype(F32)).astype(BF)
    return a, b, c


def whole(shape):
    return pl.BlockSpec(shape, lambda *_: (0,) * len(shape))


def params(**kw):
    return pltpu.CompilerParams(vmem_limit_bytes=VMEM_LIMIT, **kw)


def norm_stats(x):
    mean = jnp.mean(x, axis=-1, keepdims=True)
    center = x - mean
    inv = lax.rsqrt(jnp.mean(center * center, axis=-1, keepdims=True) + EPS)
    return center * inv, inv


def norm_back(xhat, inv, g):
    return inv * (
        g
        - jnp.mean(g, axis=-1, keepdims=True)
        - xhat * jnp.mean(g * xhat, axis=-1, keepdims=True)
    )


def pad_rows(parts, width):
    have = sum(p.shape[0] for p in parts)
    return jnp.concatenate(parts + [jnp.zeros((PAD - have, width), F32)], axis=0).astype(BF)


def norm_one_kernel(
    x_ref, gain_ref, shift_ref, dq_ref, dv_ref, uq_ref, uv_ref,
    n_ref, narrow_ref, down_ref, upq_ref, upv_ref,
):
    width = x_ref.shape[1]
    rank = dq_ref.shape[0]

    @pl.when(pl.program_id(0) == 0)
    def _():
        blank = jnp.zeros((rank, width), F32)
        down_ref[...] = pad_rows([dq_ref[...], dv_ref[...]], width)
        upq_ref[...] = pad_rows([uq_ref[...]], width)
        upv_ref[...] = pad_rows([blank, uv_ref[...]], width)

    xhat, _ = norm_stats(x_ref[...].astype(F32))
    low = (xhat * gain_ref[...] + shift_ref[...]).astype(BF)
    n_ref[...] = low
    narrow_ref[...] = dot_nt(low, down_ref[...]).astype(BF)


def norm_one(x, gain, shift, dq, dv, uq, uv):
    length, width = x.shape
    small = whole((1, width))
    adapter = whole(dq.shape)
    padded = whole((PAD, width))
    return pl.pallas_call(
        norm_one_kernel,
        grid=(length // BLOCK,),
        in_specs=[pl.BlockSpec((BLOCK, width), lambda i: (i, 0)), small, small] + [adapter] * 4,
        out_specs=[
            pl.BlockSpec((BLOCK, width), lambda i: (i, 0)),
            pl.BlockSpec((BLOCK, PAD), lambda i: (i, 0)),
            padded, padded, padded,
        ],
        out_shape=[
            jax.ShapeDtypeStruct((length, width), BF),
            jax.ShapeDtypeStruct((length, PAD), BF),
        ]
        + [jax.ShapeDtypeStruct((PAD, width), BF)] * 3,
        compiler_params=params(),
        name="norm_one",
    )(x, gain, shift, dq, dv, uq, uv)


def attend_pair(length, q, kp, vp, o_ref, qx_ref, col, kx, vx):
    size = kp.shape[0]
    ln = lane((size, PAIR))
    first = ln < HD
    bias = jnp.where(row((size, PAIR)) < length, 0.0, NEG).astype(BF)
    zero = jnp.zeros((size, PAIR), BF)
    kx[0] = jnp.where(first, kp, jnp.where(ln == HD, bias, zero))
    kx[1] = jnp.where(first, jnp.where(ln == 0, bias, zero), kp)
    vx[:, :PAIR] = vp
    vx[:, PAIR:] = jnp.ones((size, PAIR), BF)
    for i in range(size // BLOCK):
        begin, end = i * BLOCK, (i + 1) * BLOCK
        lq = lane((BLOCK, PAIR))
        fq = lq < HD
        qs = q[begin:end].astype(F32) * (1.0 / HD**0.5)
        outs = []
        for h in range(2):
            other = HD * (1 - h)
            base = jnp.where(fq if h == 0 else ~fq, qs, jnp.where(lq == other, 1.0, 0.0))
            qh = base.astype(BF)
            near = dot_nt(qh, kx[h, begin:end, :])
            near = jnp.where(lane((BLOCK, BLOCK)) <= row((BLOCK, BLOCK)), near, NEG)
            top = jnp.max(near, axis=-1, keepdims=True)
            if i:
                far = dot_nt(qh, kx[h, :begin, :])
                top = jnp.maximum(top, jnp.max(far, axis=-1, keepdims=True))
            acc = dot(jnp.exp(near - top).astype(BF), vx[begin:end, :])
            if i:
                acc = acc + dot(jnp.exp(far - top).astype(BF), vx[:begin, :])
            total = acc[:, PAIR:]
            outs.append(acc[:, :PAIR] / total)
            a, b, c = split3(-(top + jnp.log(total)))
            kept = jnp.where(
                lq == other + 1,
                a.astype(F32),
                jnp.where(
                    lq == other + 2,
                    b.astype(F32),
                    jnp.where(lq == other + 3, c.astype(F32), base),
                ),
            )
            at = 2 * col + h * PAIR
            qx_ref[begin:end, at : at + PAIR] = kept.astype(BF)
        o_ref[begin:end, col : col + PAIR] = jnp.where(fq, outs[0], outs[1]).astype(BF)


QUAD = 2 * PAIR


def qkv_copies(parts, index_ref, shards, wbuf, sem, step, slot, group):
    rows = shards[0].shape[0]
    copies = []
    for i, ref in enumerate(shards):
        at = pl.multiple_of(index_ref[i] * rows, rows)
        for p in range(parts):
            src = ref.at[:, pl.ds(pl.multiple_of(p * group + step * QUAD, QUAD), QUAD)]
            dst = wbuf.at[slot, pl.ds(at, rows), pl.ds(p * QUAD, QUAD)]
            copies.append(pltpu.make_async_copy(src, dst, sem.at[slot]))
    return copies


def forward_kernel(count, len_ref, index_ref, *refs):
    shards = refs[:count]
    n_ref, narrow_ref, upq_ref, upv_ref, o_ref, qx_ref, k_ref, v_ref, wbuf, kx, vx, sem = refs[count:]
    step = pl.program_id(0)
    steps = pl.num_programs(0)
    group = shards[0].shape[1] // 3
    slot = lax.rem(step, 2)

    @pl.when(step == 0)
    def _():
        for c in qkv_copies(3, index_ref, shards, wbuf, sem, 0, 0, group):
            c.start()

    @pl.when(step + 1 < steps)
    def _():
        for c in qkv_copies(3, index_ref, shards, wbuf, sem, step + 1, 1 - slot, group):
            c.start()

    for c in qkv_copies(3, index_ref, shards, wbuf, sem, step, slot, group):
        c.wait()
    n = n_ref[...]
    narrow = narrow_ref[...]
    q = dot(n, wbuf[slot, :, :QUAD]) + SCALE * dot(narrow, upq_ref[...])
    k = dot(n, wbuf[slot, :, QUAD : 2 * QUAD])
    v = dot(n, wbuf[slot, :, 2 * QUAD :]) + SCALE * dot(narrow, upv_ref[...])
    q = q.astype(BF)
    k_ref[...] = k.astype(BF)
    v_ref[...] = v.astype(BF)
    length = len_ref[0]
    for p in range(2):
        col = p * PAIR
        attend_pair(
            length,
            q[:, col : col + PAIR],
            k_ref[:, col : col + PAIR],
            v_ref[:, col : col + PAIR],
            o_ref, qx_ref, col, kx, vx,
        )


def attention_forward(lengths, index, shards, n, narrow, upq, upv):
    length, width = n.shape
    group = shards[0].shape[1] // 3
    steps = group // QUAD
    quad = pl.BlockSpec((length, QUAD), lambda s: (0, s))
    up = pl.BlockSpec((PAD, QUAD), lambda s: (0, s))
    return pl.pallas_call(
        functools.partial(forward_kernel, len(shards)),
        grid=(steps,),
        in_specs=[SMEM, SMEM]
        + [ANY] * len(shards)
        + [whole((length, width)), whole((length, PAD)), up, up],
        out_specs=[quad, pl.BlockSpec((length, 2 * QUAD), lambda s: (0, s)), quad, quad],
        out_shape=[
            jax.ShapeDtypeStruct((length, group), BF),
            jax.ShapeDtypeStruct((length, 2 * group), BF),
            jax.ShapeDtypeStruct((length, group), BF),
            jax.ShapeDtypeStruct((length, group), BF),
        ],
        scratch_shapes=[
            pltpu.VMEM((2, width, 3 * QUAD), BF),
            pltpu.VMEM((2, length, PAIR), BF),
            pltpu.VMEM((length, QUAD), BF),
            pltpu.SemaphoreType.DMA((2,)),
        ],
        compiler_params=params(),
        name="attention_forward",
    )(lengths, index, *shards, n, narrow, upq, upv)


def ff_copies(index_ref, fcs, outs, fbuf, obuf, sem, step, slot):
    rows = fcs[0].shape[0]
    copies = []
    for i, ref in enumerate(fcs):
        at = pl.multiple_of(index_ref[i] * rows, rows)
        src = ref.at[:, pl.ds(pl.multiple_of(step * FF_STEP, FF_STEP), FF_STEP)]
        copies.append(pltpu.make_async_copy(src, fbuf.at[slot, pl.ds(at, rows), :], sem.at[slot]))
    src = outs.at[pl.ds(pl.multiple_of(step * FF_STEP, FF_STEP), FF_STEP), :]
    copies.append(pltpu.make_async_copy(src, obuf.at[slot], sem.at[slot]))
    return copies


def proj_copies(index_ref, projs, wbuf, sem):
    rows = projs[0].shape[0]
    copies = []
    for i, ref in enumerate(projs):
        at = pl.multiple_of(index_ref[i] * rows, rows)
        copies.append(pltpu.make_async_copy(ref, wbuf.at[pl.ds(at, rows), :], sem.at[0]))
    return copies


def gelu_both(v):
    square = v * v
    t = jnp.tanh(v * (GELU_C + (GELU_C * GELU_A) * square))
    half = 0.5 * t + 0.5
    act = v * half
    slope = half + act * (1.0 - half) * (2.0 * GELU_C + (6.0 * GELU_C * GELU_A) * square)
    return act, slope


def middle_kernel(count, heads, len_ref, index_ref, *refs):
    projs, refs = refs[:count], refs[count:]
    fcs, refs = refs[:count], refs[count:]
    outs, refs = refs[0], refs[1:]
    atts, refs = refs[:heads], refs[heads:]
    (x_ref, cot_ref, gain_ref, shift_ref, block_ref, gh_ref, ga_ref,
     wproj, fbuf, obuf, hidden, n2, low, acc, back, psem, sem) = refs
    step = pl.program_id(0)
    steps = pl.num_programs(0)
    size = x_ref.shape[0]
    slot = lax.rem(step, 2)

    @pl.when(step == 0)
    def _():
        first = proj_copies(index_ref, projs, wproj, psem)
        for c in first:
            c.start()
        for c in ff_copies(index_ref, fcs, outs, fbuf, obuf, sem, 0, 0):
            c.start()
        for c in first:
            c.wait()
        for i in range(size // BLOCK):
            at = pl.ds(i * BLOCK, BLOCK)
            total = x_ref[at, :].astype(F32)
            for j, ref in enumerate(atts):
                wide = ref.shape[1]
                total = total + dot(ref[at, :], wproj[j * wide : (j + 1) * wide, :])
            hidden[at, :] = total
            xhat, _ = norm_stats(total)
            n2[at, :] = (xhat * gain_ref[...] + shift_ref[...]).astype(BF)
            keep = row((BLOCK, 1)) + i * BLOCK < len_ref[0]
            low[at, :] = jnp.where(keep, cot_ref[at, :].astype(F32), 0.0).astype(BF)

    @pl.when(step + 1 < steps)
    def _():
        for c in ff_copies(index_ref, fcs, outs, fbuf, obuf, sem, step + 1, 1 - slot):
            c.start()

    for c in ff_copies(index_ref, fcs, outs, fbuf, obuf, sem, step, slot):
        c.wait()
    fc = fbuf[slot]
    out = obuf[slot]
    for i in range(size // BLOCK):
        at = pl.ds(i * BLOCK, BLOCK)
        act, slope = gelu_both(dot(n2[at, :], fc))
        mlp = dot(act.astype(BF), out)
        grad = (dot_nt(low[at, :], out) * slope).astype(BF)
        u = dot_nt(grad, fc)

        @pl.when(step == 0)
        def _():
            acc[at, :] = mlp
            back[at, :] = u

        @pl.when(step > 0)
        def _():
            acc[at, :] += mlp
            back[at, :] += u

    @pl.when(step == steps - 1)
    def _():
        for i in range(size // BLOCK):
            at = pl.ds(i * BLOCK, BLOCK)
            h = hidden[at, :]
            keep = row((BLOCK, 1)) + i * BLOCK < len_ref[0]
            block_ref[at, :] = jnp.where(keep, h + acc[at, :], 0.0).astype(BF)
            xhat, inv = norm_stats(h)
            gh = low[at, :].astype(F32) + norm_back(xhat, inv, gain_ref[...] * back[at, :])
            gh_ref[at, :] = gh
            ga_ref[at, :] = dot_nt(gh.astype(BF), wproj[...]).astype(BF)


def middle(lengths, index, projs, fcs, outs, atts, x, cot, gain, shift):
    size, width = x.shape
    hidden_units = outs.shape[0]
    full = whole((size, width))
    once = pl.BlockSpec((size, width), lambda s: (0, 0), pipeline_mode=pl.Buffered(1))
    return pl.pallas_call(
        functools.partial(middle_kernel, len(projs), len(atts)),
        grid=(hidden_units // FF_STEP,),
        in_specs=[SMEM, SMEM]
        + [ANY] * (2 * len(projs) + 1)
        + [whole(a.shape) for a in atts]
        + [once, once, whole((1, width)), whole((1, width))],
        out_specs=[full, full, full],
        out_shape=[
            jax.ShapeDtypeStruct((size, width), BF),
            jax.ShapeDtypeStruct((size, width), F32),
            jax.ShapeDtypeStruct((size, width), BF),
        ],
        scratch_shapes=[
            pltpu.VMEM((width, width), BF),
            pltpu.VMEM((2, width, FF_STEP), BF),
            pltpu.VMEM((2, FF_STEP, width), BF),
            pltpu.VMEM((size, width), F32),
            pltpu.VMEM((size, width), BF),
            pltpu.VMEM((size, width), BF),
            pltpu.VMEM((size, width), F32),
            pltpu.VMEM((size, width), F32),
            pltpu.SemaphoreType.DMA((1,)),
            pltpu.SemaphoreType.DMA((2,)),
        ],
        compiler_params=params(),
        name="middle",
    )(lengths, index, *projs, *fcs, outs, *atts, x, cot, gain, shift)


def backward_kernel(
    len_ref, qx_ref, k_ref, v_ref, o_ref, g_ref, dq_ref, dk_ref, dv_ref, kx, vx, gx, dqa
):
    size = k_ref.shape[0]
    ln = lane((size, PAIR))
    first = ln < HD
    bias = jnp.where(row((size, PAIR)) < len_ref[0], 0.0, NEG).astype(BF)
    kp = k_ref[...]
    vp = v_ref[...]
    g = g_ref[...]
    zero = jnp.zeros((size, PAIR), BF)
    one = jnp.ones((size, PAIR), BF)
    prod = g.astype(F32) * o_ref[...].astype(F32)
    for h in range(2):
        other = HD * (1 - h)
        mine = first if h == 0 else ~first
        extra = (ln > other) & (ln <= other + 3)
        kx[h] = jnp.where(mine, kp, jnp.where(ln == other, bias, jnp.where(extra, one, zero)))
        vx[h] = jnp.where(mine, vp, jnp.where(extra, one, zero))
        dots = jnp.sum(jnp.where(mine, prod, 0.0), axis=-1, keepdims=True)
        a, b, c = split3(jnp.broadcast_to(-dots, (size, PAIR)))
        gx[h] = jnp.where(
            mine,
            g,
            jnp.where(
                ln == other + 1,
                a,
                jnp.where(ln == other + 2, b, jnp.where(ln == other + 3, c, zero)),
            ),
        )
    qp = jnp.where(first, qx_ref[:, :PAIR], qx_ref[:, PAIR:])
    blocks = size // BLOCK
    for kb in range(blocks):
        keys = slice(kb * BLOCK, (kb + 1) * BLOCK)
        dvs = []
        dks = []
        for h in range(2):
            dv = dk = None
            for qb in range(kb, blocks):
                queries = slice(qb * BLOCK, (qb + 1) * BLOCK)
                st = dot_nt(kx[h, keys, :], qx_ref[queries, h * PAIR : (h + 1) * PAIR])
                if qb == kb:
                    st = jnp.where(row((BLOCK, BLOCK)) <= lane((BLOCK, BLOCK)), st, NEG)
                p = jnp.exp(st)
                dp = dot_nt(vx[h, keys, :], gx[h, queries, :])
                ds = (p * dp).astype(BF)
                a = dot(p.astype(BF), g[queries])
                b = dot(ds, qp[queries])
                c = dot_tn(ds, kp[keys])
                dv = a if dv is None else dv + a
                dk = b if dk is None else dk + b
                if kb == 0:
                    dqa[h, queries, :] = c
                else:
                    dqa[h, queries, :] += c
            dvs.append(dv)
            dks.append(dk)
        f = lane((BLOCK, PAIR)) < HD
        dv_ref[keys, :] = jnp.where(f, dvs[0], dvs[1]).astype(BF)
        dk_ref[keys, :] = jnp.where(f, dks[0], dks[1]).astype(BF)
    dq_ref[...] = (jnp.where(first, dqa[0], dqa[1]) * (1.0 / HD**0.5)).astype(BF)


def attention_backward(lengths, qx, k, v, o, ga, at):
    size, group = k.shape
    pair = pl.BlockSpec((size, PAIR), lambda p: (0, p))
    start = at // PAIR
    return pl.pallas_call(
        backward_kernel,
        grid=(group // PAIR,),
        in_specs=[
            SMEM,
            pl.BlockSpec((size, 2 * PAIR), lambda p: (0, p)),
            pair, pair, pair,
            pl.BlockSpec((size, PAIR), lambda p: (0, p + start)),
        ],
        out_specs=[pair] * 3,
        out_shape=[jax.ShapeDtypeStruct((size, group), BF)] * 3,
        scratch_shapes=[pltpu.VMEM((2, size, PAIR), BF)] * 3 + [pltpu.VMEM((2, size, PAIR), F32)],
        compiler_params=params(),
        name="attention_backward",
    )(lengths, qx, k, v, o, ga)


def adapter_kernel(groups, *refs):
    dqs, refs = refs[:groups], refs[groups:]
    dvs, refs = refs[:groups], refs[groups:]
    n_ref, narrow_ref, upq_ref, upv_ref, joint_ref, sums_ref = refs
    narrow = narrow_ref[...]
    total = None
    for j in range(groups):
        wide = dqs[j].shape[1]
        cols = slice(j * wide, (j + 1) * wide)
        dq = dqs[j][...]
        dv = dvs[j][...]
        part = dot_nt(dq, upq_ref[:, cols]) + dot_nt(dv, upv_ref[:, cols])
        total = part if total is None else total + part
        gq = SCALE * dot_tn(narrow, dq)
        gv = SCALE * dot_tn(narrow, dv)
        sums_ref[8:16, cols] = jnp.where(row((8, wide)) < 4, gq[:8], gv[:8])
    joint = (SCALE * total).astype(BF)
    joint_ref[...] = joint
    sums_ref[0:8, :] = dot_tn(joint, n_ref[...])[:8]


def adapter_sums(dqs, dvs, n, narrow, upq, upv):
    size, width = n.shape
    return pl.pallas_call(
        functools.partial(adapter_kernel, len(dqs)),
        out_shape=[
            jax.ShapeDtypeStruct((size, PAD), BF),
            jax.ShapeDtypeStruct((16, width), F32),
        ],
        compiler_params=params(),
        name="adapter_sums",
    )(*dqs, *dvs, n, narrow, upq, upv)


def token_copies(index_ref, shards, wbuf, sem, step, slot, group):
    rows = shards[0].shape[0]
    copies = []
    for i, ref in enumerate(shards):
        at = pl.multiple_of(index_ref[i] * rows, rows)
        copies.append(
            pltpu.make_async_copy(
                ref.at[:, step * group : (step + 1) * group],
                wbuf.at[slot, pl.ds(at, rows), :],
                sem.at[slot],
            )
        )
    return copies


def token_kernel(count, groups, index_ref, *refs):
    shards, refs = refs[: count * groups], refs[count * groups :]
    grads, refs = refs[: 3 * groups], refs[3 * groups :]
    joint_ref, down_ref, gh_ref, x_ref, gain_ref, o_ref, wbuf, acc, sem = refs
    size = x_ref.shape[0]
    group = shards[0].shape[1] // 3
    steps = [(j, p) for j in range(groups) for p in range(3)]

    def copies(s):
        j, p = steps[s]
        return token_copies(
            index_ref, shards[j * count : (j + 1) * count], wbuf, sem, p, s % 2, group
        )

    for c in copies(0):
        c.start()
    for s, (j, p) in enumerate(steps):
        if s + 1 < len(steps):
            for c in copies(s + 1):
                c.start()
        for c in copies(s):
            c.wait()
        g = grads[p * groups + j]
        for i in range(size // BLOCK):
            at = pl.ds(i * BLOCK, BLOCK)
            part = dot_nt(g[at, :], wbuf[s % 2])
            if s == 0:
                part = part + dot(joint_ref[at, :], down_ref[...])
            else:
                part = part + acc[at, :]
            if s + 1 < len(steps):
                acc[at, :] = part
            else:
                xhat, inv = norm_stats(x_ref[at, :].astype(F32))
                o_ref[at, :] = (
                    gh_ref[at, :] + norm_back(xhat, inv, gain_ref[...] * part)
                ).astype(BF)


def token_gradient(index, shards, dqs, dks, dvs, joint, down, gh, x, gain):
    size, width = x.shape
    groups = len(dqs)
    count = len(shards[0])
    group = shards[0][0].shape[1] // 3
    flat = [s for part in shards for s in part]
    vm = pl.BlockSpec(memory_space=pltpu.VMEM)
    return pl.pallas_call(
        functools.partial(token_kernel, count, groups),
        in_specs=[SMEM] + [ANY] * len(flat) + [vm] * (3 * groups + 5),
        out_specs=vm,
        out_shape=jax.ShapeDtypeStruct((size, width), BF),
        scratch_shapes=[
            pltpu.VMEM((2, width, group), BF),
            pltpu.VMEM((size, width), F32),
            pltpu.SemaphoreType.DMA((2,)),
        ],
        compiler_params=params(),
        name="token_gradient",
    )(index, *flat, *dqs, *dks, *dvs, joint, down, gh, x, gain)


def local(
    tokens, lengths, cotangent, gain_one, shift_one, gain_two, shift_two,
    w_qkv, w_proj, w_fc, w_out,
    query_down_factor, query_up_factor, value_down_factor, value_up_factor,
):
    _, size, width = tokens.shape
    x = tokens.reshape(size, width)
    cot = cotangent.reshape(size, width)

    def gather(w):
        return lax.all_gather(w, "fsdp", axis=0, tiled=True)

    qkv, proj, fc, out = gather(w_qkv), gather(w_proj), gather(w_fc), gather(w_out)
    index = jnp.zeros((1,), jnp.int32)

    n, narrow, down, upq, upv = norm_one(
        x, gain_one[None], shift_one[None],
        query_down_factor.T, value_down_factor.T, query_up_factor, value_up_factor,
    )
    o, qx, k, v = attention_forward(lengths, index, [qkv], n, narrow, upq, upv)
    block_out, gh, ga = middle(
        lengths, index, [proj], [fc], out, [o], x, cot, gain_two[None], shift_two[None]
    )
    dq, dk, dv = attention_backward(lengths, qx, k, v, o, ga, 0)
    joint, sums = adapter_sums([dq], [dv], n, narrow, upq, upv)
    sums = lax.psum(sums, ("dp", "fsdp"))
    grad = token_gradient(index, [[qkv]], [dq], [dk], [dv], joint, down, gh, x, gain_one[None])
    return (
        block_out.reshape(tokens.shape),
        grad.reshape(tokens.shape),
        sums[0:4].T,
        sums[8:12],
        sums[4:8].T,
        sums[12:16],
    )


def solution(mesh):
    rows = P(("dp", "fsdp"), None, None)
    frozen = P("fsdp", None)
    return jax.shard_map(
        local,
        mesh=mesh,
        in_specs=(rows, P(("dp", "fsdp")), rows, P(), P(), P(), P())
        + (frozen,) * 4
        + (P(),) * 4,
        out_specs=(rows, rows, P(), P(), P(), P()),
        check_vma=False,
    )
```

time: 512 us -> 473 us (0.924); the launches traced: 503 us -> 472 us
  matrix products: 223 us -> 0 us
  Pallas kernels: 0 us -> 202 us
  waiting for transfers between devices: 142 us -> 254 us
  other arithmetic: 78.4 us -> 0 us
  local copies, waits for them, and re-layouts: 43.4 us -> 1.48 us
    dot_general x40 -> x0, matrix products: 223 us -> none  [the longest x4 35.3 us: attention_backward(): jnp.einsum('qhd,khd->hqk', grad_part, v_part, preferred_element_type=jnp....]
    pallas_call x0 -> x6, Pallas kernels: none -> 202 us  [the longest x1 81 us: middle(): pl.pallas_call(functools.partial(middle_kernel, len(projs), len(atts)), g...]
    all_gather x4, waiting for transfers between devices: 50 us -> 149 us  [gather(): return lax.all_gather(w, 'fsdp', axis=0, tiled=True)]
    unnamed x166 -> x0, local copies, waits for them, and re-layouts: 34.4 us -> none
    convert_element_type x8 -> x0, other arithmetic: 33.4 us -> none  [the longest x4 30.8 us: attention_backward(): grad_scores = (attn_probs * (grad_probs - row_dot)).astype(jnp.bfloat16)]
    reduce_sum x9 -> x0, other arithmetic: 31.9 us -> none  [the longest x4 24.8 us: attention_forward(): row_total = jnp.sum(exp_scores, axis=-1, keepdims=True)]
    psum x1, waiting for transfers between devices: 89.3 us -> 102 us  [local(): sums = lax.psum(sums, ('dp', 'fsdp'))]
    reshape x1 -> x0, other arithmetic: 7.25 us -> none  [local(): grad_flat.astype(jnp.bfloat16).reshape(rows_here, seq_len, embedding_width)]
  transfers between devices with their start and end apart: 5 -> 5, of which waited for: 3 -> 4; matrix products, arithmetic and copies ran while one was open for 32% -> 0% of each run, Pallas kernels for 0% -> 12%
where the time goes in v1:
time: 473 us; the launch traced here: 472 us
  waiting for transfers between devices  254 us (54%)
  Pallas kernels  202 us (43%)
  between operations  14.6 us (3%)
    all_gather x4, waiting for transfers between devices, gather(): return lax.all_gather(w, 'fsdp', axis=0, tiled=True)  149 us
    psum x1, waiting for transfers between devices, local(): sums = lax.psum(sums, ('dp', 'fsdp'))  102 us
    pallas_call x1, Pallas kernels, middle(): pl.pallas_call(functools.partial(middle_kernel, len(projs), len(atts)), g...  81 us
    pallas_call x1, Pallas kernels, attention_backward(): pl.pallas_call(backward_kernel, grid=(group // PAIR,), in_specs=[SMEM, pl...  57.1 us
    pallas_call x1, Pallas kernels, attention_forward(): pl.pallas_call(functools.partial(forward_kernel, len(shards)), grid=(step...  35.4 us
    pallas_call x1, Pallas kernels, token_gradient(): pl.pallas_call(functools.partial(token_kernel, count, groups), in_specs=[...  17.2 us
  transfers between devices with their start and end apart: 5, of which 4 were waited for; matrix products, arithmetic and copies ran while one was open for 0% of the time, Pallas kernels for 12%

profile of v1, /device:TPU:1, one launch (start us, length us, event | category | flops | bytes accessed | tf_op | source)
XLA Modules:
  0.0 471.9 jit_solution(6160060237893600434)
XLA Ops:
  7.2 0.0 all-gather.11.cloned.1.call-start
  7.2 0.7 all-gather.11.cloned.1.call-update
  7.9 0.0 all-gather.5.cloned.1.call-start
  7.9 0.7 all-gather.5.cloned.1.call-update
  8.7 0.0 all-gather.7.cloned.1.call-start
  8.7 0.7 all-gather.7.cloned.1.call-update
  9.4 0.0 all-gather.9.cloned.1.call-start
  9.4 0.5 all-gather.9.cloned.1.call-update
  10.0 0.0 all-reduce.2.cloned.1.call-start
  10.7 4.8 %norm_one.1 = (bf16[1024,1024]{1,0:T(8,128)(2,1)}, bf16[1024,128]{1,0:T(8,128)(2,1)}, bf16[128,1024]{1,0:T(8,128)(2,1)}, bf16[128,1024]{1,0:T(8,128)(2,1)}, bf16[128,1024]{1,0:T(8,128)(2,1)}) custom-call(bf16[1024,1024]{1,0:T(8,128)(2,1)} %bitcast.14, f32[1,1024]{1,0:T(1,128)} %bitcast.21, f32[1,1024]{1,0:T(1,128)} %bitcast.23, f32[4,1024]{1,0:T(4,128)} %bitcast.19, ...), custom_call_target="tpu_custom_call" | custom-call | tf_op jit(solution)/shard_map/norm_one/pallas_call | solution.py:108
  15.5 42.5 %all-gather.11.cloned.1.call-done.refs_0_ = bf16[1024,3072]{1,0:T(8,128)(2,1)} async-done(((bf16[128,3072]{1,0:T(8,128)(2,1)}), bf16[1024,3072]{1,0:T(8,128)(2,1)}) %all-gather.11.cloned.1.call-update) | async-done | bytes 6291472 | tf_op jit(solution)/shard_map/all_gather | solution.py:599
  58.0 35.4 %attention_forward.1 = (bf16[1024,1024]{1,0:T(8,128)(2,1)}, bf16[1024,2048]{1,0:T(8,128)(2,1)}, bf16[1024,1024]{1,0:T(8,128)(2,1)}, bf16[1024,1024]{1,0:T(8,128)(2,1)}) custom-call(s32[1]{0:T(128)S(6)} %copy.22.len_ref, s32[1]{0:T(128)} %constant.0.clone.1.index_ref, bf16[1024,3072]{1,0:T(8,128)(2,1)} %all-gather.11.cloned.1.call-done.refs_0_, ...), custom_call_target="tpu_custom_call" | custom-call | tf_op jit(solution)/shard_map/attention_forward/pallas_call | solution.py:234
  93.3 0.0 all-gather.5.cloned.1.call-done.refs_0_
  93.4 50.7 %all-gather.7.cloned.1.call-done.refs_1_ = bf16[1024,4096]{1,0:T(8,128)(2,1)} async-done(((bf16[128,4096]{1,0:T(8,128)(2,1)}), bf16[1024,4096]{1,0:T(8,128)(2,1)}) %all-gather.7.cloned.1.call-update) | async-done | bytes 8388624 | tf_op jit(solution)/shard_map/all_gather | solution.py:599
  144.1 56.2 %all-gather.9.cloned.1.call-done.refs_2_ = bf16[4096,1024]{1,0:T(8,128)(2,1)} async-done(((bf16[512,1024]{1,0:T(8,128)(2,1)}), bf16[4096,1024]{1,0:T(8,128)(2,1)}) %all-gather.9.cloned.1.call-update) | async-done | bytes 8388624 | tf_op jit(solution)/shard_map/all_gather | solution.py:599
  200.3 81.0 %middle.1 = (bf16[1024,1024]{1,0:T(8,128)(2,1)}, f32[1024,1024]{1,0:T(8,128)}, bf16[1024,1024]{1,0:T(8,128)(2,1)}) custom-call(s32[1]{0:T(128)S(6)} %copy.22.len_ref, s32[1]{0:T(128)} %constant.0.clone.1.index_ref, bf16[1024,1024]{1,0:T(8,128)(2,1)} %all-gather.5.cloned.1.call-done.refs_0_, bf16[1024,4096]{1,0:T(8,128)(2,1)} %all-gather.7.cloned.1.call-done.refs_1_, ...), custom_call_target="tpu_custom_call" | custom-call | tf_op jit(solution)/shard_map/middle/pallas_call | solution.py:365
  281.3 57.1 %attention_backward.1 = (bf16[1024,1024]{1,0:T(8,128)(2,1)}, bf16[1024,1024]{1,0:T(8,128)(2,1)}, bf16[1024,1024]{1,0:T(8,128)(2,1)}) custom-call(s32[1]{0:T(128)S(6)} %copy.22.len_ref, bf16[1024,2048]{1,0:T(8,128)(2,1)} %get-tuple-element.29.qx_ref, bf16[1024,1024]{1,0:T(8,128)(2,1)} %get-tuple-element.30.k_ref, bf16[1024,1024]{1,0:T(8,128)(2,1)} %get-tuple-element.31.v_ref, ...), custom_call_target="tpu_custom_call" | custom-call | tf_op jit(solution)/shard_map/attention_backward/pallas_call | solution.py:462
  338.4 6.2 %adapter_sums.1 = (bf16[1024,128]{1,0:T(8,128)(2,1)}, f32[16,1024]{1,0:T(8,128)}) custom-call(bf16[1024,1024]{1,0:T(8,128)(2,1)} %get-tuple-element.33.refs_0_.refs_1_, bf16[1024,1024]{1,0:T(8,128)(2,1)} %get-tuple-element.35.refs_1_.refs_3_, bf16[1024,1024]{1,0:T(8,128)(2,1)} %get-tuple-element.23.refs_1_.refs_2_, ...), custom_call_target="tpu_custom_call" | custom-call | tf_op jit(solution)/shard_map/adapter_sums/pallas_call | solution.py:502
  344.6 0.0 all-reduce.2.cloned.1.call-update
  344.7 17.2 %token_gradient.1 = bf16[1024,1024]{1,0:T(8,128)(2,1)} custom-call(s32[1]{0:T(128)} %constant.0.clone.1.index_ref, bf16[1024,3072]{1,0:T(8,128)(2,1)} %all-gather.11.cloned.1.call-done.refs_0_, bf16[1024,1024]{1,0:T(8,128)(2,1)} %get-tuple-element.33.refs_0_.refs_1_, bf16[1024,1024]{1,0:T(8,128)(2,1)} %get-tuple-element.34.refs_2_, ...), custom_call_target="tpu_custom_call" | custom-call | tf_op jit(solution)/shard_map/token_gradient/pallas_call | solution.py:574
  361.9 101.8 %all-reduce.2.cloned.1.call-done = f32[16,1024]{1,0:T(8,128)} async-done(((f32[16,1024]{1,0:T(8,128)}), f32[16,1024]{1,0:T(8,128)}) %all-reduce.2.cloned.1.call-update) | async-done | bytes 65552 | tf_op jit(solution)/shard_map/psum | solution.py:614
  463.7 1.5 fusion
Async XLA Ops:
  7.2 50.8 %all-gather.11.cloned.1.call-start = ((), (), s32[]{:S(2)}) async-start(), calls=%async_computation.3 | async-start | bytes 7077888 | tf_op jit(solution)/shard_map/all_gather | solution.py:599
  7.9 85.5 %all-gather.5.cloned.1.call-start = ((), (), s32[]{:S(2)}) async-start(), calls=%async_computation | async-start | bytes 2359296 | tf_op jit(solution)/shard_map/all_gather | solution.py:599
  8.7 135.4 %all-gather.7.cloned.1.call-start = ((), (), s32[]{:S(2)}) async-start(), calls=%async_computation.1 | async-start | bytes 9437184 | tf_op jit(solution)/shard_map/all_gather | solution.py:599
  9.4 190.9 %all-gather.9.cloned.1.call-start = ((), (), s32[]{:S(2)}) async-start(), calls=%async_computation.2 | async-start | bytes 9437184 | tf_op jit(solution)/shard_map/all_gather | solution.py:599
  10.0 453.7 %all-reduce.2.cloned.1.call-start = ((), (), s32[]{:S(2)}) async-start(), calls=%async_computation.4 | async-start | bytes 131072 | tf_op jit(solution)/shard_map/psum | solution.py:614
Sparse Core Ops, SparseCore 0:
  9.9 48.0 all-gather.10
  59.8 27.8 all-gather.4
  89.7 54.3 all-gather.6
  145.8 54.3 all-gather.8
  344.8 118.8 all-reduce.1

commit v2 on v1

--- a/solution.py
+++ b/solution.py
@@ -173,43 +173,32 @@
 QUAD = 2 * PAIR
 
 
-def qkv_copies(parts, index_ref, shards, wbuf, sem, step, slot, group):
+def qkv_copies(index_ref, shards, wbuf, sem, quad, group):
     rows = shards[0].shape[0]
     copies = []
     for i, ref in enumerate(shards):
         at = pl.multiple_of(index_ref[i] * rows, rows)
-        for p in range(parts):
-            src = ref.at[:, pl.ds(pl.multiple_of(p * group + step * QUAD, QUAD), QUAD)]
-            dst = wbuf.at[slot, pl.ds(at, rows), pl.ds(p * QUAD, QUAD)]
-            copies.append(pltpu.make_async_copy(src, dst, sem.at[slot]))
+        for p in range(3):
+            col = p * group + quad * QUAD
+            src = ref.at[:, col : col + QUAD]
+            dst = wbuf.at[pl.ds(at, rows), p * QUAD : (p + 1) * QUAD]
+            copies.append(pltpu.make_async_copy(src, dst, sem.at[p]))
     return copies
 
 
-def forward_kernel(count, len_ref, index_ref, *refs):
-    shards = refs[:count]
-    n_ref, narrow_ref, upq_ref, upv_ref, o_ref, qx_ref, k_ref, v_ref, wbuf, kx, vx, sem = refs[count:]
-    step = pl.program_id(0)
-    steps = pl.num_programs(0)
-    group = shards[0].shape[1] // 3
-    slot = lax.rem(step, 2)
-
-    @pl.when(step == 0)
-    def _():
-        for c in qkv_copies(3, index_ref, shards, wbuf, sem, 0, 0, group):
-            c.start()
-
-    @pl.when(step + 1 < steps)
-    def _():
-        for c in qkv_copies(3, index_ref, shards, wbuf, sem, step + 1, 1 - slot, group):
-            c.start()
-
-    for c in qkv_copies(3, index_ref, shards, wbuf, sem, step, slot, group):
+def forward_kernel(count, kept, quad, group, len_ref, index_ref, *refs):
+    shards, refs = refs[:count], refs[count + kept :]
+    n_ref, narrow_ref, upq_ref, upv_ref, o_ref, qx_ref, k_ref, v_ref, wbuf, kx, vx, sem = refs
+    copies = qkv_copies(index_ref, shards, wbuf, sem, quad, group)
+    for c in copies:
+        c.start()
+    for c in copies:
         c.wait()
     n = n_ref[...]
     narrow = narrow_ref[...]
-    q = dot(n, wbuf[slot, :, :QUAD]) + SCALE * dot(narrow, upq_ref[...])
-    k = dot(n, wbuf[slot, :, QUAD : 2 * QUAD])
-    v = dot(n, wbuf[slot, :, 2 * QUAD :]) + SCALE * dot(narrow, upv_ref[...])
+    q = dot(n, wbuf[:, :QUAD]) + SCALE * dot(narrow, upq_ref[...])
+    k = dot(n, wbuf[:, QUAD : 2 * QUAD])
+    v = dot(n, wbuf[:, 2 * QUAD :]) + SCALE * dot(narrow, upv_ref[...])
     q = q.astype(BF)
     k_ref[...] = k.astype(BF)
     v_ref[...] = v.astype(BF)
@@ -225,54 +214,66 @@
         )
 
 
-def attention_forward(lengths, index, shards, n, narrow, upq, upv):
+def attention_forward(lengths, index, shards, n, narrow, upq, upv, quad, group, at, kept):
     length, width = n.shape
-    group = shards[0].shape[1] // 3
-    steps = group // QUAD
-    quad = pl.BlockSpec((length, QUAD), lambda s: (0, s))
-    up = pl.BlockSpec((PAD, QUAD), lambda s: (0, s))
+    here = at // QUAD + quad
+    block = pl.BlockSpec((length, QUAD), lambda s: (0, here))
+    up = pl.BlockSpec((PAD, QUAD), lambda s: (0, here))
+    first = 2 + len(shards)
     return pl.pallas_call(
-        functools.partial(forward_kernel, len(shards)),
-        grid=(steps,),
+        functools.partial(forward_kernel, len(shards), len(kept), quad, group),
+        grid=(1,),
         in_specs=[SMEM, SMEM]
-        + [ANY] * len(shards)
+        + [ANY] * (len(shards) + len(kept))
         + [whole((length, width)), whole((length, PAD)), up, up],
-        out_specs=[quad, pl.BlockSpec((length, 2 * QUAD), lambda s: (0, s)), quad, quad],
+        out_specs=[block, pl.BlockSpec((length, 2 * QUAD), lambda s: (0, here)), block, block],
         out_shape=[
-            jax.ShapeDtypeStruct((length, group), BF),
-            jax.ShapeDtypeStruct((length, 2 * group), BF),
-            jax.ShapeDtypeStruct((length, group), BF),
-            jax.ShapeDtypeStruct((length, group), BF),
-        ],
+            jax.ShapeDtypeStruct((length, width), BF),
+            jax.ShapeDtypeStruct((length, 2 * width), BF),
+            jax.ShapeDtypeStruct((length, width), BF),
+            jax.ShapeDtypeStruct((length, width), BF),
+        ],
+        input_output_aliases={first + i: i for i in range(len(kept))},
         scratch_shapes=[
-            pltpu.VMEM((2, width, 3 * QUAD), BF),
+            pltpu.VMEM((width, 3 * QUAD), BF),
             pltpu.VMEM((2, length, PAIR), BF),
             pltpu.VMEM((length, QUAD), BF),
-            pltpu.SemaphoreType.DMA((2,)),
+            pltpu.SemaphoreType.DMA((3,)),
         ],
         compiler_params=params(),
+        cost_estimate=pl.CostEstimate(
+            flops=2 * length * width * 3 * QUAD + 16 * length * length * QUAD,
+            bytes_accessed=8 * 2**20,
+            transcendentals=4 * length * length,
+        ),
         name="attention_forward",
-    )(lengths, index, *shards, n, narrow, upq, upv)
-
-
-def ff_copies(index_ref, fcs, outs, fbuf, obuf, sem, step, slot):
+    )(lengths, index, *shards, *kept, n, narrow, upq, upv)
+
+
+def ff_copies(index_ref, fcs, outs, fbuf, obuf, sem, step):
     rows = fcs[0].shape[0]
+    per = outs[0].shape[0] // FF_STEP
+    slot = step % 2
+    shard, part = divmod(step, per)
+    col = pl.multiple_of((index_ref[shard] * per + part) * FF_STEP, FF_STEP)
     copies = []
     for i, ref in enumerate(fcs):
         at = pl.multiple_of(index_ref[i] * rows, rows)
-        src = ref.at[:, pl.ds(pl.multiple_of(step * FF_STEP, FF_STEP), FF_STEP)]
+        src = ref.at[:, pl.ds(col, FF_STEP)]
         copies.append(pltpu.make_async_copy(src, fbuf.at[slot, pl.ds(at, rows), :], sem.at[slot]))
-    src = outs.at[pl.ds(pl.multiple_of(step * FF_STEP, FF_STEP), FF_STEP), :]
+    src = outs[shard].at[part * FF_STEP : (part + 1) * FF_STEP, :]
     copies.append(pltpu.make_async_copy(src, obuf.at[slot], sem.at[slot]))
     return copies
 
 
-def proj_copies(index_ref, projs, wbuf, sem):
+def proj_copies(index_ref, projs, col, wbuf, sem):
     rows = projs[0].shape[0]
+    width = wbuf.shape[1]
     copies = []
     for i, ref in enumerate(projs):
         at = pl.multiple_of(index_ref[i] * rows, rows)
-        copies.append(pltpu.make_async_copy(ref, wbuf.at[pl.ds(at, rows), :], sem.at[0]))
+        src = ref.at[:, col : col + width]
+        copies.append(pltpu.make_async_copy(src, wbuf.at[pl.ds(at, rows), :], sem.at[0]))
     return copies
 
 
@@ -285,64 +286,58 @@
     return act, slope
 
 
-def middle_kernel(count, heads, len_ref, index_ref, *refs):
+def middle_kernel(count, col, len_ref, index_ref, *refs):
     projs, refs = refs[:count], refs[count:]
     fcs, refs = refs[:count], refs[count:]
-    outs, refs = refs[0], refs[1:]
-    atts, refs = refs[:heads], refs[heads:]
-    (x_ref, cot_ref, gain_ref, shift_ref, block_ref, gh_ref, ga_ref,
+    outs, refs = refs[:count], refs[count:]
+    (att_ref, x_ref, cot_ref, gain_ref, shift_ref, block_ref, gh_ref, ga_ref,
      wproj, fbuf, obuf, hidden, n2, low, acc, back, psem, sem) = refs
+    size = x_ref.shape[0]
+    steps = count * outs[0].shape[0] // FF_STEP
     step = pl.program_id(0)
-    steps = pl.num_programs(0)
-    size = x_ref.shape[0]
     slot = lax.rem(step, 2)
+    copies = functools.partial(ff_copies, index_ref, fcs, outs, fbuf, obuf, sem)
 
     @pl.when(step == 0)
     def _():
-        first = proj_copies(index_ref, projs, wproj, psem)
+        first = proj_copies(index_ref, projs, col, wproj, psem)
         for c in first:
             c.start()
-        for c in ff_copies(index_ref, fcs, outs, fbuf, obuf, sem, 0, 0):
+        for c in copies(0):
             c.start()
         for c in first:
             c.wait()
         for i in range(size // BLOCK):
             at = pl.ds(i * BLOCK, BLOCK)
-            total = x_ref[at, :].astype(F32)
-            for j, ref in enumerate(atts):
-                wide = ref.shape[1]
-                total = total + dot(ref[at, :], wproj[j * wide : (j + 1) * wide, :])
+            total = x_ref[at, :].astype(F32) + dot(att_ref[at, :], wproj[...])
             hidden[at, :] = total
             xhat, _ = norm_stats(total)
             n2[at, :] = (xhat * gain_ref[...] + shift_ref[...]).astype(BF)
             keep = row((BLOCK, 1)) + i * BLOCK < len_ref[0]
             low[at, :] = jnp.where(keep, cot_ref[at, :].astype(F32), 0.0).astype(BF)
-
-    @pl.when(step + 1 < steps)
-    def _():
-        for c in ff_copies(index_ref, fcs, outs, fbuf, obuf, sem, step + 1, 1 - slot):
-            c.start()
-
-    for c in ff_copies(index_ref, fcs, outs, fbuf, obuf, sem, step, slot):
-        c.wait()
-    fc = fbuf[slot]
-    out = obuf[slot]
+            acc[at, :] = jnp.zeros((BLOCK, x_ref.shape[1]), F32)
+            back[at, :] = jnp.zeros((BLOCK, x_ref.shape[1]), F32)
+
+    for s in range(1, steps):
+
+        @pl.when(step + 1 == s)
+        def _(s=s):
+            for c in copies(s):
+                c.start()
+
+    for even in range(2):
+
+        @pl.when(slot == even)
+        def _(even=even):
+            for c in copies(even):
+                c.wait()
+
     for i in range(size // BLOCK):
         at = pl.ds(i * BLOCK, BLOCK)
-        act, slope = gelu_both(dot(n2[at, :], fc))
-        mlp = dot(act.astype(BF), out)
-        grad = (dot_nt(low[at, :], out) * slope).astype(BF)
-        u = dot_nt(grad, fc)
-
-        @pl.when(step == 0)
-        def _():
-            acc[at, :] = mlp
-            back[at, :] = u
-
-        @pl.when(step > 0)
-        def _():
-            acc[at, :] += mlp
-            back[at, :] += u
+        act, slope = gelu_both(dot(n2[at, :], fbuf[slot]))
+        acc[at, :] += dot(act.astype(BF), obuf[slot])
+        grad = (dot_nt(low[at, :], obuf[slot]) * slope).astype(BF)
+        back[at, :] += dot_nt(grad, fbuf[slot])
 
     @pl.when(step == steps - 1)
     def _():
@@ -357,19 +352,15 @@
             ga_ref[at, :] = dot_nt(gh.astype(BF), wproj[...]).astype(BF)
 
 
-def middle(lengths, index, projs, fcs, outs, atts, x, cot, gain, shift):
+def middle(lengths, index, projs, col, fcs, outs, att, x, cot, gain, shift):
     size, width = x.shape
-    hidden_units = outs.shape[0]
-    full = whole((size, width))
-    once = pl.BlockSpec((size, width), lambda s: (0, 0), pipeline_mode=pl.Buffered(1))
+    vm = pl.BlockSpec(memory_space=pltpu.VMEM)
+    units = len(outs) * outs[0].shape[0]
     return pl.pallas_call(
-        functools.partial(middle_kernel, len(projs), len(atts)),
-        grid=(hidden_units // FF_STEP,),
-        in_specs=[SMEM, SMEM]
-        + [ANY] * (2 * len(projs) + 1)
-        + [whole(a.shape) for a in atts]
-        + [once, once, whole((1, width)), whole((1, width))],
-        out_specs=[full, full, full],
+        functools.partial(middle_kernel, len(projs), col),
+        grid=(units // FF_STEP,),
+        in_specs=[SMEM, SMEM] + [ANY] * (3 * len(projs)) + [vm] * 5,
+        out_specs=[vm] * 3,
         out_shape=[
             jax.ShapeDtypeStruct((size, width), BF),
             jax.ShapeDtypeStruct((size, width), F32),
@@ -388,8 +379,13 @@
             pltpu.SemaphoreType.DMA((2,)),
         ],
         compiler_params=params(),
+        cost_estimate=pl.CostEstimate(
+            flops=8 * size * width * units + 4 * size * width * width,
+            bytes_accessed=32 * 2**20,
+            transcendentals=size * units,
+        ),
         name="middle",
-    )(lengths, index, *projs, *fcs, outs, *atts, x, cot, gain, shift)
+    )(lengths, index, *projs, *fcs, *outs, att, x, cot, gain, shift)
 
 
 def backward_kernel(
@@ -455,18 +451,16 @@
     dq_ref[...] = (jnp.where(first, dqa[0], dqa[1]) * (1.0 / HD**0.5)).astype(BF)
 
 
-def attention_backward(lengths, qx, k, v, o, ga, at):
+def attention_backward(lengths, qx, k, v, o, ga):
     size, group = k.shape
     pair = pl.BlockSpec((size, PAIR), lambda p: (0, p))
-    start = at // PAIR
     return pl.pallas_call(
         backward_kernel,
         grid=(group // PAIR,),
         in_specs=[
             SMEM,
             pl.BlockSpec((size, 2 * PAIR), lambda p: (0, p)),
-            pair, pair, pair,
-            pl.BlockSpec((size, PAIR), lambda p: (0, p + start)),
+            pair, pair, pair, pair,
         ],
         out_specs=[pair] * 3,
         out_shape=[jax.ShapeDtypeStruct((size, group), BF)] * 3,
@@ -476,48 +470,39 @@
     )(lengths, qx, k, v, o, ga)
 
 
-def adapter_kernel(groups, *refs):
-    dqs, refs = refs[:groups], refs[groups:]
-    dvs, refs = refs[:groups], refs[groups:]
-    n_ref, narrow_ref, upq_ref, upv_ref, joint_ref, sums_ref = refs
+def adapter_kernel(dq_ref, dv_ref, n_ref, narrow_ref, upq_ref, upv_ref, joint_ref, sums_ref):
     narrow = narrow_ref[...]
-    total = None
-    for j in range(groups):
-        wide = dqs[j].shape[1]
-        cols = slice(j * wide, (j + 1) * wide)
-        dq = dqs[j][...]
-        dv = dvs[j][...]
-        part = dot_nt(dq, upq_ref[:, cols]) + dot_nt(dv, upv_ref[:, cols])
-        total = part if total is None else total + part
-        gq = SCALE * dot_tn(narrow, dq)
-        gv = SCALE * dot_tn(narrow, dv)
-        sums_ref[8:16, cols] = jnp.where(row((8, wide)) < 4, gq[:8], gv[:8])
-    joint = (SCALE * total).astype(BF)
+    dq = dq_ref[...]
+    dv = dv_ref[...]
+    joint = (SCALE * (dot_nt(dq, upq_ref[...]) + dot_nt(dv, upv_ref[...]))).astype(BF)
     joint_ref[...] = joint
+    gq = SCALE * dot_tn(narrow, dq)[:8]
+    gv = SCALE * dot_tn(narrow, dv)[:8]
     sums_ref[0:8, :] = dot_tn(joint, n_ref[...])[:8]
-
-
-def adapter_sums(dqs, dvs, n, narrow, upq, upv):
+    sums_ref[8:16, :] = jnp.where(row(gq.shape) < 4, gq, gv)
+
+
+def adapter_sums(dq, dv, n, narrow, upq, upv):
     size, width = n.shape
     return pl.pallas_call(
-        functools.partial(adapter_kernel, len(dqs)),
+        adapter_kernel,
         out_shape=[
             jax.ShapeDtypeStruct((size, PAD), BF),
             jax.ShapeDtypeStruct((16, width), F32),
         ],
         compiler_params=params(),
         name="adapter_sums",
-    )(*dqs, *dvs, n, narrow, upq, upv)
-
-
-def token_copies(index_ref, shards, wbuf, sem, step, slot, group):
+    )(dq, dv, n, narrow, upq, upv)
+
+
+def token_copies(index_ref, shards, wbuf, sem, part, slot, group):
     rows = shards[0].shape[0]
     copies = []
     for i, ref in enumerate(shards):
         at = pl.multiple_of(index_ref[i] * rows, rows)
         copies.append(
             pltpu.make_async_copy(
-                ref.at[:, step * group : (step + 1) * group],
+                ref.at[:, part * group : (part + 1) * group],
                 wbuf.at[slot, pl.ds(at, rows), :],
                 sem.at[slot],
             )
@@ -525,19 +510,19 @@
     return copies
 
 
-def token_kernel(count, groups, index_ref, *refs):
-    shards, refs = refs[: count * groups], refs[count * groups :]
-    grads, refs = refs[: 3 * groups], refs[3 * groups :]
+def token_kernel(counts, group, index_ref, *refs):
+    shards = []
+    for count in counts:
+        shards.append(refs[:count])
+        refs = refs[count:]
+    grads, refs = refs[:3], refs[3:]
     joint_ref, down_ref, gh_ref, x_ref, gain_ref, o_ref, wbuf, acc, sem = refs
     size = x_ref.shape[0]
-    group = shards[0].shape[1] // 3
-    steps = [(j, p) for j in range(groups) for p in range(3)]
+    steps = [(j, p) for j in range(len(counts)) for p in range(3)]
 
     def copies(s):
         j, p = steps[s]
-        return token_copies(
-            index_ref, shards[j * count : (j + 1) * count], wbuf, sem, p, s % 2, group
-        )
+        return token_copies(index_ref, shards[j], wbuf, sem, p, s % 2, group)
 
     for c in copies(0):
         c.start()
@@ -547,10 +532,9 @@
                 c.start()
         for c in copies(s):
             c.wait()
-        g = grads[p * groups + j]
         for i in range(size // BLOCK):
             at = pl.ds(i * BLOCK, BLOCK)
-            part = dot_nt(g[at, :], wbuf[s % 2])
+            part = dot_nt(grads[p][at, j * group : (j + 1) * group], wbuf[s % 2])
             if s == 0:
                 part = part + dot(joint_ref[at, :], down_ref[...])
             else:
@@ -564,16 +548,13 @@
                 ).astype(BF)
 
 
-def token_gradient(index, shards, dqs, dks, dvs, joint, down, gh, x, gain):
+def token_gradient(index, shards, group, dq, dk, dv, joint, down, gh, x, gain):
     size, width = x.shape
-    groups = len(dqs)
-    count = len(shards[0])
-    group = shards[0][0].shape[1] // 3
     flat = [s for part in shards for s in part]
     vm = pl.BlockSpec(memory_space=pltpu.VMEM)
     return pl.pallas_call(
-        functools.partial(token_kernel, count, groups),
-        in_specs=[SMEM] + [ANY] * len(flat) + [vm] * (3 * groups + 5),
+        functools.partial(token_kernel, [len(p) for p in shards], group),
+        in_specs=[SMEM] + [ANY] * len(flat) + [vm] * 8,
         out_specs=vm,
         out_shape=jax.ShapeDtypeStruct((size, width), BF),
         scratch_shapes=[
@@ -582,37 +563,103 @@
             pltpu.SemaphoreType.DMA((2,)),
         ],
         compiler_params=params(),
+        cost_estimate=pl.CostEstimate(
+            flops=6 * size * width * width, bytes_accessed=20 * 2**20, transcendentals=0
+        ),
         name="token_gradient",
-    )(index, *flat, *dqs, *dks, *dvs, joint, down, gh, x, gain)
+    )(index, *flat, dq, dk, dv, joint, down, gh, x, gain)
+
+
+BOTH = ("dp", "fsdp")
+
+
+def swap(value, fn, total):
+    return lax.ppermute(value, BOTH, [(i, fn(i)) for i in range(total)])
+
+
+def cube_gather(w, after, total, fsdp):
+    if after is not None:
+        w, _ = lax.optimization_barrier((w, after))
+
+    def even(i):
+        return (i // fsdp) % 2 == 0
+
+    a = swap(w, lambda i: i ^ (2 if even(i) else 4), total)
+    b = swap(a, lambda i: i ^ (4 if even(i) else 2), total)
+    c = swap(a, lambda i: i ^ fsdp, total)
+    pairs = []
+    for part in (w, a, b, c):
+        pairs += [part, swap(part, lambda i: i ^ 1, total)]
+    return pairs, a
+
+
+def all_sum(value, total):
+    if total & (total - 1):
+        return lax.psum(value, BOTH)
+    half = value.shape[0] // 2
+    odd = lax.axis_index("fsdp") % 2
+    mine = lax.dynamic_slice_in_dim(value, odd * half, half)
+    other = lax.dynamic_slice_in_dim(value, (1 - odd) * half, half)
+    mine = mine + swap(other, lambda i: i ^ 1, total)
+    bit = 2
+    while bit < total:
+        mine = mine + swap(mine, lambda i, bit=bit: i ^ bit, total)
+        bit *= 2
+    other = swap(mine, lambda i: i ^ 1, total)
+    top = jnp.where(odd == 0, mine, other)
+    low = jnp.where(odd == 0, other, mine)
+    return jnp.concatenate([top, low], axis=0)
 
 
 def local(
-    tokens, lengths, cotangent, gain_one, shift_one, gain_two, shift_two,
+    sizes, tokens, lengths, cotangent, gain_one, shift_one, gain_two, shift_two,
     w_qkv, w_proj, w_fc, w_out,
     query_down_factor, query_up_factor, value_down_factor, value_up_factor,
 ):
     _, size, width = tokens.shape
+    dp, fsdp = sizes
+    total = dp * fsdp
     x = tokens.reshape(size, width)
     cot = cotangent.reshape(size, width)
-
-    def gather(w):
-        return lax.all_gather(w, "fsdp", axis=0, tiled=True)
-
-    qkv, proj, fc, out = gather(w_qkv), gather(w_proj), gather(w_fc), gather(w_out)
-    index = jnp.zeros((1,), jnp.int32)
+    group = width // 2
+    cols = [jnp.concatenate([w_qkv[:, p * width + j * group : p * width + (j + 1) * group]
+                             for p in range(3)] + ([w_proj] if j else []), axis=1)
+            for j in range(2)]
+    if fsdp == 8 and dp % 2 == 0:
+        here = lax.axis_index("fsdp").astype(jnp.int32)
+        odd = lax.axis_index("dp").astype(jnp.int32) % 2
+        a, c = 2 + 2 * odd, 4 - 2 * odd
+        index = jnp.stack([here ^ (m ^ s) for m in (0, a, 6, c) for s in (0, 1)])
+        first, sent = cube_gather(cols[0], None, total, fsdp)
+        second, sent = cube_gather(cols[1], sent, total, fsdp)
+        fcs, sent = cube_gather(w_fc, sent, total, fsdp)
+        outs, sent = cube_gather(w_out, sent, total, fsdp)
+    else:
+        index = jnp.zeros((1,), jnp.int32)
+        first, second, fcs, outs = [
+            [lax.all_gather(w, "fsdp", axis=0, tiled=True)] for w in cols + [w_fc, w_out]
+        ]
 
     n, narrow, down, upq, upv = norm_one(
         x, gain_one[None], shift_one[None],
         query_down_factor.T, value_down_factor.T, query_up_factor, value_up_factor,
     )
-    o, qx, k, v = attention_forward(lengths, index, [qkv], n, narrow, upq, upv)
+    kept = []
+    for j, shards in enumerate((first, second)):
+        for quad in range(group // QUAD):
+            kept = attention_forward(
+                lengths, index, shards, n, narrow, upq, upv, quad, group, j * group, kept
+            )
+    o, qx, k, v = kept
     block_out, gh, ga = middle(
-        lengths, index, [proj], [fc], out, [o], x, cot, gain_two[None], shift_two[None]
+        lengths, index, second, 3 * group, fcs, outs, o, x, cot, gain_two[None], shift_two[None]
     )
-    dq, dk, dv = attention_backward(lengths, qx, k, v, o, ga, 0)
-    joint, sums = adapter_sums([dq], [dv], n, narrow, upq, upv)
-    sums = lax.psum(sums, ("dp", "fsdp"))
-    grad = token_gradient(index, [[qkv]], [dq], [dk], [dv], joint, down, gh, x, gain_one[None])
+    dq, dk, dv = attention_backward(lengths, qx, k, v, o, ga)
+    joint, sums = adapter_sums(dq, dv, n, narrow, upq, upv)
+    sums = all_sum(sums, total)
+    grad = token_gradient(
+        index, [first, second], group, dq, dk, dv, joint, down, gh, x, gain_one[None]
+    )
     return (
         block_out.reshape(tokens.shape),
         grad.reshape(tokens.shape),
@@ -624,14 +671,12 @@
 
 
 def solution(mesh):
-    rows = P(("dp", "fsdp"), None, None)
+    rows = P(BOTH, None, None)
     frozen = P("fsdp", None)
     return jax.shard_map(
-        local,
+        functools.partial(local, (mesh.shape["dp"], mesh.shape["fsdp"])),
         mesh=mesh,
-        in_specs=(rows, P(("dp", "fsdp")), rows, P(), P(), P(), P())
-        + (frozen,) * 4
-        + (P(),) * 4,
+        in_specs=(rows, P(BOTH), rows, P(), P(), P(), P()) + (frozen,) * 4 + (P(),) * 4,
         out_specs=(rows, rows, P(), P(), P(), P()),
         check_vma=False,
     )

time: 473 us -> 309 us (0.65)
  waiting for transfers between devices: 254 us -> 55.4 us
  starting transfers between devices: 0.19 us -> 44.6 us
  between operations: 14.6 us -> 1.84 us
    all_gather x4 -> x0, waiting for transfers between devices: 149 us -> none  [gather(): return lax.all_gather(w, 'fsdp', axis=0, tiled=True)]
    psum x1 -> x0, waiting for transfers between devices: 102 us -> none  [local(): sums = lax.psum(sums, ('dp', 'fsdp'))]
    ppermute x0 -> x34, waiting for transfers between devices: none -> 55.4 us  [swap(): return lax.ppermute(value, BOTH, [(i, fn(i)) for i in range(total)])]
    ppermute x0 -> x34, starting transfers between devices: none -> 44.6 us  [swap(): return lax.ppermute(value, BOTH, [(i, fn(i)) for i in range(total)])]
    pallas_call x4 -> x7, Pallas kernels: 140 us -> 136 us  [the longest x1 62.3 us: middle(): pl.pallas_call(functools.partial(middle_kernel, len(projs), col), grid=(u...]
  transfers between devices with their start and end apart: 5 -> 34, of which waited for: 4 -> 13; matrix products, arithmetic and copies ran while one was open for 0% -> 0% of each run, Pallas kernels for 12% -> 24%
where the time goes in v2:
time: 309 us; the launch traced here: 306 us
  Pallas kernels  198 us (64%)
  waiting for transfers between devices  55.4 us (18%)
  starting transfers between devices  44.6 us (14%)
  local copies, waits for them, and re-layouts  5.2 us (2%)
    pallas_call x1, Pallas kernels, middle(): pl.pallas_call(functools.partial(middle_kernel, len(projs), col), grid=(u...  62.3 us
    pallas_call x1, Pallas kernels, attention_backward(): pl.pallas_call(backward_kernel, grid=(group // PAIR,), in_specs=[SMEM, pl...  57 us
    ppermute x34, waiting for transfers between devices, swap(): return lax.ppermute(value, BOTH, [(i, fn(i)) for i in range(total)])  55.4 us
    pallas_call x4, Pallas kernels, attention_forward(): pl.pallas_call(functools.partial(forward_kernel, len(shards), len(kept),...  49.4 us
    ppermute x34, starting transfers between devices, swap(): return lax.ppermute(value, BOTH, [(i, fn(i)) for i in range(total)])  44.6 us
    pallas_call x1, Pallas kernels, token_gradient(): pl.pallas_call(functools.partial(token_kernel, [len(p) for p in shards],...  17.7 us
    pallas_call x1, Pallas kernels, adapter_sums(): pl.pallas_call(adapter_kernel, out_shape=[jax.ShapeDtypeStruct((size, PAD...  6.25 us
  transfers between devices with their start and end apart: 34, of which 13 were waited for; matrix products, arithmetic and copies ran while one was open for 0% of the time, Pallas kernels for 24%

profile of v2, /device:TPU:1, one launch (start us, length us, event | category | flops | bytes accessed | tf_op | source)
XLA Modules:
  0.0 305.6 jit_solution(15905517026456835411)
XLA Ops:
  0.7 1.4 fusion
  2.1 2.1 collective-permute-start
  4.3 8.8 %collective-permute-done.refs_2_ = bf16[128,1536]{1,0:T(8,128)(2,1)S(1)} collective-permute-done((bf16[128,1536]{1,0:T(8,128)(2,1)S(1)}, bf16[128,1536]{1,0:T(8,128)(2,1)S(1)}, u32[]{:S(2)}, u32[]{:S(2)}) %collective-permute-start) | collective-permute-done | bytes 393248 | tf_op jit(solution)/shard_map/ppermute | solution.py:577
  14.2 1.8 collective-permute-start.22
  16.1 12.0 %collective-permute-done.2.refs_2_.refs_10_ = bf16[128,2560]{1,0:T(8,128)(2,1)S(1)} collective-permute-done((bf16[128,2560]{1,0:T(8,128)(2,1)S(1)}, bf16[128,2560]{1,0:T(8,128)(2,1)S(1)}, u32[]{:S(2)}, u32[]{:S(2)}) %collective-permute-start.2) | collective-permute-done | bytes 655392 | tf_op jit(solution)/shard_map/ppermute | solution.py:577
  31.4 3.3 %collective-permute-start.1 = (bf16[128,2560]{1,0:T(8,128)(2,1)S(1)}, bf16[128,2560]{1,0:T(8,128)(2,1)S(1)}, u32[]{:S(2)}, u32[]{:S(2)}) collective-permute-start(bf16[128,2560]{1,0:T(8,128)(2,1)S(1)} %pad_maximum_fusion.refs_0_.refs_8_), channel_id=1, source_target_pairs={{0,1},{1,0},{2,3},{3,2},{4,5},{5,4},{6,7},{7,6},{8,9},{9,8},{10,11... | collective-permute-start | bytes 1966088 | tf_op jit(solution)/shard_map/ppermute | solution.py:577
  34.8 1.9 collective-permute-done.24.refs_4_
  36.8 3.7 %collective-permute-start.25 = (bf16[128,1536]{1,0:T(8,128)(2,1)S(1)}, bf16[128,1536]{1,0:T(8,128)(2,1)S(1)}, u32[]{:S(2)}, u32[]{:S(2)}) collective-permute-start(bf16[128,1536]{1,0:T(8,128)(2,1)S(1)} %collective-permute-done.24.refs_4_), channel_id=1, source_target_pairs={{0,1},{1,0},{2,3},{3,2},{4,5},{5,4},{6,7},{7,6},{8,9},{9,8},{10,11... | collective-permute-start | bytes 1179656 | tf_op jit(solution)/shard_map/ppermute | solution.py:577
  42.2 1.3 collective-permute-start.6
  44.0 6.7 %collective-permute-done.9.refs_10_ = bf16[128,4096]{1,0:T(8,128)(2,1)S(1)} collective-permute-done((bf16[128,4096]{1,0:T(8,128)(2,1)S(1)}, bf16[128,4096]{1,0:T(8,128)(2,1)S(1)}, u32[]{:S(2)}, u32[]{:S(2)}) %collective-permute-start.9) | collective-permute-done | bytes 1048608 | tf_op jit(solution)/shard_map/ppermute | solution.py:577
  50.7 3.0 collective-permute-start.8
  55.6 2.1 collective-permute-start.15
  61.0 5.0 %norm_one.1 = (bf16[1024,1024]{1,0:T(8,128)(2,1)}, bf16[1024,128]{1,0:T(8,128)(2,1)}, bf16[128,1024]{1,0:T(8,128)(2,1)}, bf16[128,1024]{1,0:T(8,128)(2,1)}, bf16[128,1024]{1,0:T(8,128)(2,1)}) custom-call(bf16[1024,1024]{1,0:T(8,128)(2,1)} %bitcast.22, f32[1,1024]{1,0:T(1,128)} %bitcast.28, f32[1,1024]{1,0:T(1,128)} %bitcast.27, f32[4,1024]{1,0:T(4,128)} %bitcast.25, ...), custom_call_target="tpu_custom_call" | custom-call | tf_op jit(solution)/shard_map/norm_one/pallas_call | solution.py:108
  67.9 1.3 collective-permute-start.13
  69.7 8.9 %collective-permute-done.16.refs_18_ = bf16[512,1024]{1,0:T(8,128)(2,1)} collective-permute-done((bf16[512,1024]{1,0:T(8,128)(2,1)S(1)}, bf16[512,1024]{1,0:T(8,128)(2,1)}, u32[]{:S(2)}, u32[]{:S(2)}) %collective-permute-start.16) | collective-permute-done | bytes 1048608 | tf_op jit(solution)/shard_map/ppermute | solution.py:577
  80.7 12.2 %attention_forward.4 = (bf16[1024,1024]{1,0:T(8,128)(2,1)}, bf16[1024,2048]{1,0:T(8,128)(2,1)}, bf16[1024,1024]{1,0:T(8,128)(2,1)}, bf16[1024,1024]{1,0:T(8,128)(2,1)}) custom-call(s32[1]{0:T(128)S(6)} %copy.45.len_ref, s32[8]{0:T(128)} %stack.35.index_ref, bf16[128,1536]{1,0:T(8,128)(2,1)} %copy-done.1, bf16[128,1536]{1,0:T(8,128)(2,1)} %copy-done.15, ...), custom_call_target="tpu_custom_call" | custom-call | flops 5905580032 | bytes 8388608 | tf_op jit(solution)/shard_map/attention_forward/pallas_call | solution.py:223
  93.0 12.7 %attention_forward.5 = (bf16[1024,1024]{1,0:T(8,128)(2,1)}, bf16[1024,2048]{1,0:T(8,128)(2,1)}, bf16[1024,1024]{1,0:T(8,128)(2,1)}, bf16[1024,1024]{1,0:T(8,128)(2,1)}) custom-call(s32[1]{0:T(128)S(6)} %copy.45.len_ref, s32[8]{0:T(128)} %stack.35.index_ref, ...), custom_call_target="tpu_custom_call", output_to_operand_aliasing={{0}: (10, {}), {1}: (11, {}), {2}: (12, {}), {3}: (13, {})} | custom-call | flops 5905580032 | bytes 8388608 | tf_op jit(solution)/shard_map/attention_forward/pallas_call | solution.py:223
  105.7 1.4 collective-permute-start.17
  107.6 6.6 %collective-permute-done.18.refs_20_ = bf16[512,1024]{1,0:T(8,128)(2,1)} collective-permute-done((bf16[512,1024]{1,0:T(8,128)(2,1)}, bf16[512,1024]{1,0:T(8,128)(2,1)}, u32[]{:S(2)}, u32[]{:S(2)}) %collective-permute-start.18) | collective-permute-done | bytes 1048608 | tf_op jit(solution)/shard_map/ppermute | solution.py:577
  116.1 12.2 %attention_forward.6 = (bf16[1024,1024]{1,0:T(8,128)(2,1)}, bf16[1024,2048]{1,0:T(8,128)(2,1)}, bf16[1024,1024]{1,0:T(8,128)(2,1)}, bf16[1024,1024]{1,0:T(8,128)(2,1)}) custom-call(s32[1]{0:T(128)S(6)} %copy.45.len_ref, s32[8]{0:T(128)} %stack.35.index_ref, ...), custom_call_target="tpu_custom_call", output_to_operand_aliasing={{0}: (10, {}), {1}: (11, {}), {2}: (12, {}), {3}: (13, {})} | custom-call | flops 5905580032 | bytes 8388608 | tf_op jit(solution)/shard_map/attention_forward/pallas_call | solution.py:223
  128.4 12.2 %attention_forward.7 = (bf16[1024,1024]{1,0:T(8,128)(2,1)}, bf16[1024,2048]{1,0:T(8,128)(2,1)}, bf16[1024,1024]{1,0:T(8,128)(2,1)}, bf16[1024,1024]{1,0:T(8,128)(2,1)}) custom-call(s32[1]{0:T(128)S(6)} %copy.45.len_ref, s32[8]{0:T(128)} %stack.35.index_ref, ...), custom_call_target="tpu_custom_call", output_to_operand_aliasing={{0}: (10, {}), {1}: (11, {}), {2}: (12, {}), {3}: (13, {})} | custom-call | flops 5905580032 | bytes 8388608 | tf_op jit(solution)/shard_map/attention_forward/pallas_call | solution.py:223
  141.6 62.3 %middle.1 = (bf16[1024,1024]{1,0:T(8,128)(2,1)}, f32[1024,1024]{1,0:T(8,128)}, bf16[1024,1024]{1,0:T(8,128)(2,1)}) custom-call(s32[1]{0:T(128)S(6)} %copy.45.len_ref, s32[8]{0:T(128)} %stack.35.index_ref, bf16[128,2560]{1,0:T(8,128)(2,1)} %copy-done, bf16[128,2560]{1,0:T(8,128)(2,1)} %copy-done.12, bf16[128,2560]{1,0:T(8,128)(2,1)} %copy-done.11, ...), custom_call_target="tpu_custom_call" | custom-call | flops 38654705664 | bytes 33554432 | tf_op jit(solution)/shard_map/middle/pallas_call | solution.py:359
  204.0 57.0 %attention_backward.1 = (bf16[1024,1024]{1,0:T(8,128)(2,1)}, bf16[1024,1024]{1,0:T(8,128)(2,1)}, bf16[1024,1024]{1,0:T(8,128)(2,1)}) custom-call(s32[1]{0:T(128)S(6)} %copy.45.len_ref, bf16[1024,2048]{1,0:T(8,128)(2,1)} %get-tuple-element.59.qx_ref, bf16[1024,1024]{1,0:T(8,128)(2,1)} %get-tuple-element.60.k_ref, bf16[1024,1024]{1,0:T(8,128)(2,1)} %get-tuple-element.61.v_ref, ...), custom_call_target="tpu_custom_call" | custom-call | tf_op jit(solution)/shard_map/attention_backward/pallas_call | solution.py:457
  261.0 6.2 %adapter_sums.1 = (bf16[1024,128]{1,0:T(8,128)(2,1)}, f32[16,1024]{1,0:T(8,128)}) custom-call(bf16[1024,1024]{1,0:T(8,128)(2,1)} %get-tuple-element.63.dq_ref.refs_16_, bf16[1024,1024]{1,0:T(8,128)(2,1)} %get-tuple-element.65.dv_ref.refs_18_, bf16[1024,1024]{1,0:T(8,128)(2,1)} %get-tuple-element.41.refs_8_.refs_12_.n_ref, ...), custom_call_target="tpu_custom_call" | custom-call | tf_op jit(solution)/shard_map/adapter_sums/pallas_call | solution.py:487
  270.3 2.5 collective-permute-done.29
  273.3 2.3 collective-permute-done.30
  275.6 1.3 collective-permute-start.31
  276.9 1.5 collective-permute-done.31
  278.4 2.3 collective-permute-start.32
  280.7 1.3 collective-permute-done.32
  282.0 4.9 %collective-permute-start.33 = (f32[8,1024]{1,0:T(8,128)S(1)}, f32[8,1024]{1,0:T(8,128)S(1)}, u32[]{:S(2)}, u32[]{:S(2)}) collective-permute-start(f32[8,1024]{1,0:T(8,128)S(1)} %add.40), channel_id=1, source_target_pairs={{0,1},{1,0},{2,3},{3,2},{4,5},{5,4},{6,7},{7,6},{8,9},{9,8},{10,11... | collective-permute-start | bytes 98312 | tf_op jit(solution)/shard_map/ppermute | solution.py:577
  287.0 17.7 %token_gradient.1 = bf16[1024,1024]{1,0:T(8,128)(2,1)} custom-call(s32[8]{0:T(128)} %stack.35.index_ref, bf16[128,1536]{1,0:T(8,128)(2,1)} %copy-done.1, bf16[128,1536]{1,0:T(8,128)(2,1)} %copy-done.15, bf16[128,1536]{1,0:T(8,128)(2,1)} %copy-done.14, bf16[128,1536]{1,0:T(8,128)(2,1)} %copy-done.18, bf16[128,1536]{1,0:T(8,128)(2,1)} %copy-done.16, ...), custom_call_target="tpu_custom_call" | custom-call | flops 6442450944 | bytes 20971520 | tf_op jit(solution)/shard_map/token_gradient/pallas_call | solution.py:555
  (99 shorter events, 23.5 us)
Async XLA Ops:
  2.1 10.9 %collective-permute-start = (bf16[128,1536]{1,0:T(8,128)(2,1)S(1)}, bf16[128,1536]{1,0:T(8,128)(2,1)S(1)}, u32[]{:S(2)}, u32[]{:S(2)}) collective-permute-start(bf16[128,1536]{1,0:T(8,128)(2,1)S(1)} %pad_maximum_fusion.1.refs_0_), channel_id=1, source_target_pairs={{0,2},{1,3},{2,0},{3,1},{4,6},{5,7},{6,4},{7,5},{8,12},{9,13},{10,... | collective-permute-start | bytes 1179656 | tf_op jit(solution)/shard_map/ppermute | solution.py:577
  13.1 15.0 %collective-permute-start.2 = (bf16[128,2560]{1,0:T(8,128)(2,1)S(1)}, bf16[128,2560]{1,0:T(8,128)(2,1)S(1)}, u32[]{:S(2)}, u32[]{:S(2)}) collective-permute-start(bf16[128,2560]{1,0:T(8,128)(2,1)S(1)} %pad_maximum_fusion.refs_0_.refs_8_), channel_id=1, source_target_pairs={{0,2},{1,3},{2,0},{3,1},{4,6},{5,7},{6,4},{7,5},{8,12},{9,13},{10,... | collective-permute-start | bytes 1966088 | tf_op jit(solution)/shard_map/ppermute | solution.py:577
  14.2 20.5 %collective-permute-start.22 = (bf16[128,1536]{1,0:T(8,128)(2,1)S(1)}, bf16[128,1536]{1,0:T(8,128)(2,1)S(1)}, u32[]{:S(2)}, u32[]{:S(2)}) collective-permute-start(bf16[128,1536]{1,0:T(8,128)(2,1)S(1)} %pad_maximum_fusion.1.refs_0_), channel_id=1, source_target_pairs={{0,1},{1,0},{2,3},{3,2},{4,5},{5,4},{6,7},{7,6},{8,9},{9,8},{10,11... | collective-permute-start | bytes 1179656 | tf_op jit(solution)/shard_map/ppermute | solution.py:577
  28.1 22.6 %collective-permute-start.9 = (bf16[128,4096]{1,0:T(8,128)(2,1)S(1)}, bf16[128,4096]{1,0:T(8,128)(2,1)S(1)}, u32[]{:S(2)}, u32[]{:S(2)}) collective-permute-start(bf16[128,4096]{1,0:T(8,128)(2,1)S(1)} %copy-done.3), channel_id=1, source_target_pairs={{0,2},{1,3},{2,0},{3,1},{4,6},{5,7},{6,4},{7,5},{8,12},{9,13},{10,... | collective-permute-start | bytes 3145736 | tf_op jit(solution)/shard_map/ppermute | solution.py:577
  28.9 7.9 %collective-permute-start.24 = (bf16[128,1536]{1,0:T(8,128)(2,1)S(1)}, bf16[128,1536]{1,0:T(8,128)(2,1)S(1)}, u32[]{:S(2)}, u32[]{:S(2)}) collective-permute-start(bf16[128,1536]{1,0:T(8,128)(2,1)S(1)} %collective-permute-done.refs_2_), channel_id=1, source_target_pairs={{0,4},{1,5},{2,6},{3,7},{4,0},{5,1},{6,2},{7,3},{8,10},{9,11},{10,... | collective-permute-start | bytes 1179656 | tf_op jit(solution)/shard_map/ppermute | solution.py:577
  30.2 10.3 %collective-permute-start.26 = (bf16[128,1536]{1,0:T(8,128)(2,1)S(1)}, bf16[128,1536]{1,0:T(8,128)(2,1)S(1)}, u32[]{:S(2)}, u32[]{:S(2)}) collective-permute-start(bf16[128,1536]{1,0:T(8,128)(2,1)S(1)} %collective-permute-done.refs_2_), channel_id=1, source_target_pairs={{0,8},{1,9},{2,10},{3,11},{4,12},{5,13},{6,14},{7,15},{8,0},{9,1},... | collective-permute-start | bytes 1179656 | tf_op jit(solution)/shard_map/ppermute | solution.py:577
  31.4 10.8 %collective-permute-start.1 = (bf16[128,2560]{1,0:T(8,128)(2,1)S(1)}, bf16[128,2560]{1,0:T(8,128)(2,1)S(1)}, u32[]{:S(2)}, u32[]{:S(2)}) collective-permute-start(bf16[128,2560]{1,0:T(8,128)(2,1)S(1)} %pad_maximum_fusion.refs_0_.refs_8_), channel_id=1, source_target_pairs={{0,1},{1,0},{2,3},{3,2},{4,5},{5,4},{6,7},{7,6},{8,9},{9,8},{10,11... | collective-permute-start | bytes 1966088 | tf_op jit(solution)/shard_map/ppermute | solution.py:577
  34.8 6.9 %collective-permute-start.23 = (bf16[128,1536]{1,0:T(8,128)(2,1)S(1)}, bf16[128,1536]{1,0:T(8,128)(2,1)S(1)}, u32[]{:S(2)}, u32[]{:S(2)}) collective-permute-start(bf16[128,1536]{1,0:T(8,128)(2,1)S(1)} %collective-permute-done.refs_2_), channel_id=1, source_target_pairs={{0,1},{1,0},{2,3},{3,2},{4,5},{5,4},{6,7},{7,6},{8,9},{9,8},{10,11... | collective-permute-start | bytes 1179656 | tf_op jit(solution)/shard_map/ppermute | solution.py:577
  36.8 6.8 %collective-permute-start.25 = (bf16[128,1536]{1,0:T(8,128)(2,1)S(1)}, bf16[128,1536]{1,0:T(8,128)(2,1)S(1)}, u32[]{:S(2)}, u32[]{:S(2)}) collective-permute-start(bf16[128,1536]{1,0:T(8,128)(2,1)S(1)} %collective-permute-done.24.refs_4_), channel_id=1, source_target_pairs={{0,1},{1,0},{2,3},{3,2},{4,5},{5,4},{6,7},{7,6},{8,9},{9,8},{10,11... | collective-permute-start | bytes 1179656 | tf_op jit(solution)/shard_map/ppermute | solution.py:577
  40.5 15.2 %collective-permute-start.4 = (bf16[128,2560]{1,0:T(8,128)(2,1)S(1)}, bf16[128,2560]{1,0:T(8,128)(2,1)}, u32[]{:S(2)}, u32[]{:S(2)}) collective-permute-start(bf16[128,2560]{1,0:T(8,128)(2,1)S(1)} %collective-permute-done.2.refs_2_.refs_10_), channel_id=1, source_target_pairs={{0,4},{1,5},{2,6},{3,7},{4,0},{5,1},{6,2},{7,3},{8,10},{9,11},{10,... | collective-permute-start | bytes 1966088 | tf_op jit(solution)/shard_map/ppermute | solution.py:577
  41.7 12.0 %collective-permute-start.27 = (bf16[128,1536]{1,0:T(8,128)(2,1)S(1)}, bf16[128,1536]{1,0:T(8,128)(2,1)S(1)}, u32[]{:S(2)}, u32[]{:S(2)}) collective-permute-start(bf16[128,1536]{1,0:T(8,128)(2,1)S(1)} %collective-permute-done.26.refs_6_), channel_id=1, source_target_pairs={{0,1},{1,0},{2,3},{3,2},{4,5},{5,4},{6,7},{7,6},{8,9},{9,8},{10,11... | collective-permute-start | bytes 1179656 | tf_op jit(solution)/shard_map/ppermute | solution.py:577
  42.2 16.4 %collective-permute-start.6 = (bf16[128,2560]{1,0:T(8,128)(2,1)S(1)}, bf16[128,2560]{1,0:T(8,128)(2,1)}, u32[]{:S(2)}, u32[]{:S(2)}) collective-permute-start(bf16[128,2560]{1,0:T(8,128)(2,1)S(1)} %collective-permute-done.2.refs_2_.refs_10_), channel_id=1, source_target_pairs={{0,8},{1,9},{2,10},{3,11},{4,12},{5,13},{6,14},{7,15},{8,0},{9,1},... | collective-permute-start | bytes 1966088 | tf_op jit(solution)/shard_map/ppermute | solution.py:577
  43.6 15.9 %collective-permute-start.3 = (bf16[128,2560]{1,0:T(8,128)(2,1)S(1)}, bf16[128,2560]{1,0:T(8,128)(2,1)S(1)}, u32[]{:S(2)}, u32[]{:S(2)}) collective-permute-start(bf16[128,2560]{1,0:T(8,128)(2,1)S(1)} %collective-permute-done.2.refs_2_.refs_10_), channel_id=1, source_target_pairs={{0,1},{1,0},{2,3},{3,2},{4,5},{5,4},{6,7},{7,6},{8,9},{9,8},{10,11... | collective-permute-start | bytes 1966088 | tf_op jit(solution)/shard_map/ppermute | solution.py:577
  50.7 15.9 %collective-permute-start.8 = (bf16[128,4096]{1,0:T(8,128)(2,1)S(1)}, bf16[128,4096]{1,0:T(8,128)(2,1)}, u32[]{:S(2)}, u32[]{:S(2)}) collective-permute-start(bf16[128,4096]{1,0:T(8,128)(2,1)S(1)} %copy-done.3), channel_id=1, source_target_pairs={{0,1},{1,0},{2,3},{3,2},{4,5},{5,4},{6,7},{7,6},{8,9},{9,8},{10,11... | collective-permute-start | bytes 3145736 | tf_op jit(solution)/shard_map/ppermute | solution.py:577
  53.7 24.9 %collective-permute-start.16 = (bf16[512,1024]{1,0:T(8,128)(2,1)S(1)}, bf16[512,1024]{1,0:T(8,128)(2,1)}, u32[]{:S(2)}, u32[]{:S(2)}) collective-permute-start(bf16[512,1024]{1,0:T(8,128)(2,1)S(1)} %copy-done.4), channel_id=1, source_target_pairs={{0,2},{1,3},{2,0},{3,1},{4,6},{5,7},{6,4},{7,5},{8,12},{9,13},{10,... | collective-permute-start | bytes 3145736 | tf_op jit(solution)/shard_map/ppermute | solution.py:577
  55.6 23.9 %collective-permute-start.15 = (bf16[512,1024]{1,0:T(8,128)(2,1)S(1)}, bf16[512,1024]{1,0:T(8,128)(2,1)}, u32[]{:S(2)}, u32[]{:S(2)}) collective-permute-start(bf16[512,1024]{1,0:T(8,128)(2,1)S(1)} %copy-done.4), channel_id=1, source_target_pairs={{0,1},{1,0},{2,3},{3,2},{4,5},{5,4},{6,7},{7,6},{8,9},{9,8},{10,11... | collective-permute-start | bytes 3145736 | tf_op jit(solution)/shard_map/ppermute | solution.py:577
  58.6 9.2 %collective-permute-start.5 = (bf16[128,2560]{1,0:T(8,128)(2,1)}, bf16[128,2560]{1,0:T(8,128)(2,1)}, u32[]{:S(2)}, u32[]{:S(2)}) collective-permute-start(bf16[128,2560]{1,0:T(8,128)(2,1)} %collective-permute-done.4.refs_4_.refs_12_), channel_id=1, source_target_pairs={{0,1},{1,0},{2,3},{3,2},{4,5},{5,4},{6,7},{7,6},{8,9},{9,8},{10,11... | collective-permute-start | bytes 1966088 | tf_op jit(solution)/shard_map/ppermute | solution.py:577
  59.5 9.7 %collective-permute-start.7 = (bf16[128,2560]{1,0:T(8,128)(2,1)}, bf16[128,2560]{1,0:T(8,128)(2,1)}, u32[]{:S(2)}, u32[]{:S(2)}) collective-permute-start(bf16[128,2560]{1,0:T(8,128)(2,1)} %collective-permute-done.6.refs_6_.refs_14_), channel_id=1, source_target_pairs={{0,1},{1,0},{2,3},{3,2},{4,5},{5,4},{6,7},{7,6},{8,9},{9,8},{10,11... | collective-permute-start | bytes 1966088 | tf_op jit(solution)/shard_map/ppermute | solution.py:577
  66.6 39.0 %collective-permute-start.11 = (bf16[128,4096]{1,0:T(8,128)(2,1)}, bf16[128,4096]{1,0:T(8,128)(2,1)S(1)}, u32[]{:S(2)}, u32[]{:S(2)}) collective-permute-start(bf16[128,4096]{1,0:T(8,128)(2,1)} %copy-done.5), channel_id=1, source_target_pairs={{0,4},{1,5},{2,6},{3,7},{4,0},{5,1},{6,2},{7,3},{8,10},{9,11},{10,... | collective-permute-start | bytes 3145736 | tf_op jit(solution)/shard_map/ppermute | solution.py:577
  67.9 39.2 %collective-permute-start.13 = (bf16[128,4096]{1,0:T(8,128)(2,1)}, bf16[128,4096]{1,0:T(8,128)(2,1)S(1)}, u32[]{:S(2)}, u32[]{:S(2)}) collective-permute-start(bf16[128,4096]{1,0:T(8,128)(2,1)} %copy-done.5), channel_id=1, source_target_pairs={{0,8},{1,9},{2,10},{3,11},{4,12},{5,13},{6,14},{7,15},{8,0},{9,1},... | collective-permute-start | bytes 3145736 | tf_op jit(solution)/shard_map/ppermute | solution.py:577
  69.2 38.0 %collective-permute-start.10 = (bf16[128,4096]{1,0:T(8,128)(2,1)}, bf16[128,4096]{1,0:T(8,128)(2,1)S(1)}, u32[]{:S(2)}, u32[]{:S(2)}) collective-permute-start(bf16[128,4096]{1,0:T(8,128)(2,1)} %copy-done.5), channel_id=1, source_target_pairs={{0,1},{1,0},{2,3},{3,2},{4,5},{5,4},{6,7},{7,6},{8,9},{9,8},{10,11... | collective-permute-start | bytes 3145736 | tf_op jit(solution)/shard_map/ppermute | solution.py:577
  78.6 35.6 %collective-permute-start.18 = (bf16[512,1024]{1,0:T(8,128)(2,1)}, bf16[512,1024]{1,0:T(8,128)(2,1)}, u32[]{:S(2)}, u32[]{:S(2)}) collective-permute-start(bf16[512,1024]{1,0:T(8,128)(2,1)} %collective-permute-done.16.refs_18_), channel_id=1, source_target_pairs={{0,4},{1,5},{2,6},{3,7},{4,0},{5,1},{6,2},{7,3},{8,10},{9,11},{10,... | collective-permute-start | bytes 3145736 | tf_op jit(solution)/shard_map/ppermute | solution.py:577
  79.5 35.5 %collective-permute-start.20 = (bf16[512,1024]{1,0:T(8,128)(2,1)}, bf16[512,1024]{1,0:T(8,128)(2,1)S(1)}, u32[]{:S(2)}, u32[]{:S(2)}) collective-permute-start(bf16[512,1024]{1,0:T(8,128)(2,1)} %collective-permute-done.16.refs_18_), channel_id=1, source_target_pairs={{0,8},{1,9},{2,10},{3,11},{4,12},{5,13},{6,14},{7,15},{8,0},{9,1},... | collective-permute-start | bytes 3145736 | tf_op jit(solution)/shard_map/ppermute | solution.py:577
  105.7 35.0 %collective-permute-start.17 = (bf16[512,1024]{1,0:T(8,128)(2,1)}, bf16[512,1024]{1,0:T(8,128)(2,1)S(1)}, u32[]{:S(2)}, u32[]{:S(2)}) collective-permute-start(bf16[512,1024]{1,0:T(8,128)(2,1)} %collective-permute-done.16.refs_18_), channel_id=1, source_target_pairs={{0,1},{1,0},{2,3},{3,2},{4,5},{5,4},{6,7},{7,6},{8,9},{9,8},{10,11... | collective-permute-start | bytes 3145736 | tf_op jit(solution)/shard_map/ppermute | solution.py:577
  107.1 33.6 %collective-permute-start.12 = (bf16[128,4096]{1,0:T(8,128)(2,1)S(1)}, bf16[128,4096]{1,0:T(8,128)(2,1)}, u32[]{:S(2)}, u32[]{:S(2)}) collective-permute-start(bf16[128,4096]{1,0:T(8,128)(2,1)S(1)} %collective-permute-done.11.refs_12_), channel_id=1, source_target_pairs={{0,1},{1,0},{2,3},{3,2},{4,5},{5,4},{6,7},{7,6},{8,9},{9,8},{10,11... | collective-permute-start | bytes 3145736 | tf_op jit(solution)/shard_map/ppermute | solution.py:577
  107.2 33.5 %collective-permute-start.14 = (bf16[128,4096]{1,0:T(8,128)(2,1)S(1)}, bf16[128,4096]{1,0:T(8,128)(2,1)}, u32[]{:S(2)}, u32[]{:S(2)}) collective-permute-start(bf16[128,4096]{1,0:T(8,128)(2,1)S(1)} %collective-permute-done.13.refs_14_), channel_id=1, source_target_pairs={{0,1},{1,0},{2,3},{3,2},{4,5},{5,4},{6,7},{7,6},{8,9},{9,8},{10,11... | collective-permute-start | bytes 3145736 | tf_op jit(solution)/shard_map/ppermute | solution.py:577
  114.2 26.5 %collective-permute-start.19 = (bf16[512,1024]{1,0:T(8,128)(2,1)}, bf16[512,1024]{1,0:T(8,128)(2,1)}, u32[]{:S(2)}, u32[]{:S(2)}) collective-permute-start(bf16[512,1024]{1,0:T(8,128)(2,1)} %collective-permute-done.18.refs_20_), channel_id=1, source_target_pairs={{0,1},{1,0},{2,3},{3,2},{4,5},{5,4},{6,7},{7,6},{8,9},{9,8},{10,11... | collective-permute-start | bytes 3145736 | tf_op jit(solution)/shard_map/ppermute | solution.py:577
  115.0 25.7 %collective-permute-start.21 = (bf16[512,1024]{1,0:T(8,128)(2,1)S(1)}, bf16[512,1024]{1,0:T(8,128)(2,1)}, u32[]{:S(2)}, u32[]{:S(2)}) collective-permute-start(bf16[512,1024]{1,0:T(8,128)(2,1)S(1)} %collective-permute-done.20.refs_22_), channel_id=1, source_target_pairs={{0,1},{1,0},{2,3},{3,2},{4,5},{5,4},{6,7},{7,6},{8,9},{9,8},{10,11... | collective-permute-start | bytes 3145736 | tf_op jit(solution)/shard_map/ppermute | solution.py:577
  270.0 2.8 collective-permute-start.29
  272.8 2.8 collective-permute-start.30
  278.4 3.7 %collective-permute-start.32 = (f32[8,1024]{1,0:T(8,128)S(1)}, f32[8,1024]{1,0:T(8,128)S(1)}, u32[]{:S(2)}, u32[]{:S(2)}) collective-permute-start(f32[8,1024]{1,0:T(8,128)S(1)} %add.39), channel_id=1, source_target_pairs={{0,16},{1,17},{2,18},{3,19},{4,20},{5,21},{6,22},{7,23},{8,24},{9,... | collective-permute-start | bytes 98312 | tf_op jit(solution)/shard_map/ppermute | solution.py:577
  282.0 22.6 %collective-permute-start.33 = (f32[8,1024]{1,0:T(8,128)S(1)}, f32[8,1024]{1,0:T(8,128)S(1)}, u32[]{:S(2)}, u32[]{:S(2)}) collective-permute-start(f32[8,1024]{1,0:T(8,128)S(1)} %add.40), channel_id=1, source_target_pairs={{0,1},{1,0},{2,3},{3,2},{4,5},{5,4},{6,7},{7,6},{8,9},{9,8},{10,11... | collective-permute-start | bytes 98312 | tf_op jit(solution)/shard_map/ppermute | solution.py:577
  (23 other events, 532.7 us)

commit v3 on v2

v3 whole, which is shorter than its diff:
```python
import functools

import jax
import jax.numpy as jnp
from jax import lax
from jax.experimental import pallas as pl
from jax.experimental.pallas import tpu as pltpu
from jax.sharding import PartitionSpec as P

BF = jnp.bfloat16
F32 = jnp.float32
HD = 64
PAIR = 2 * HD
PAD = 16
SCALE = 8.0
EPS = 1e-05
NEG = -1e30
BLOCK = 256
FF_STEP = 1024
ROWS = 512
VMEM_LIMIT = 58 * 2**20
GELU_C = 0.7978845608028654
GELU_A = 0.044715
ANY = pl.BlockSpec(memory_space=pl.ANY)
SMEM = pl.BlockSpec(memory_space=pltpu.SMEM)
CHEAP = pl.CostEstimate(flops=1000, bytes_accessed=1000, transcendentals=0)


def dot(a, b):
    return lax.dot_general(a, b, (((1,), (0,)), ((), ())), preferred_element_type=F32)


def dot_nt(a, b):
    return lax.dot_general(a, b, (((1,), (1,)), ((), ())), preferred_element_type=F32)


def dot_tn(a, b):
    return lax.dot_general(a, b, (((0,), (0,)), ((), ())), preferred_element_type=F32)


def lane(shape):
    return lax.broadcasted_iota(jnp.int32, shape, 1)


def row(shape):
    return lax.broadcasted_iota(jnp.int32, shape, 0)


def split3(x):
    a = x.astype(BF)
    r = x - a.astype(F32)
    b = r.astype(BF)
    c = (r - b.astype(F32)).astype(BF)
    return a, b, c


def whole(shape):
    return pl.BlockSpec(shape, lambda *_: (0,) * len(shape))


def params(**kw):
    return pltpu.CompilerParams(vmem_limit_bytes=VMEM_LIMIT, **kw)


def norm_stats(x):
    mean = jnp.mean(x, axis=-1, keepdims=True)
    center = x - mean
    inv = lax.rsqrt(jnp.mean(center * center, axis=-1, keepdims=True) + EPS)
    return center * inv, inv


def norm_back(xhat, inv, g):
    return inv * (
        g
        - jnp.mean(g, axis=-1, keepdims=True)
        - xhat * jnp.mean(g * xhat, axis=-1, keepdims=True)
    )


def pad_rows(parts, width):
    have = sum(p.shape[0] for p in parts)
    return jnp.concatenate(parts + [jnp.zeros((PAD - have, width), F32)], axis=0).astype(BF)


def norm_one_kernel(
    x_ref, gain_ref, shift_ref, dq_ref, dv_ref, uq_ref, uv_ref,
    n_ref, narrow_ref, down_ref, upq_ref, upv_ref,
):
    width = x_ref.shape[1]
    rank = dq_ref.shape[0]

    @pl.when(pl.program_id(0) == 0)
    def _():
        blank = jnp.zeros((rank, width), F32)
        down_ref[...] = pad_rows([dq_ref[...], dv_ref[...]], width)
        upq_ref[...] = pad_rows([uq_ref[...]], width)
        upv_ref[...] = pad_rows([blank, uv_ref[...]], width)

    xhat, _ = norm_stats(x_ref[...].astype(F32))
    low = (xhat * gain_ref[...] + shift_ref[...]).astype(BF)
    n_ref[...] = low
    narrow_ref[...] = dot_nt(down_ref[...], low).astype(BF)


def norm_one(x, gain, shift, dq, dv, uq, uv):
    length, width = x.shape
    small = whole((1, width))
    adapter = whole(dq.shape)
    padded = whole((PAD, width))
    return pl.pallas_call(
        norm_one_kernel,
        grid=(length // BLOCK,),
        in_specs=[pl.BlockSpec((BLOCK, width), lambda i: (i, 0)), small, small] + [adapter] * 4,
        out_specs=[
            pl.BlockSpec((BLOCK, width), lambda i: (i, 0)),
            pl.BlockSpec((PAD, BLOCK), lambda i: (0, i)),
            padded, padded, padded,
        ],
        out_shape=[
            jax.ShapeDtypeStruct((length, width), BF),
            jax.ShapeDtypeStruct((PAD, length), BF),
        ]
        + [jax.ShapeDtypeStruct((PAD, width), BF)] * 3,
        compiler_params=params(),
        name="norm_one",
    )(x, gain, shift, dq, dv, uq, uv)


def repack_kernel(quads, half, qkv_ref, proj_ref, a_ref, b_ref):
    width = proj_ref.shape[1]
    for q in range(quads):
        ref, place = (a_ref, q) if q < half else (b_ref, q - half)
        for p in range(3):
            at = (3 * place + p) * QUAD
            ref[:, at : at + QUAD] = qkv_ref[:, p * width + q * QUAD : p * width + (q + 1) * QUAD]
    at = 3 * (quads - half) * QUAD
    b_ref[:, at : at + width] = proj_ref[...]


def repack(w_qkv, w_proj, half):
    rows, width = w_proj.shape
    quads = width // QUAD
    return pl.pallas_call(
        functools.partial(repack_kernel, quads, half),
        out_shape=[
            jax.ShapeDtypeStruct((rows, 3 * half * QUAD), BF),
            jax.ShapeDtypeStruct((rows, 3 * (quads - half) * QUAD + width), BF),
        ],
        compiler_params=params(),
        name="repack",
    )(w_qkv, w_proj)


QUAD = 2 * PAIR


def causal_below(x):
    size, wide = x.shape
    near = jnp.where(row((size, size)) <= lane((size, size)), x[:, :size], NEG)
    return near if wide == size else jnp.concatenate([near, x[:, size:]], axis=1)


def attend(length, pairs, o_ref, qx_ref, kx, vt, qt, ot):
    size = pairs[0][0].shape[0]
    ln = lane((size, PAIR))
    first = ln < HD
    bias = jnp.where(row((size, PAIR)) < length, 0.0, NEG).astype(BF)
    zero = jnp.zeros((size, PAIR), BF)
    ones = jnp.ones((16, size), BF)
    extra = jnp.where(row((HD, size)) == 0, 1.0, 0.0).astype(BF)

    def prepare(p):
        q, k, v = pairs[p]
        kx[2 * p] = jnp.where(first, k, jnp.where(ln == HD, bias, zero))
        kx[2 * p + 1] = jnp.where(first, jnp.where(ln == 0, bias, zero), k)
        v_t = v.T
        q_t = q.T
        for h in range(2):
            mine = slice(h * HD, (h + 1) * HD)
            vt[2 * p + h, :HD, :] = v_t[mine]
            vt[2 * p + h, HD:, :] = ones
            parts = [q_t[mine], extra] if h == 0 else [extra, q_t[mine]]
            qt[2 * p + h] = jnp.concatenate(parts, axis=0)

    def scores(t):
        return [
            (b, causal_below(dot(kx[t, b : b + BLOCK, :], qt[t, :, b:])))
            for b in range(0, size, BLOCK)
        ]

    def finish(t, parts):
        top = None
        for b, s in parts:
            high = jnp.max(s, axis=0, keepdims=True)
            if b == 0:
                top = high
            else:
                top = jnp.concatenate([top[:, :b], jnp.maximum(top[:, b:], high)], axis=1)
        acc = None
        for b, s in parts:
            p = jnp.exp(s - top[:, b:]).astype(BF)
            a = dot(vt[t, :, b : b + BLOCK], p)
            acc = a if b == 0 else jnp.concatenate([acc[:, :b], acc[:, b:] + a], axis=1)
        total = acc[HD : HD + 1]
        ot[t * HD : (t + 1) * HD, :] = acc[:HD] * (1.0 / total)
        a, b, c = split3(-(top + jnp.log(total)))
        r = row((HD, size))
        more = jnp.where(
            r == 0,
            1.0,
            jnp.where(
                r == 1,
                a.astype(F32),
                jnp.where(r == 2, b.astype(F32), jnp.where(r == 3, c.astype(F32), 0.0)),
            ),
        ).astype(BF)
        at = t * PAIR
        h = t % 2
        qx_ref[at + h * HD : at + (h + 1) * HD, :] = qt[t, h * HD : (h + 1) * HD, :]
        qx_ref[at + (1 - h) * HD : at + (2 - h) * HD, :] = more

    count = 2 * len(pairs)
    prepare(0)
    later = scores(0)
    for t in range(count):
        now = later
        if t + 1 < count:
            if t % 2:
                prepare((t + 1) // 2)
            later = scores(t + 1)
        finish(t, now)
    o_ref[...] = ot[...].T.astype(BF)


def qkv_copies(index_ref, shards, wbuf, sem, quad):
    rows = shards[0].shape[0]
    wide = wbuf.shape[1]
    copies = []
    for i, ref in enumerate(shards):
        at = pl.multiple_of(index_ref[i] * rows, rows)
        src = ref.at[:, quad * wide : (quad + 1) * wide]
        copies.append(pltpu.make_async_copy(src, wbuf.at[pl.ds(at, rows), :], sem))
    return copies


def forward_kernel(count, kept, quads, len_ref, index_ref, *refs):
    shards, refs = refs[:count], refs[count + kept :]
    (n_ref, narrow_ref, upq_ref, upv_ref, o_ref, qx_ref, q_ref, k_ref, v_ref,
     wbuf, kx, vt, qt, ot, sem) = refs
    step = pl.program_id(0)

    def copies(i):
        return qkv_copies(index_ref, shards, wbuf.at[i], sem.at[i], quads[i])

    @pl.when(step == 0)
    def _():
        for i in range(len(quads)):
            for c in copies(i):
                c.start()

    for i in range(len(quads)):

        @pl.when(step == i)
        def _(i=i):
            for c in copies(i):
                c.wait()

    n = n_ref[...]
    narrow = narrow_ref[...]
    w = wbuf.at[step]
    q = dot(n, w[:, :QUAD]) + SCALE * dot_tn(narrow, upq_ref[...])
    k = dot(n, w[:, QUAD : 2 * QUAD])
    v = dot(n, w[:, 2 * QUAD :]) + SCALE * dot_tn(narrow, upv_ref[...])
    q_ref[...] = (q.astype(BF).astype(F32) * (1.0 / HD**0.5)).astype(BF)
    k_ref[...] = k.astype(BF)
    v_ref[...] = v.astype(BF)
    cols = [slice(p * PAIR, (p + 1) * PAIR) for p in range(QUAD // PAIR)]
    pairs = [(q_ref[:, c], k_ref[:, c], v_ref[:, c]) for c in cols]
    attend(len_ref[0], pairs, o_ref, qx_ref, kx, vt, qt, ot)


def attention_forward(lengths, index, shards, n, narrow, upq, upv, quads, here, kept):
    length, width = n.shape
    block = pl.BlockSpec((length, QUAD), lambda s: (0, here + s))
    up = pl.BlockSpec((PAD, QUAD), lambda s: (0, here + s))
    first = 2 + len(shards)
    heads = QUAD // HD
    return pl.pallas_call(
        functools.partial(forward_kernel, len(shards), len(kept), quads),
        grid=(len(quads),),
        in_specs=[SMEM, SMEM]
        + [ANY] * (len(shards) + len(kept))
        + [whole((length, width)), whole((PAD, length)), up, up],
        out_specs=[block, pl.BlockSpec((2 * QUAD, length), lambda s: (here + s, 0))] + [block] * 3,
        out_shape=[
            jax.ShapeDtypeStruct((length, width), BF),
            jax.ShapeDtypeStruct((2 * width, length), BF),
        ]
        + [jax.ShapeDtypeStruct((length, width), BF)] * 3,
        input_output_aliases={first + i: i for i in range(len(kept))},
        scratch_shapes=[
            pltpu.VMEM((len(quads), width, 3 * QUAD), BF),
            pltpu.VMEM((heads, length, PAIR), BF),
            pltpu.VMEM((heads, HD + 16, length), BF),
            pltpu.VMEM((heads, PAIR, length), BF),
            pltpu.VMEM((QUAD, length), F32),
            pltpu.SemaphoreType.DMA((len(quads),)),
        ],
        compiler_params=params(),
        cost_estimate=CHEAP,
        name="attention_forward",
    )(lengths, index, *shards, *kept, n, narrow, upq, upv)


def rows_copies(index_ref, shards, col, wide, wbuf, sem):
    rows = shards[0].shape[0]
    copies = []
    for i, ref in enumerate(shards):
        at = pl.multiple_of(index_ref[i] * rows, rows)
        src = ref.at[:, pl.ds(col, wide)]
        copies.append(pltpu.make_async_copy(src, wbuf.at[pl.ds(at, rows), :], sem))
    return copies


def out_slice(index_ref, outs, step):
    rows = outs[0].shape[0]
    if rows >= FF_STEP:
        shard, part = divmod(step, rows // FF_STEP)
        begin = index_ref[shard] * rows + part * FF_STEP
        return pl.multiple_of(begin, FF_STEP), [(outs[shard], part * FF_STEP, 0, FF_STEP)]
    each = FF_STEP // rows
    begin = index_ref[step * each] * rows // FF_STEP * FF_STEP
    begin = pl.multiple_of(begin, FF_STEP)
    pieces = [
        (outs[i], 0, pl.multiple_of(index_ref[i] * rows - begin, rows), rows)
        for i in range(step * each, (step + 1) * each)
    ]
    return begin, pieces


def gelu_both(v):
    square = v * v
    t = jnp.tanh(v * (GELU_C + (GELU_C * GELU_A) * square))
    half = 0.5 * t + 0.5
    act = v * half
    slope = half + act * (1.0 - half) * (2.0 * GELU_C + (6.0 * GELU_C * GELU_A) * square)
    return act, slope


def blocks_of(size, rows):
    return [pl.ds(i * rows, rows) for i in range(size // rows)]


def rise_kernel(count, col, index_ref, *refs):
    projs, refs = refs[:count], refs[count:]
    fcs, refs = refs[:count], refs[count:]
    (o_ref, x_ref, gain_ref, shift_ref, pre_ref, hidden_ref,
     wproj, fbuf, obuf, xbuf, hidden, n2, psem, fsem, osem, hsem) = refs
    step = pl.program_id(0)
    steps = pl.num_programs(0)
    size, width = xbuf.shape
    slot = lax.rem(step, 2)
    places = blocks_of(size, BLOCK)

    def fc_copies(s, slot):
        col = pl.multiple_of(s * FF_STEP, FF_STEP)
        return rows_copies(index_ref, fcs, col, FF_STEP, fbuf.at[slot], fsem.at[slot])

    def row_copies(i):
        at = places[i]
        return [
            pltpu.make_async_copy(o_ref.at[at, :], obuf.at[at, :], osem.at[i]),
            pltpu.make_async_copy(x_ref.at[at, :], xbuf.at[at, :], osem.at[i]),
        ]

    def hidden_copy(i):
        at = places[i]
        return pltpu.make_async_copy(hidden.at[at, :], hidden_ref.at[at, :], hsem)

    @pl.when(step == 0)
    def _():
        first = rows_copies(index_ref, projs, col, width, wproj, psem)
        for c in first:
            c.start()
        for i in range(len(places)):
            for c in row_copies(i):
                c.start()
        for c in fc_copies(0, 0):
            c.start()
        for c in first:
            c.wait()
        for i, at in enumerate(places):
            for c in row_copies(i):
                c.wait()
            hidden[at, :] = xbuf[at, :].astype(F32) + dot(obuf[at, :], wproj[...])
            hidden_copy(i).start()
        for at in places:
            xhat, _ = norm_stats(hidden[at, :])
            n2[at, :] = (xhat * gain_ref[...] + shift_ref[...]).astype(BF)

    @pl.when(step + 1 < steps)
    def _():
        for c in fc_copies(step + 1, 1 - slot):
            c.start()

    for c in fc_copies(step, slot):
        c.wait()
    for at in blocks_of(size, ROWS):
        pre_ref[at, :] = dot(n2[at, :], fbuf[slot])

    @pl.when(step == steps - 1)
    def _():
        for i in range(len(places)):
            hidden_copy(i).wait()


def rise(index, projs, col, fcs, o, x, gain, shift):
    size, width = x.shape
    units = fcs[0].shape[1]
    small = whole((1, width))
    return pl.pallas_call(
        functools.partial(rise_kernel, len(projs), col),
        grid=(units // FF_STEP,),
        in_specs=[SMEM] + [ANY] * (2 * len(projs) + 2) + [small, small],
        out_specs=[pl.BlockSpec((size, FF_STEP), lambda s: (0, s)), ANY],
        out_shape=[
            jax.ShapeDtypeStruct((size, units), F32),
            jax.ShapeDtypeStruct((size, width), F32),
        ],
        scratch_shapes=[
            pltpu.VMEM((width, width), BF),
            pltpu.VMEM((2, width, FF_STEP), BF),
            pltpu.VMEM((size, width), BF),
            pltpu.VMEM((size, width), BF),
            pltpu.VMEM((size, width), F32),
            pltpu.VMEM((size, width), BF),
            pltpu.SemaphoreType.DMA,
            pltpu.SemaphoreType.DMA((2,)),
            pltpu.SemaphoreType.DMA((size // BLOCK,)),
            pltpu.SemaphoreType.DMA,
        ],
        compiler_params=params(),
        cost_estimate=CHEAP,
        name="rise",
    )(index, *projs, *fcs, o, x, gain, shift)


def fall_kernel(count, col, steps, len_ref, index_ref, *refs):
    projs, refs = refs[:count], refs[count:]
    fcs, refs = refs[:count], refs[count:]
    outs, refs = refs[:count], refs[count:]
    (pre_ref, hidden_ref, cot_ref, gain_ref, block_ref, gh_ref, ga_ref,
     wproj, fbuf, obuf, pbuf, hidden, cbuf, low, acc, back, block, gatt, sem, lsem, wsem) = refs
    step = pl.program_id(0)
    size, width = low.shape
    slot = lax.rem(step, 2)

    def copies(s):
        begin, pieces = out_slice(index_ref, outs, s)
        slot = s % 2
        found = []
        for ref, at, to, rows in pieces:
            found.append(
                pltpu.make_async_copy(
                    ref.at[at : at + rows, :], obuf.at[slot, pl.ds(to, rows), :], sem.at[slot]
                )
            )
        src = pre_ref.at[:, pl.ds(begin, FF_STEP)]
        found.append(pltpu.make_async_copy(src, pbuf.at[slot], sem.at[slot]))
        return found + rows_copies(index_ref, fcs, begin, FF_STEP, fbuf.at[slot], sem.at[slot])

    late = [pltpu.make_async_copy(hidden_ref, hidden, lsem.at[1])]
    late += rows_copies(index_ref, projs, col, width, wproj, lsem.at[1])
    first = pltpu.make_async_copy(cot_ref, cbuf, lsem.at[0])

    @pl.when(step == 0)
    def _():
        first.start()
        for c in copies(0):
            c.start()
        for c in copies(1):
            c.start()
        for c in late:
            c.start()
        first.wait()
        for i, at in enumerate(blocks_of(size, BLOCK)):
            keep = row((BLOCK, 1)) + i * BLOCK < len_ref[0]
            low[at, :] = jnp.where(keep, cbuf[at, :].astype(F32), 0.0).astype(BF)

    for s in range(2, steps):

        @pl.when(step + 1 == s)
        def _(s=s):
            for c in copies(s):
                c.start()

    for even in range(2):

        @pl.when(slot == even)
        def _(even=even):
            for c in copies(even):
                c.wait()

    def body(begin):
        for at in blocks_of(size, ROWS):
            act, slope = gelu_both(pbuf[slot, at, :])
            mlp = dot(act.astype(BF), obuf[slot])
            grad = (dot_nt(low[at, :], obuf[slot]) * slope).astype(BF)
            u = dot_nt(grad, fbuf[slot])
            if begin:
                acc[at, :] = mlp
                back[at, :] = u
            else:
                acc[at, :] += mlp
                back[at, :] += u

    @pl.when(step == 0)
    def _():
        body(True)

    @pl.when(step > 0)
    def _():
        body(False)

    @pl.when(step == steps - 1)
    def _():
        for c in late:
            c.wait()
        sent = []
        for i, at in enumerate(blocks_of(size, BLOCK)):
            h = hidden[at, :]
            keep = row((BLOCK, 1)) + i * BLOCK < len_ref[0]
            block[at, :] = jnp.where(keep, h + acc[at, :], 0.0).astype(BF)
            xhat, inv = norm_stats(h)
            gh = low[at, :].astype(F32) + norm_back(xhat, inv, gain_ref[...] * back[at, :])
            hidden[at, :] = gh
            gatt[at, :] = dot_nt(gh.astype(BF), wproj[...]).astype(BF)
            here = [
                pltpu.make_async_copy(block.at[at, :], block_ref.at[at, :], wsem),
                pltpu.make_async_copy(hidden.at[at, :], gh_ref.at[at, :], wsem),
                pltpu.make_async_copy(gatt.at[at, :], ga_ref.at[at, :], wsem),
            ]
            for c in here:
                c.start()
            sent += here
        for c in sent:
            c.wait()


def fall(lengths, index, projs, col, fcs, outs, pre, hidden, cot, gain):
    size, width = cot.shape
    units = pre.shape[1]
    steps = units // FF_STEP
    return pl.pallas_call(
        functools.partial(fall_kernel, len(projs), col, steps),
        grid=(steps,),
        in_specs=[SMEM, SMEM] + [ANY] * (3 * len(projs) + 3) + [whole((1, width))],
        out_specs=[ANY] * 3,
        out_shape=[
            jax.ShapeDtypeStruct((size, width), BF),
            jax.ShapeDtypeStruct((size, width), F32),
            jax.ShapeDtypeStruct((size, width), BF),
        ],
        scratch_shapes=[
            pltpu.VMEM((width, width), BF),
            pltpu.VMEM((2, width, FF_STEP), BF),
            pltpu.VMEM((2, FF_STEP, width), BF),
            pltpu.VMEM((2, size, FF_STEP), F32),
            pltpu.VMEM((size, width), F32),
            pltpu.VMEM((size, width), BF),
            pltpu.VMEM((size, width), BF),
            pltpu.VMEM((size, width), F32),
            pltpu.VMEM((size, width), F32),
            pltpu.VMEM((size, width), BF),
            pltpu.VMEM((size, width), BF),
            pltpu.SemaphoreType.DMA((2,)),
            pltpu.SemaphoreType.DMA((2,)),
            pltpu.SemaphoreType.DMA,
        ],
        compiler_params=params(),
        cost_estimate=CHEAP,
        name="fall",
    )(lengths, index, *projs, *fcs, *outs, pre, hidden, cot, gain)


def backward_kernel(
    len_ref, qx_ref, q_ref, k_ref, v_ref, o_ref, g_ref, upq_ref, upv_ref, narrow_ref, n_ref,
    dq_ref, dk_ref, dv_ref, joint_ref, sums_ref, kx, vx, gx, kt, dqt, total,
):
    size = k_ref.shape[0]
    step = pl.program_id(0)
    ln = lane((size, PAIR))
    first = ln < HD
    bias = jnp.where(row((size, PAIR)) < len_ref[0], 0.0, NEG).astype(BF)
    kp = k_ref[...]
    vp = v_ref[...]
    g = g_ref[...]
    qp = q_ref[...]
    zero = jnp.zeros((size, PAIR), BF)
    one = jnp.ones((size, PAIR), BF)
    prod = g.astype(F32) * o_ref[...].astype(F32)
    for h in range(2):
        other = HD * (1 - h)
        mine = first if h == 0 else ~first
        extra = (ln > other) & (ln <= other + 3)
        kx[h] = jnp.where(mine, kp, jnp.where(ln == other, bias, jnp.where(extra, one, zero)))
        vx[h] = jnp.where(mine, vp, jnp.where(extra, one, zero))
        dots = jnp.sum(jnp.where(mine, prod, 0.0), axis=-1, keepdims=True)
        a, b, c = split3(jnp.broadcast_to(-dots, (size, PAIR)))
        gx[h] = jnp.where(
            mine,
            g,
            jnp.where(
                ln == other + 1,
                a,
                jnp.where(ln == other + 2, b, jnp.where(ln == other + 3, c, zero)),
            ),
        )
    kt[...] = kp.T

    def products(b, h):
        st = dot(kx[h, b : b + BLOCK, :], qx_ref[h * PAIR : (h + 1) * PAIR, b:])
        return st, dot_nt(vx[h, b : b + BLOCK, :], gx[h, b:, :])

    held = {}

    def finish(b, h, st, dp):
        p = jnp.exp(causal_below(st))
        ds = (p * dp).astype(BF)
        mine = slice(h * HD, (h + 1) * HD)
        c = dot(kt[mine, b : b + BLOCK], ds)
        if b == 0:
            dqt[mine, :] = c
        else:
            dqt[mine, b:] += c
        held[h] = (dot(p.astype(BF), g[b:]), dot(ds, qp[b:]))
        if h == 1:
            f = lane((BLOCK, PAIR)) < HD
            dv_ref[b : b + BLOCK, :] = jnp.where(f, held[0][0], held[1][0]).astype(BF)
            dk_ref[b : b + BLOCK, :] = jnp.where(f, held[0][1], held[1][1]).astype(BF)

    tasks = [(b, h) for b in range(0, size, BLOCK) for h in range(2)]
    later = products(*tasks[0])
    for j, t in enumerate(tasks):
        now = later
        if j + 1 < len(tasks):
            later = products(*tasks[j + 1])
        finish(*t, *now)
    dq = (dqt[...] * (1.0 / HD**0.5)).T.astype(BF)
    dq_ref[...] = dq
    dv = dv_ref[...]
    narrow = narrow_ref[...]
    part = dot_nt(upq_ref[...], dq) + dot_nt(upv_ref[...], dv)
    gq = SCALE * dot(narrow, dq)[:8]
    gv = SCALE * dot(narrow, dv)[:8]
    cols = pl.ds(pl.multiple_of(step * PAIR, PAIR), PAIR)
    sums_ref[8:16, cols] = jnp.where(row((8, PAIR)) < 4, gq, gv)

    @pl.when(step == 0)
    def _():
        total[...] = part

    @pl.when(step > 0)
    def _():
        total[...] += part

    @pl.when(step == pl.num_programs(0) - 1)
    def _():
        joint = (SCALE * total[...]).astype(BF)
        joint_ref[...] = joint
        sums_ref[0:8, :] = dot(joint, n_ref[...])[:8]


def attention_backward(lengths, qx, q, k, v, o, ga, upq, upv, narrow, n):
    size, width = k.shape
    pair = pl.BlockSpec((size, PAIR), lambda p: (0, p))
    up = pl.BlockSpec((PAD, PAIR), lambda p: (0, p))
    return pl.pallas_call(
        backward_kernel,
        grid=(width // PAIR,),
        in_specs=[SMEM, pl.BlockSpec((2 * PAIR, size), lambda p: (p, 0))]
        + [pair] * 5
        + [up, up, whole((PAD, size)), whole((size, width))],
        out_specs=[pair] * 3 + [whole((PAD, size)), whole((16, width))],
        out_shape=[jax.ShapeDtypeStruct((size, width), BF)] * 3
        + [jax.ShapeDtypeStruct((PAD, size), BF), jax.ShapeDtypeStruct((16, width), F32)],
        scratch_shapes=[pltpu.VMEM((2, size, PAIR), BF)] * 3
        + [
            pltpu.VMEM((PAIR, size), BF),
            pltpu.VMEM((PAIR, size), F32),
            pltpu.VMEM((PAD, size), F32),
        ],
        compiler_params=params(),
        cost_estimate=CHEAP,
        name="attention_backward",
    )(lengths, qx, q, k, v, o, ga, upq, upv, narrow, n)


def token_kernel(counts, quads, index_ref, *refs):
    shards = []
    for count in counts:
        shards.append(refs[:count])
        refs = refs[count:]
    (dq_ref, dk_ref, dv_ref, joint_ref, down_ref, gh_ref, x_ref, gain_ref, o_ref, wbuf, sem) = refs
    step = pl.program_id(0)
    pieces = [(j, q) for j in range(len(counts)) for q in range(quads[j])]

    def copies(s):
        j, q = pieces[s]
        return qkv_copies(index_ref, shards[j], wbuf.at[s], sem.at[s], q)

    @pl.when(step == 0)
    def _():
        for s in range(len(pieces)):
            for c in copies(s):
                c.start()

    total = dot_tn(joint_ref[...], down_ref[...])
    for s in range(len(pieces)):

        @pl.when(step == 0)
        def _(s=s):
            for c in copies(s):
                c.wait()

        cols = slice(s * QUAD, (s + 1) * QUAD)
        g = jnp.concatenate([ref[:, cols] for ref in (dq_ref, dk_ref, dv_ref)], axis=1)
        total = total + dot_nt(g, wbuf[s])
    xhat, inv = norm_stats(x_ref[...].astype(F32))
    o_ref[...] = (gh_ref[...] + norm_back(xhat, inv, gain_ref[...] * total)).astype(BF)


def token_gradient(index, shards, quads, dq, dk, dv, joint, down, gh, x, gain):
    size, width = x.shape
    flat = [s for part in shards for s in part]
    block = pl.BlockSpec((BLOCK, width), lambda i: (i, 0))
    return pl.pallas_call(
        functools.partial(token_kernel, [len(p) for p in shards], quads),
        grid=(size // BLOCK,),
        in_specs=[SMEM]
        + [ANY] * len(flat)
        + [block] * 3
        + [pl.BlockSpec((PAD, BLOCK), lambda i: (0, i)), whole((PAD, width))]
        + [block, block, whole((1, width))],
        out_specs=block,
        out_shape=jax.ShapeDtypeStruct((size, width), BF),
        scratch_shapes=[
            pltpu.VMEM((sum(quads), width, 3 * QUAD), BF),
            pltpu.SemaphoreType.DMA((sum(quads),)),
        ],
        compiler_params=params(),
        cost_estimate=CHEAP,
        name="token_gradient",
    )(index, *flat, dq, dk, dv, joint, down, gh, x, gain)


BOTH = ("dp", "fsdp")


def swap(value, fn, total):
    return lax.ppermute(value, BOTH, [(i, fn(i)) for i in range(total)])


def after(value, *others):
    return lax.optimization_barrier((value,) + others)[0]


class Cube:
    def __init__(self, total, fsdp):
        self.total, self.fsdp = total, fsdp

    def even(self, i):
        return (i // self.fsdp) % 2 == 0

    def sibling(self, value):
        return swap(value, lambda i: i ^ 1, self.total)

    def first(self, value):
        return swap(value, lambda i: i ^ (2 if self.even(i) else 4), self.total)

    def second(self, value):
        b = swap(value, lambda i: i ^ (4 if self.even(i) else 2), self.total)
        c = swap(value, lambda i: i ^ self.fsdp, self.total)
        return b, c

    def index(self):
        here = lax.axis_index("fsdp").astype(jnp.int32)
        odd = lax.axis_index("dp").astype(jnp.int32) % 2
        a, c = 2 + 2 * odd, 4 - 2 * odd
        return jnp.stack([here ^ (m ^ s) for m in (0, a, 6, c) for s in (0, 1)])


def all_sum(value, total):
    if total & (total - 1):
        return lax.psum(value, BOTH)
    half = value.shape[0] // 2
    odd = lax.axis_index("fsdp") % 2
    mine = lax.dynamic_slice_in_dim(value, odd * half, half)
    other = lax.dynamic_slice_in_dim(value, (1 - odd) * half, half)
    mine = mine + swap(other, lambda i: i ^ 1, total)
    bit = 2
    while bit < total:
        mine = mine + swap(mine, lambda i, bit=bit: i ^ bit, total)
        bit *= 2
    other = swap(mine, lambda i: i ^ 1, total)
    top = jnp.where(odd == 0, mine, other)
    low = jnp.where(odd == 0, other, mine)
    return jnp.concatenate([top, low], axis=0)


def local(
    sizes, tokens, lengths, cotangent, gain_one, shift_one, gain_two, shift_two,
    w_qkv, w_proj, w_fc, w_out,
    query_down_factor, query_up_factor, value_down_factor, value_up_factor,
):
    _, size, width = tokens.shape
    dp, fsdp = sizes
    total = dp * fsdp
    x = tokens.reshape(size, width)
    cot = cotangent.reshape(size, width)
    quads = width // QUAD
    half = quads // 2
    w0, w1 = repack(w_qkv, w_proj, half)
    small = (
        x, gain_one[None], shift_one[None],
        query_down_factor.T, value_down_factor.T, query_up_factor, value_up_factor,
    )
    low = tuple(range(half))
    col = 3 * (quads - half) * QUAD
    if fsdp == 8 and dp % 2 == 0:
        cube = Cube(total, fsdp)
        index = cube.index()
        a0, a1, af, ao = [cube.first(w) for w in (w0, w1, w_fc, w_out)]
        s0, s1, sf, so = [cube.sibling(w) for w in (w0, w1, w_fc, w_out)]
        n, narrow, down, upq, upv = norm_one(*small)
        attend = functools.partial(
            attention_forward, lengths, index, n=n, narrow=narrow, upq=upq, upv=upv
        )
        a0 = after(a0, n)
        b0, c0 = cube.second(a0)
        first = [w0, s0] + [p for t in (a0, b0, c0) for p in (t, cube.sibling(t))]
        kept = attend(first, quads=low[:1], here=0, kept=[])
        a1 = after(a1, kept[0])
        b1, c1 = cube.second(a1)
        kept = attend(first, quads=low[1:], here=1, kept=kept)
        b1, c1 = after(b1, kept[0]), after(c1, kept[0])
        second = [w1, s1] + [p for t in (a1, b1, c1) for p in (t, cube.sibling(t))]
        af = after(af, kept[0])
        bf, cf = cube.second(af)
        kept = attend(second, quads=low, here=half, kept=kept)
        bf, cf = after(bf, kept[0]), after(cf, kept[0])
        fcs = [w_fc, sf] + [p for t in (af, bf, cf) for p in (t, cube.sibling(t))]
        ao = after(ao, kept[0])
        bo, co = cube.second(ao)
        o, qx, q, k, v = kept
        pre, hidden = rise(index, second, col, fcs, o, x, gain_two[None], shift_two[None])
        bo, co = after(bo, hidden), after(co, hidden)
        outs = [w_out, so] + [p for t in (ao, bo, co) for p in (t, cube.sibling(t))]
    else:
        index = jnp.zeros((1,), jnp.int32)
        first, second, fcs, outs = [
            [lax.all_gather(w, "fsdp", axis=0, tiled=True)] for w in (w0, w1, w_fc, w_out)
        ]
        n, narrow, down, upq, upv = norm_one(*small)
        kept = attention_forward(lengths, index, first, n, narrow, upq, upv, low, 0, [])
        kept = attention_forward(lengths, index, second, n, narrow, upq, upv, low, half, kept)
        o, qx, q, k, v = kept
        pre, hidden = rise(index, second, col, fcs, o, x, gain_two[None], shift_two[None])
    block_out, gh, ga = fall(
        lengths, index, second, col, fcs, outs, pre, hidden, cot, gain_two[None]
    )
    dq, dk, dv, joint, sums = attention_backward(
        lengths, qx, q, k, v, o, ga, upq, upv, narrow, n
    )
    sums = all_sum(sums, total)
    grad = token_gradient(
        index, [first, second], (half, quads - half), dq, dk, dv, joint, down, gh, x,
        gain_one[None],
    )
    return (
        block_out.reshape(tokens.shape),
        grad.reshape(tokens.shape),
        sums[0:4].T,
        sums[8:12],
        sums[4:8].T,
        sums[12:16],
    )


def solution(mesh):
    rows = P(BOTH, None, None)
    frozen = P("fsdp", None)
    return jax.shard_map(
        functools.partial(local, (mesh.shape["dp"], mesh.shape["fsdp"])),
        mesh=mesh,
        in_specs=(rows, P(BOTH), rows, P(), P(), P(), P()) + (frozen,) * 4 + (P(),) * 4,
        out_specs=(rows, rows, P(), P(), P(), P()),
        check_vma=False,
    )
```

time: 309 us -> 240 us (0.78)
  Pallas kernels: 198 us -> 164 us
  waiting for transfers between devices: 55.4 us -> 34.3 us
  starting transfers between devices: 44.6 us -> 32.1 us
    ppermute x34, waiting for transfers between devices: 55.4 us -> 34.3 us  [swap(): return lax.ppermute(value, BOTH, [(i, fn(i)) for i in range(total)])]
    pallas_call x3 -> x4, Pallas kernels: 126 us -> 110 us  [the longest x1 52 us: fall(): pl.pallas_call(functools.partial(fall_kernel, len(projs), col, steps), gr...]
    pallas_call x4 -> x3, Pallas kernels: 49.4 us -> 34.8 us  [attention_forward(): pl.pallas_call(functools.partial(forward_kernel, len(shards), len(kept),...]
    ppermute x34, starting transfers between devices: 44.6 us -> 32.1 us  [swap(): return lax.ppermute(value, BOTH, [(i, fn(i)) for i in range(total)])]
  transfers between devices with their start and end apart: 34 -> 34, of which waited for: 13 -> 15; matrix products, arithmetic and copies ran while one was open for 0% -> 0% of each run, Pallas kernels for 24% -> 31%
where the time goes in v3:
time: 240 us; the launch traced here: 236 us
  Pallas kernels  164 us (68%)
  waiting for transfers between devices  34.3 us (14%)
  starting transfers between devices  32.1 us (13%)
  local copies, waits for them, and re-layouts  3.52 us (1%)
    pallas_call x1, Pallas kernels, fall(): pl.pallas_call(functools.partial(fall_kernel, len(projs), col, steps), gr...  52 us
    pallas_call x1, Pallas kernels, attention_backward(): pl.pallas_call(backward_kernel, grid=(width // PAIR,), in_specs=[SMEM, pl...  35.6 us
    pallas_call x3, Pallas kernels, attention_forward(): pl.pallas_call(functools.partial(forward_kernel, len(shards), len(kept),...  34.8 us
    ppermute x34, waiting for transfers between devices, swap(): return lax.ppermute(value, BOTH, [(i, fn(i)) for i in range(total)])  34.3 us
    ppermute x34, starting transfers between devices, swap(): return lax.ppermute(value, BOTH, [(i, fn(i)) for i in range(total)])  32.1 us
    pallas_call x1, Pallas kernels, rise(): pl.pallas_call(functools.partial(rise_kernel, len(projs), col), grid=(uni...  19.9 us
    pallas_call x1, Pallas kernels, token_gradient(): pl.pallas_call(functools.partial(token_kernel, [len(p) for p in shards],...  14.8 us
  transfers between devices with their start and end apart: 34, of which 15 were waited for; matrix products, arithmetic and copies ran while one was open for 0% of the time, Pallas kernels for 31%

profile of v3, /device:TPU:1, one launch (start us, length us, event | category | flops | bytes accessed | tf_op | source)
XLA Modules:
  0.0 236.1 jit_solution(13347329886587891294)
XLA Ops:
  0.6 2.2 repack.1
  2.8 2.0 collective-permute-start.3
  4.9 4.5 %norm_one.1 = (bf16[1024,1024]{1,0:T(8,128)(2,1)}, bf16[16,1024]{1,0:T(8,128)(2,1)}, bf16[16,1024]{1,0:T(8,128)(2,1)}, bf16[16,1024]{1,0:T(8,128)(2,1)}, bf16[16,1024]{1,0:T(8,128)(2,1)}) custom-call(bf16[1024,1024]{1,0:T(8,128)(2,1)} %bitcast.22, f32[1,1024]{1,0:T(1,128)} %bitcast.31, f32[1,1024]{1,0:T(1,128)} %bitcast.33, f32[4,1024]{1,0:T(4,128)} %bitcast.27, ...), custom_call_target="tpu_custom_call" | custom-call | tf_op jit(solution)/shard_map/norm_one/pallas_call | solution.py:110
  9.4 4.5 %collective-permute-done.3.refs_2_ = bf16[128,1536]{1,0:T(8,128)(2,1)S(1)} collective-permute-done((bf16[128,1536]{1,0:T(8,128)(2,1)}, bf16[128,1536]{1,0:T(8,128)(2,1)S(1)}, u32[]{:S(2)}, u32[]{:S(2)}) %collective-permute-start.3) | collective-permute-done | bytes 393248 | tf_op jit(solution)/shard_map/ppermute | solution.py:761
  15.1 1.3 collective-permute-start.7
  16.6 2.4 %collective-permute-start.2 = (bf16[128,1536]{1,0:T(8,128)(2,1)S(1)}, bf16[128,1536]{1,0:T(8,128)(2,1)S(1)}, u32[]{:S(2)}, u32[]{:S(2)}) collective-permute-start(bf16[128,1536]{1,0:T(8,128)(2,1)S(1)} %copy-done.11), channel_id=1, source_target_pairs={{0,1},{1,0},{2,3},{3,2},{4,5},{5,4},{6,7},{7,6},{8,9},{9,8},{10,11... | collective-permute-start | bytes 1179656 | tf_op jit(solution)/shard_map/ppermute | solution.py:761
  19.0 4.3 %collective-permute-done.5.refs_4_ = bf16[128,1536]{1,0:T(8,128)(2,1)S(1)} collective-permute-done((bf16[128,1536]{1,0:T(8,128)(2,1)S(1)}, bf16[128,1536]{1,0:T(8,128)(2,1)S(1)}, u32[]{:S(2)}, u32[]{:S(2)}) %collective-permute-start.5) | collective-permute-done | bytes 393248 | tf_op jit(solution)/shard_map/ppermute | solution.py:761
  23.3 2.2 collective-permute-start.6
  26.6 1.2 collective-permute-start.15
  29.2 9.6 %attention_forward.3 = (bf16[1024,1024]{1,0:T(8,128)(2,1)}, bf16[2048,1024]{1,0:T(8,128)(2,1)}, bf16[1024,1024]{1,0:T(8,128)(2,1)}, bf16[1024,1024]{1,0:T(8,128)(2,1)}, bf16[1024,1024]{1,0:T(8,128)(2,1)}) custom-call(s32[1]{0:T(128)S(6)} %copy.41.len_ref, s32[8]{0:T(128)} %stack.35.index_ref, bf16[128,1536]{1,0:T(8,128)(2,1)} %get-tuple-element.49.refs_0_, ...), custom_call_target="tpu_custom_call" | custom-call | flops 1000 | bytes 1000 | tf_op jit(solution)/shard_map/attention_forward/pallas_call | solution.py:288
  38.8 1.4 collective-permute-start.12
  41.3 9.7 %attention_forward.4 = (bf16[1024,1024]{1,0:T(8,128)(2,1)}, bf16[2048,1024]{1,0:T(8,128)(2,1)}, bf16[1024,1024]{1,0:T(8,128)(2,1)}, bf16[1024,1024]{1,0:T(8,128)(2,1)}, bf16[1024,1024]{1,0:T(8,128)(2,1)}) custom-call(s32[1]{0:T(128)S(6)} %copy.41.len_ref, ...), custom_call_target="tpu_custom_call", output_to_operand_aliasing={{0}: (10, {}), {1}: (11, {}), {2}: (12, {}), {3}: (13, {}),... | custom-call | flops 1000 | bytes 1000 | tf_op jit(solution)/shard_map/attention_forward/pallas_call | solution.py:288
  51.0 4.0 %collective-permute-done.12.refs_6_.refs_14_ = bf16[128,2560]{1,0:T(8,128)(2,1)S(1)} collective-permute-done((bf16[128,2560]{1,0:T(8,128)(2,1)S(1)}, bf16[128,2560]{1,0:T(8,128)(2,1)S(1)}, u32[]{:S(2)}, u32[]{:S(2)}) %collective-permute-start.12) | collective-permute-done | bytes 655392 | tf_op jit(solution)/shard_map/ppermute | solution.py:761
  56.0 1.3 collective-permute-start.19
  59.1 3.1 %collective-permute-done.11.refs_5_.refs_13_ = bf16[128,2560]{1,0:T(8,128)(2,1)S(1)} collective-permute-done((bf16[128,2560]{1,0:T(8,128)(2,1)S(1)}, bf16[128,2560]{1,0:T(8,128)(2,1)S(1)}, u32[]{:S(2)}, u32[]{:S(2)}) %collective-permute-start.11) | collective-permute-done | bytes 655392 | tf_op jit(solution)/shard_map/ppermute | solution.py:761
  63.0 15.5 %attention_forward.5 = (bf16[1024,1024]{1,0:T(8,128)(2,1)}, bf16[2048,1024]{1,0:T(8,128)(2,1)}, bf16[1024,1024]{1,0:T(8,128)(2,1)}, bf16[1024,1024]{1,0:T(8,128)(2,1)}, bf16[1024,1024]{1,0:T(8,128)(2,1)}) custom-call(s32[1]{0:T(128)S(6)} %copy.41.len_ref, ...), custom_call_target="tpu_custom_call", output_to_operand_aliasing={{0}: (10, {}), {1}: (11, {}), {2}: (12, {}), {3}: (13, {}),... | custom-call | flops 1000 | bytes 1000 | tf_op jit(solution)/shard_map/attention_forward/pallas_call | solution.py:288
  78.5 2.5 %collective-permute-done.19.refs_14_ = bf16[128,4096]{1,0:T(8,128)(2,1)S(1)} collective-permute-done((bf16[128,4096]{1,0:T(8,128)(2,1)}, bf16[128,4096]{1,0:T(8,128)(2,1)S(1)}, u32[]{:S(2)}, u32[]{:S(2)}) %collective-permute-start.19) | collective-permute-done | bytes 1048608 | tf_op jit(solution)/shard_map/ppermute | solution.py:761
  82.0 1.2 collective-permute-start.18
  83.6 1.6 collective-permute-start.21
  86.8 19.9 %rise.1 = (f32[1024,4096]{1,0:T(8,128)}, f32[1024,1024]{1,0:T(8,128)}) custom-call(s32[8]{0:T(128)} %stack.35.index_ref, bf16[128,2560]{1,0:T(8,128)(2,1)} %get-tuple-element.48.refs_0_.refs_8_, bf16[128,2560]{1,0:T(8,128)(2,1)} %copy-done.3, bf16[128,2560]{1,0:T(8,128)(2,1)} %copy-done.1, bf16[128,2560]{1,0:T(8,128)(2,1)} %copy-done.5, ...), custom_call_target="tpu_custom_call" | custom-call | flops 1000 | bytes 1000 | tf_op jit(solution)/shard_map/rise/pallas_call | solution.py:421
  106.7 1.3 collective-permute-done.26.refs_22_
  109.2 2.2 collective-permute-done.27.refs_23_
  111.4 1.5 collective-permute-done.25.refs_21_
  112.9 52.0 %fall.1 = (bf16[1024,1024]{1,0:T(8,128)(2,1)}, f32[1024,1024]{1,0:T(8,128)}, bf16[1024,1024]{1,0:T(8,128)(2,1)}) custom-call(s32[1]{0:T(128)S(6)} %copy.41.len_ref, s32[8]{0:T(128)} %stack.35.index_ref, bf16[128,2560]{1,0:T(8,128)(2,1)} %get-tuple-element.48.refs_0_.refs_8_, bf16[128,2560]{1,0:T(8,128)(2,1)} %copy-done.3, bf16[128,2560]{1,0:T(8,128)(2,1)} %copy-done.1, ...), custom_call_target="tpu_custom_call" | custom-call | flops 1000 | bytes 1000 | tf_op jit(solution)/shard_map/fall/pallas_call | solution.py:554
  164.9 35.6 %attention_backward.1 = (bf16[1024,1024]{1,0:T(8,128)(2,1)}, bf16[1024,1024]{1,0:T(8,128)(2,1)}, bf16[1024,1024]{1,0:T(8,128)(2,1)}, bf16[16,1024]{1,0:T(8,128)(2,1)}, f32[16,1024]{1,0:T(8,128)}) custom-call(s32[1]{0:T(128)S(6)} %copy.41.len_ref, bf16[2048,1024]{1,0:T(8,128)(2,1)} %get-tuple-element.78.qx_ref, bf16[1024,1024]{1,0:T(8,128)(2,1)} %get-tuple-element.79.q_ref, ...), custom_call_target="tpu_custom_call" | custom-call | flops 1000 | bytes 1000 | tf_op jit(solution)/shard_map/attention_backward/pallas_call | solution.py:678
  203.6 2.5 %collective-permute-done.29 = f32[8,1024]{1,0:T(8,128)S(1)} collective-permute-done((f32[8,1024]{1,0:T(8,128)S(1)}, f32[8,1024]{1,0:T(8,128)S(1)}, u32[]{:S(2)}, u32[]{:S(2)}) %collective-permute-start.29) | collective-permute-done | bytes 32800 | tf_op jit(solution)/shard_map/ppermute | solution.py:761
  206.3 2.5 %collective-permute-done.30 = f32[8,1024]{1,0:T(8,128)S(1)} collective-permute-done((f32[8,1024]{1,0:T(8,128)S(1)}, f32[8,1024]{1,0:T(8,128)S(1)}, u32[]{:S(2)}, u32[]{:S(2)}) %collective-permute-start.30) | collective-permute-done | bytes 32800 | tf_op jit(solution)/shard_map/ppermute | solution.py:761
  209.0 2.6 %collective-permute-done.31 = f32[8,1024]{1,0:T(8,128)S(1)} collective-permute-done((f32[8,1024]{1,0:T(8,128)S(1)}, f32[8,1024]{1,0:T(8,128)S(1)}, u32[]{:S(2)}, u32[]{:S(2)}) %collective-permute-start.31) | collective-permute-done | bytes 32800 | tf_op jit(solution)/shard_map/ppermute | solution.py:761
  211.6 2.3 collective-permute-start.32
  213.9 1.6 collective-permute-done.32
  215.5 4.9 %collective-permute-start.33 = (f32[8,1024]{1,0:T(8,128)S(1)}, f32[8,1024]{1,0:T(8,128)S(1)}, u32[]{:S(2)}, u32[]{:S(2)}) collective-permute-start(f32[8,1024]{1,0:T(8,128)S(1)} %add.40), channel_id=1, source_target_pairs={{0,1},{1,0},{2,3},{3,2},{4,5},{5,4},{6,7},{7,6},{8,9},{9,8},{10,11... | collective-permute-start | bytes 98312 | tf_op jit(solution)/shard_map/ppermute | solution.py:761
  220.5 14.8 %token_gradient.1 = bf16[1024,1024]{1,0:T(8,128)(2,1)} custom-call(s32[8]{0:T(128)} %stack.35.index_ref, bf16[128,1536]{1,0:T(8,128)(2,1)} %get-tuple-element.49.refs_0_, bf16[128,1536]{1,0:T(8,128)(2,1)} %copy-done.15, bf16[128,1536]{1,0:T(8,128)(2,1)} %copy-done.12, bf16[128,1536]{1,0:T(8,128)(2,1)} %collective-permute-done.4.refs_3_, ...), custom_call_target="tpu_custom_call" | custom-call | flops 1000 | bytes 1000 | tf_op jit(solution)/shard_map/token_gradient/pallas_call | solution.py:737
  (90 shorter events, 16.2 us)
Async XLA Ops:
  2.8 11.1 %collective-permute-start.3 = (bf16[128,1536]{1,0:T(8,128)(2,1)}, bf16[128,1536]{1,0:T(8,128)(2,1)S(1)}, u32[]{:S(2)}, u32[]{:S(2)}) collective-permute-start(bf16[128,1536]{1,0:T(8,128)(2,1)} %get-tuple-element.49.refs_0_), channel_id=1, source_target_pairs={{0,2},{1,3},{2,0},{3,1},{4,6},{5,7},{6,4},{7,5},{8,12},{9,13},{10,... | collective-permute-start | bytes 1179656 | tf_op jit(solution)/shard_map/ppermute | solution.py:761
  13.9 9.4 %collective-permute-start.5 = (bf16[128,1536]{1,0:T(8,128)(2,1)S(1)}, bf16[128,1536]{1,0:T(8,128)(2,1)S(1)}, u32[]{:S(2)}, u32[]{:S(2)}) collective-permute-start(bf16[128,1536]{1,0:T(8,128)(2,1)S(1)} %collective-permute-done.3.refs_2_), channel_id=1, source_target_pairs={{0,4},{1,5},{2,6},{3,7},{4,0},{5,1},{6,2},{7,3},{8,10},{9,11},{10,... | collective-permute-start | bytes 1179656 | tf_op jit(solution)/shard_map/ppermute | solution.py:761
  15.1 10.4 %collective-permute-start.7 = (bf16[128,1536]{1,0:T(8,128)(2,1)S(1)}, bf16[128,1536]{1,0:T(8,128)(2,1)S(1)}, u32[]{:S(2)}, u32[]{:S(2)}) collective-permute-start(bf16[128,1536]{1,0:T(8,128)(2,1)S(1)} %collective-permute-done.3.refs_2_), channel_id=1, source_target_pairs={{0,8},{1,9},{2,10},{3,11},{4,12},{5,13},{6,14},{7,15},{8,0},{9,1},... | collective-permute-start | bytes 1179656 | tf_op jit(solution)/shard_map/ppermute | solution.py:761
  16.4 22.4 %collective-permute-start.1 = (bf16[128,2560]{1,0:T(8,128)(2,1)S(1)}, bf16[128,2560]{1,0:T(8,128)(2,1)S(1)}, u32[]{:S(2)}, u32[]{:S(2)}) collective-permute-start(bf16[128,2560]{1,0:T(8,128)(2,1)S(1)} %copy-done), channel_id=1, source_target_pairs={{0,2},{1,3},{2,0},{3,1},{4,6},{5,7},{6,4},{7,5},{8,12},{9,13},{10,... | collective-permute-start | bytes 1966088 | tf_op jit(solution)/shard_map/ppermute | solution.py:761
  16.6 10.0 %collective-permute-start.2 = (bf16[128,1536]{1,0:T(8,128)(2,1)S(1)}, bf16[128,1536]{1,0:T(8,128)(2,1)S(1)}, u32[]{:S(2)}, u32[]{:S(2)}) collective-permute-start(bf16[128,1536]{1,0:T(8,128)(2,1)S(1)} %copy-done.11), channel_id=1, source_target_pairs={{0,1},{1,0},{2,3},{3,2},{4,5},{5,4},{6,7},{7,6},{8,9},{9,8},{10,11... | collective-permute-start | bytes 1179656 | tf_op jit(solution)/shard_map/ppermute | solution.py:761
  19.0 10.1 %collective-permute-start.4 = (bf16[128,1536]{1,0:T(8,128)(2,1)S(1)}, bf16[128,1536]{1,0:T(8,128)(2,1)}, u32[]{:S(2)}, u32[]{:S(2)}) collective-permute-start(bf16[128,1536]{1,0:T(8,128)(2,1)S(1)} %collective-permute-done.3.refs_2_), channel_id=1, source_target_pairs={{0,1},{1,0},{2,3},{3,2},{4,5},{5,4},{6,7},{7,6},{8,9},{9,8},{10,11... | collective-permute-start | bytes 1179656 | tf_op jit(solution)/shard_map/ppermute | solution.py:761
  23.3 5.8 %collective-permute-start.6 = (bf16[128,1536]{1,0:T(8,128)(2,1)S(1)}, bf16[128,1536]{1,0:T(8,128)(2,1)}, u32[]{:S(2)}, u32[]{:S(2)}) collective-permute-start(bf16[128,1536]{1,0:T(8,128)(2,1)S(1)} %collective-permute-done.5.refs_4_), channel_id=1, source_target_pairs={{0,1},{1,0},{2,3},{3,2},{4,5},{5,4},{6,7},{7,6},{8,9},{9,8},{10,11... | collective-permute-start | bytes 1179656 | tf_op jit(solution)/shard_map/ppermute | solution.py:761
  25.5 3.7 %collective-permute-start.8 = (bf16[128,1536]{1,0:T(8,128)(2,1)S(1)}, bf16[128,1536]{1,0:T(8,128)(2,1)}, u32[]{:S(2)}, u32[]{:S(2)}) collective-permute-start(bf16[128,1536]{1,0:T(8,128)(2,1)S(1)} %collective-permute-done.7.refs_6_), channel_id=1, source_target_pairs={{0,1},{1,0},{2,3},{3,2},{4,5},{5,4},{6,7},{7,6},{8,9},{9,8},{10,11... | collective-permute-start | bytes 1179656 | tf_op jit(solution)/shard_map/ppermute | solution.py:761
  26.6 29.4 %collective-permute-start.15 = (bf16[128,4096]{1,0:T(8,128)(2,1)}, bf16[128,4096]{1,0:T(8,128)(2,1)}, u32[]{:S(2)}, u32[]{:S(2)}) collective-permute-start(bf16[128,4096]{1,0:T(8,128)(2,1)} %refs_8_.3), channel_id=1, source_target_pairs={{0,2},{1,3},{2,0},{3,1},{4,6},{5,7},{6,4},{7,5},{8,12},{9,13},{10,... | collective-permute-start | bytes 3145736 | tf_op jit(solution)/shard_map/ppermute | solution.py:761
  38.8 16.1 %collective-permute-start.12 = (bf16[128,2560]{1,0:T(8,128)(2,1)S(1)}, bf16[128,2560]{1,0:T(8,128)(2,1)S(1)}, u32[]{:S(2)}, u32[]{:S(2)}) collective-permute-start(bf16[128,2560]{1,0:T(8,128)(2,1)S(1)} %collective-permute-done.1.refs_2_.refs_10_), channel_id=1, source_target_pairs={{0,8},{1,9},{2,10},{3,11},{4,12},{5,13},{6,14},{7,15},{8,0},{9,1},... | collective-permute-start | bytes 1966088 | tf_op jit(solution)/shard_map/ppermute | solution.py:761
  40.2 17.2 %collective-permute-start = (bf16[128,2560]{1,0:T(8,128)(2,1)S(1)}, bf16[128,2560]{1,0:T(8,128)(2,1)S(1)}, u32[]{:S(2)}, u32[]{:S(2)}) collective-permute-start(bf16[128,2560]{1,0:T(8,128)(2,1)S(1)} %copy-done), channel_id=1, source_target_pairs={{0,1},{1,0},{2,3},{3,2},{4,5},{5,4},{6,7},{7,6},{8,9},{9,8},{10,11... | collective-permute-start | bytes 1966088 | tf_op jit(solution)/shard_map/ppermute | solution.py:761
  40.8 16.8 %collective-permute-start.10 = (bf16[128,2560]{1,0:T(8,128)(2,1)S(1)}, bf16[128,2560]{1,0:T(8,128)(2,1)S(1)}, u32[]{:S(2)}, u32[]{:S(2)}) collective-permute-start(bf16[128,2560]{1,0:T(8,128)(2,1)S(1)} %collective-permute-done.1.refs_2_.refs_10_), channel_id=1, source_target_pairs={{0,4},{1,5},{2,6},{3,7},{4,0},{5,1},{6,2},{7,3},{8,10},{9,11},{10,... | collective-permute-start | bytes 1966088 | tf_op jit(solution)/shard_map/ppermute | solution.py:761
  41.0 17.0 %collective-permute-start.9 = (bf16[128,2560]{1,0:T(8,128)(2,1)S(1)}, bf16[128,2560]{1,0:T(8,128)(2,1)S(1)}, u32[]{:S(2)}, u32[]{:S(2)}) collective-permute-start(bf16[128,2560]{1,0:T(8,128)(2,1)S(1)} %collective-permute-done.1.refs_2_.refs_10_), channel_id=1, source_target_pairs={{0,1},{1,0},{2,3},{3,2},{4,5},{5,4},{6,7},{7,6},{8,9},{9,8},{10,11... | collective-permute-start | bytes 1966088 | tf_op jit(solution)/shard_map/ppermute | solution.py:761
  55.0 4.0 %collective-permute-start.13 = (bf16[128,2560]{1,0:T(8,128)(2,1)S(1)}, bf16[128,2560]{1,0:T(8,128)(2,1)S(1)}, u32[]{:S(2)}, u32[]{:S(2)}) collective-permute-start(bf16[128,2560]{1,0:T(8,128)(2,1)S(1)} %collective-permute-done.12.refs_6_.refs_14_), channel_id=1, source_target_pairs={{0,1},{1,0},{2,3},{3,2},{4,5},{5,4},{6,7},{7,6},{8,9},{9,8},{10,11... | collective-permute-start | bytes 1966088 | tf_op jit(solution)/shard_map/ppermute | solution.py:761
  56.0 25.0 %collective-permute-start.19 = (bf16[128,4096]{1,0:T(8,128)(2,1)}, bf16[128,4096]{1,0:T(8,128)(2,1)S(1)}, u32[]{:S(2)}, u32[]{:S(2)}) collective-permute-start(bf16[128,4096]{1,0:T(8,128)(2,1)} %collective-permute-done.15.refs_10_), channel_id=1, source_target_pairs={{0,8},{1,9},{2,10},{3,11},{4,12},{5,13},{6,14},{7,15},{8,0},{9,1},... | collective-permute-start | bytes 3145736 | tf_op jit(solution)/shard_map/ppermute | solution.py:761
  57.3 24.7 %collective-permute-start.17 = (bf16[128,4096]{1,0:T(8,128)(2,1)}, bf16[128,4096]{1,0:T(8,128)(2,1)}, u32[]{:S(2)}, u32[]{:S(2)}) collective-permute-start(bf16[128,4096]{1,0:T(8,128)(2,1)} %collective-permute-done.15.refs_10_), channel_id=1, source_target_pairs={{0,4},{1,5},{2,6},{3,7},{4,0},{5,1},{6,2},{7,3},{8,10},{9,11},{10,... | collective-permute-start | bytes 3145736 | tf_op jit(solution)/shard_map/ppermute | solution.py:761
  57.6 25.7 %collective-permute-start.22 = (bf16[512,1024]{1,0:T(8,128)(2,1)}, bf16[512,1024]{1,0:T(8,128)(2,1)}, u32[]{:S(2)}, u32[]{:S(2)}) collective-permute-start(bf16[512,1024]{1,0:T(8,128)(2,1)} %refs_16_.1), channel_id=1, source_target_pairs={{0,2},{1,3},{2,0},{3,1},{4,6},{5,7},{6,4},{7,5},{8,12},{9,13},{10,... | collective-permute-start | bytes 3145736 | tf_op jit(solution)/shard_map/ppermute | solution.py:761
  58.1 25.4 %collective-permute-start.14 = (bf16[128,4096]{1,0:T(8,128)(2,1)}, bf16[128,4096]{1,0:T(8,128)(2,1)}, u32[]{:S(2)}, u32[]{:S(2)}) collective-permute-start(bf16[128,4096]{1,0:T(8,128)(2,1)} %refs_8_.3), channel_id=1, source_target_pairs={{0,1},{1,0},{2,3},{3,2},{4,5},{5,4},{6,7},{7,6},{8,9},{9,8},{10,11... | collective-permute-start | bytes 3145736 | tf_op jit(solution)/shard_map/ppermute | solution.py:761
  59.0 3.2 %collective-permute-start.11 = (bf16[128,2560]{1,0:T(8,128)(2,1)S(1)}, bf16[128,2560]{1,0:T(8,128)(2,1)S(1)}, u32[]{:S(2)}, u32[]{:S(2)}) collective-permute-start(bf16[128,2560]{1,0:T(8,128)(2,1)S(1)} %collective-permute-done.10.refs_4_.refs_12_), channel_id=1, source_target_pairs={{0,1},{1,0},{2,3},{3,2},{4,5},{5,4},{6,7},{7,6},{8,9},{9,8},{10,11... | collective-permute-start | bytes 1966088 | tf_op jit(solution)/shard_map/ppermute | solution.py:761
  62.2 21.4 %collective-permute-start.16 = (bf16[128,4096]{1,0:T(8,128)(2,1)}, bf16[128,4096]{1,0:T(8,128)(2,1)}, u32[]{:S(2)}, u32[]{:S(2)}) collective-permute-start(bf16[128,4096]{1,0:T(8,128)(2,1)} %collective-permute-done.15.refs_10_), channel_id=1, source_target_pairs={{0,1},{1,0},{2,3},{3,2},{4,5},{5,4},{6,7},{7,6},{8,9},{9,8},{10,11... | collective-permute-start | bytes 3145736 | tf_op jit(solution)/shard_map/ppermute | solution.py:761
  81.1 4.2 %collective-permute-start.20 = (bf16[128,4096]{1,0:T(8,128)(2,1)S(1)}, bf16[128,4096]{1,0:T(8,128)(2,1)S(1)}, u32[]{:S(2)}, u32[]{:S(2)}) collective-permute-start(bf16[128,4096]{1,0:T(8,128)(2,1)S(1)} %collective-permute-done.19.refs_14_), channel_id=1, source_target_pairs={{0,1},{1,0},{2,3},{3,2},{4,5},{5,4},{6,7},{7,6},{8,9},{9,8},{10,11... | collective-permute-start | bytes 3145736 | tf_op jit(solution)/shard_map/ppermute | solution.py:761
  82.0 3.8 %collective-permute-start.18 = (bf16[128,4096]{1,0:T(8,128)(2,1)}, bf16[128,4096]{1,0:T(8,128)(2,1)S(1)}, u32[]{:S(2)}, u32[]{:S(2)}) collective-permute-start(bf16[128,4096]{1,0:T(8,128)(2,1)} %collective-permute-done.17.refs_12_), channel_id=1, source_target_pairs={{0,1},{1,0},{2,3},{3,2},{4,5},{5,4},{6,7},{7,6},{8,9},{9,8},{10,11... | collective-permute-start | bytes 3145736 | tf_op jit(solution)/shard_map/ppermute | solution.py:761
  83.2 24.7 %collective-permute-start.26 = (bf16[512,1024]{1,0:T(8,128)(2,1)}, bf16[512,1024]{1,0:T(8,128)(2,1)S(1)}, u32[]{:S(2)}, u32[]{:S(2)}) collective-permute-start(bf16[512,1024]{1,0:T(8,128)(2,1)} %collective-permute-done.22.refs_18_), channel_id=1, source_target_pairs={{0,8},{1,9},{2,10},{3,11},{4,12},{5,13},{6,14},{7,15},{8,0},{9,1},... | collective-permute-start | bytes 3145736 | tf_op jit(solution)/shard_map/ppermute | solution.py:761
  83.4 25.6 %collective-permute-start.24 = (bf16[512,1024]{1,0:T(8,128)(2,1)}, bf16[512,1024]{1,0:T(8,128)(2,1)S(1)}, u32[]{:S(2)}, u32[]{:S(2)}) collective-permute-start(bf16[512,1024]{1,0:T(8,128)(2,1)} %collective-permute-done.22.refs_18_), channel_id=1, source_target_pairs={{0,4},{1,5},{2,6},{3,7},{4,0},{5,1},{6,2},{7,3},{8,10},{9,11},{10,... | collective-permute-start | bytes 3145736 | tf_op jit(solution)/shard_map/ppermute | solution.py:761
  83.6 25.6 %collective-permute-start.21 = (bf16[512,1024]{1,0:T(8,128)(2,1)}, bf16[512,1024]{1,0:T(8,128)(2,1)}, u32[]{:S(2)}, u32[]{:S(2)}) collective-permute-start(bf16[512,1024]{1,0:T(8,128)(2,1)} %refs_16_.1), channel_id=1, source_target_pairs={{0,1},{1,0},{2,3},{3,2},{4,5},{5,4},{6,7},{7,6},{8,9},{9,8},{10,11... | collective-permute-start | bytes 3145736 | tf_op jit(solution)/shard_map/ppermute | solution.py:761
  85.3 23.9 %collective-permute-start.23 = (bf16[512,1024]{1,0:T(8,128)(2,1)}, bf16[512,1024]{1,0:T(8,128)(2,1)}, u32[]{:S(2)}, u32[]{:S(2)}) collective-permute-start(bf16[512,1024]{1,0:T(8,128)(2,1)} %collective-permute-done.22.refs_18_), channel_id=1, source_target_pairs={{0,1},{1,0},{2,3},{3,2},{4,5},{5,4},{6,7},{7,6},{8,9},{9,8},{10,11... | collective-permute-start | bytes 3145736 | tf_op jit(solution)/shard_map/ppermute | solution.py:761
  108.0 3.5 %collective-permute-start.27 = (bf16[512,1024]{1,0:T(8,128)(2,1)S(1)}, bf16[512,1024]{1,0:T(8,128)(2,1)}, u32[]{:S(2)}, u32[]{:S(2)}) collective-permute-start(bf16[512,1024]{1,0:T(8,128)(2,1)S(1)} %collective-permute-done.26.refs_22_), channel_id=1, source_target_pairs={{0,1},{1,0},{2,3},{3,2},{4,5},{5,4},{6,7},{7,6},{8,9},{9,8},{10,11... | collective-permute-start | bytes 3145736 | tf_op jit(solution)/shard_map/ppermute | solution.py:761
  109.0 3.9 %collective-permute-start.25 = (bf16[512,1024]{1,0:T(8,128)(2,1)S(1)}, bf16[512,1024]{1,0:T(8,128)(2,1)}, u32[]{:S(2)}, u32[]{:S(2)}) collective-permute-start(bf16[512,1024]{1,0:T(8,128)(2,1)S(1)} %collective-permute-done.24.refs_20_), channel_id=1, source_target_pairs={{0,1},{1,0},{2,3},{3,2},{4,5},{5,4},{6,7},{7,6},{8,9},{9,8},{10,11... | collective-permute-start | bytes 3145736 | tf_op jit(solution)/shard_map/ppermute | solution.py:761
  203.3 2.8 %collective-permute-start.29 = (f32[8,1024]{1,0:T(8,128)S(1)}, f32[8,1024]{1,0:T(8,128)S(1)}, u32[]{:S(2)}, u32[]{:S(2)}) collective-permute-start(f32[8,1024]{1,0:T(8,128)S(1)} %dynamic-slice_add_fusion), channel_id=1, source_target_pairs={{0,2},{1,3},{2,0},{3,1},{4,6},{5,7},{6,4},{7,5},{8,10},{9,11},{10,... | collective-permute-start | bytes 98312 | tf_op jit(solution)/shard_map/ppermute | solution.py:761
  206.1 2.8 %collective-permute-start.30 = (f32[8,1024]{1,0:T(8,128)S(1)}, f32[8,1024]{1,0:T(8,128)S(1)}, u32[]{:S(2)}, u32[]{:S(2)}) collective-permute-start(f32[8,1024]{1,0:T(8,128)S(1)} %add.37), channel_id=1, source_target_pairs={{0,4},{1,5},{2,6},{3,7},{4,0},{5,1},{6,2},{7,3},{8,12},{9,13},{10,... | collective-permute-start | bytes 98312 | tf_op jit(solution)/shard_map/ppermute | solution.py:761
  211.6 3.9 %collective-permute-start.32 = (f32[8,1024]{1,0:T(8,128)S(1)}, f32[8,1024]{1,0:T(8,128)S(1)}, u32[]{:S(2)}, u32[]{:S(2)}) collective-permute-start(f32[8,1024]{1,0:T(8,128)S(1)} %add.39), channel_id=1, source_target_pairs={{0,16},{1,17},{2,18},{3,19},{4,20},{5,21},{6,22},{7,23},{8,24},{9,... | collective-permute-start | bytes 98312 | tf_op jit(solution)/shard_map/ppermute | solution.py:761
  215.5 19.7 %collective-permute-start.33 = (f32[8,1024]{1,0:T(8,128)S(1)}, f32[8,1024]{1,0:T(8,128)S(1)}, u32[]{:S(2)}, u32[]{:S(2)}) collective-permute-start(f32[8,1024]{1,0:T(8,128)S(1)} %add.40), channel_id=1, source_target_pairs={{0,1},{1,0},{2,3},{3,2},{4,5},{5,4},{6,7},{7,6},{8,9},{9,8},{10,11... | collective-permute-start | bytes 98312 | tf_op jit(solution)/shard_map/ppermute | solution.py:761
  (20 other events, 113.3 us)

commit v4 on v3

--- a/solution.py
+++ b/solution.py
@@ -323,18 +323,23 @@
 
 
 def out_slice(index_ref, outs, step):
-    rows = outs[0].shape[0]
+    part = outs[0][0].shape[0]
+    rows = part * len(outs)
+    pieces = []
     if rows >= FF_STEP:
-        shard, part = divmod(step, rows // FF_STEP)
-        begin = index_ref[shard] * rows + part * FF_STEP
-        return pl.multiple_of(begin, FF_STEP), [(outs[shard], part * FF_STEP, 0, FF_STEP)]
+        shard, place = divmod(step, rows // FF_STEP)
+        begin = pl.multiple_of(index_ref[shard] * rows + place * FF_STEP, FF_STEP)
+        wide = min(part, FF_STEP)
+        for at in range(place * FF_STEP, (place + 1) * FF_STEP, wide):
+            pieces.append((outs[at // part][shard], at % part, at - place * FF_STEP, wide))
+        return begin, pieces
     each = FF_STEP // rows
     begin = index_ref[step * each] * rows // FF_STEP * FF_STEP
     begin = pl.multiple_of(begin, FF_STEP)
-    pieces = [
-        (outs[i], 0, pl.multiple_of(index_ref[i] * rows - begin, rows), rows)
-        for i in range(step * each, (step + 1) * each)
-    ]
+    for i in range(step * each, (step + 1) * each):
+        to = index_ref[i] * rows - begin
+        for h, some in enumerate(outs):
+            pieces.append((some[i], 0, pl.multiple_of(to + h * part, part), part))
     return begin, pieces
 
 
@@ -347,34 +352,41 @@
     return act, slope
 
 
+def split_list(refs, count, halves):
+    lists = [refs[h * count : (h + 1) * count] for h in range(halves)]
+    return lists, refs[count * halves :]
+
+
 def blocks_of(size, rows):
     return [pl.ds(i * rows, rows) for i in range(size // rows)]
 
 
-def rise_kernel(count, col, index_ref, *refs):
+def rise_kernel(count, halves, col, index_ref, *refs):
     projs, refs = refs[:count], refs[count:]
-    fcs, refs = refs[:count], refs[count:]
+    fcs, refs = split_list(refs, count, halves)
     (o_ref, x_ref, gain_ref, shift_ref, pre_ref, hidden_ref,
      wproj, fbuf, obuf, xbuf, hidden, n2, psem, fsem, osem, hsem) = refs
     step = pl.program_id(0)
-    steps = pl.num_programs(0)
     size, width = xbuf.shape
+    steps = halves * fcs[0][0].shape[1] // FF_STEP
     slot = lax.rem(step, 2)
     places = blocks_of(size, BLOCK)
 
-    def fc_copies(s, slot):
-        col = pl.multiple_of(s * FF_STEP, FF_STEP)
-        return rows_copies(index_ref, fcs, col, FF_STEP, fbuf.at[slot], fsem.at[slot])
+    def fc_copies(s):
+        slot = s % 2
+        each = steps // halves
+        col = s % each * FF_STEP
+        return rows_copies(index_ref, fcs[s // each], col, FF_STEP, fbuf.at[slot], fsem.at[slot])
 
     def row_copies(i):
-        at = places[i]
+        at = pl.ds(pl.multiple_of(i * BLOCK, BLOCK), BLOCK)
         return [
             pltpu.make_async_copy(o_ref.at[at, :], obuf.at[at, :], osem.at[i]),
             pltpu.make_async_copy(x_ref.at[at, :], xbuf.at[at, :], osem.at[i]),
         ]
 
     def hidden_copy(i):
-        at = places[i]
+        at = pl.ds(pl.multiple_of(i * BLOCK, BLOCK), BLOCK)
         return pltpu.make_async_copy(hidden.at[at, :], hidden_ref.at[at, :], hsem)
 
     @pl.when(step == 0)
@@ -385,28 +397,44 @@
         for i in range(len(places)):
             for c in row_copies(i):
                 c.start()
-        for c in fc_copies(0, 0):
+        for c in fc_copies(0):
             c.start()
         for c in first:
             c.wait()
-        for i, at in enumerate(places):
+
+        def begin(i, carry):
+            at = pl.ds(pl.multiple_of(i * BLOCK, BLOCK), BLOCK)
             for c in row_copies(i):
                 c.wait()
-            hidden[at, :] = xbuf[at, :].astype(F32) + dot(obuf[at, :], wproj[...])
+            total = xbuf[at, :].astype(F32) + dot(obuf[at, :], wproj[...])
+            hidden[at, :] = total
             hidden_copy(i).start()
-        for at in places:
-            xhat, _ = norm_stats(hidden[at, :])
+            xhat, _ = norm_stats(total)
             n2[at, :] = (xhat * gain_ref[...] + shift_ref[...]).astype(BF)
-
-    @pl.when(step + 1 < steps)
-    def _():
-        for c in fc_copies(step + 1, 1 - slot):
-            c.start()
-
-    for c in fc_copies(step, slot):
-        c.wait()
-    for at in blocks_of(size, ROWS):
+            return carry
+
+        lax.fori_loop(0, len(places), begin, 0)
+
+    for s in range(1, steps):
+
+        @pl.when(step + 1 == s)
+        def _(s=s):
+            for c in fc_copies(s):
+                c.start()
+
+    for even in range(2):
+
+        @pl.when(slot == even)
+        def _(even=even):
+            for c in fc_copies(even):
+                c.wait()
+
+    def body(i, carry):
+        at = pl.ds(pl.multiple_of(i * ROWS, ROWS), ROWS)
         pre_ref[at, :] = dot(n2[at, :], fbuf[slot])
+        return carry
+
+    lax.fori_loop(0, size // ROWS, body, 0)
 
     @pl.when(step == steps - 1)
     def _():
@@ -416,15 +444,16 @@
 
 def rise(index, projs, col, fcs, o, x, gain, shift):
     size, width = x.shape
-    units = fcs[0].shape[1]
+    units = sum(half[0].shape[1] for half in fcs)
     small = whole((1, width))
+    flat = [f for half in fcs for f in half]
     return pl.pallas_call(
-        functools.partial(rise_kernel, len(projs), col),
+        functools.partial(rise_kernel, len(projs), len(fcs), col),
         grid=(units // FF_STEP,),
-        in_specs=[SMEM] + [ANY] * (2 * len(projs) + 2) + [small, small],
-        out_specs=[pl.BlockSpec((size, FF_STEP), lambda s: (0, s)), ANY],
+        in_specs=[SMEM] + [ANY] * (len(projs) + len(flat) + 2) + [small, small],
+        out_specs=[pl.BlockSpec((None, size, FF_STEP), lambda s: (s, 0, 0)), ANY],
         out_shape=[
-            jax.ShapeDtypeStruct((size, units), F32),
+            jax.ShapeDtypeStruct((units // FF_STEP, size, FF_STEP), F32),
             jax.ShapeDtypeStruct((size, width), F32),
         ],
         scratch_shapes=[
@@ -442,15 +471,15 @@
         compiler_params=params(),
         cost_estimate=CHEAP,
         name="rise",
-    )(index, *projs, *fcs, o, x, gain, shift)
-
-
-def fall_kernel(count, col, steps, len_ref, index_ref, *refs):
+    )(index, *projs, *flat, o, x, gain, shift)
+
+
+def fall_kernel(count, halves, col, steps, len_ref, index_ref, *refs):
     projs, refs = refs[:count], refs[count:]
-    fcs, refs = refs[:count], refs[count:]
-    outs, refs = refs[:count], refs[count:]
+    fcs, refs = split_list(refs, count, halves[0])
+    outs, refs = split_list(refs, count, halves[1])
     (pre_ref, hidden_ref, cot_ref, gain_ref, block_ref, gh_ref, ga_ref,
-     wproj, fbuf, obuf, pbuf, hidden, cbuf, low, acc, back, block, gatt, sem, lsem, wsem) = refs
+     wproj, fbuf, obuf, pbuf, hidden, cbuf, low, acc, back, block, gatt, sem, fsem, lsem, wsem) = refs
     step = pl.program_id(0)
     size, width = low.shape
     slot = lax.rem(step, 2)
@@ -465,9 +494,30 @@
                     ref.at[at : at + rows, :], obuf.at[slot, pl.ds(to, rows), :], sem.at[slot]
                 )
             )
-        src = pre_ref.at[:, pl.ds(begin, FF_STEP)]
+        src = pre_ref.at[begin // FF_STEP]
         found.append(pltpu.make_async_copy(src, pbuf.at[slot], sem.at[slot]))
-        return found + rows_copies(index_ref, fcs, begin, FF_STEP, fbuf.at[slot], sem.at[slot])
+        return found
+
+    def fc_copies(s):
+        begin, _ = out_slice(index_ref, outs, s)
+        slot = s % 2
+        wide = fcs[0][0].shape[1]
+        which = begin // wide
+        at = pl.multiple_of(begin - which * wide, FF_STEP)
+        return which, [
+            rows_copies(index_ref, some, at, FF_STEP, fbuf.at[slot], fsem.at[slot]) for some in fcs
+        ]
+
+    def start(s):
+        for c in copies(s):
+            c.start()
+        which, found = fc_copies(s)
+        for h, some in enumerate(found):
+
+            @pl.when(which == h)
+            def _(some=some):
+                for c in some:
+                    c.start()
 
     late = [pltpu.make_async_copy(hidden_ref, hidden, lsem.at[1])]
     late += rows_copies(index_ref, projs, col, width, wproj, lsem.at[1])
@@ -476,58 +526,54 @@
     @pl.when(step == 0)
     def _():
         first.start()
-        for c in copies(0):
-            c.start()
-        for c in copies(1):
-            c.start()
+        start(0)
+        start(1)
         for c in late:
             c.start()
         first.wait()
         for i, at in enumerate(blocks_of(size, BLOCK)):
             keep = row((BLOCK, 1)) + i * BLOCK < len_ref[0]
             low[at, :] = jnp.where(keep, cbuf[at, :].astype(F32), 0.0).astype(BF)
+            acc[at, :] = jnp.zeros((BLOCK, width), F32)
+            back[at, :] = jnp.zeros((BLOCK, width), F32)
 
     for s in range(2, steps):
 
         @pl.when(step + 1 == s)
         def _(s=s):
-            for c in copies(s):
-                c.start()
+            start(s)
 
     for even in range(2):
 
         @pl.when(slot == even)
         def _(even=even):
-            for c in copies(even):
+            for c in copies(even) + fc_copies(even)[1][0]:
                 c.wait()
 
-    def body(begin):
-        for at in blocks_of(size, ROWS):
-            act, slope = gelu_both(pbuf[slot, at, :])
-            mlp = dot(act.astype(BF), obuf[slot])
-            grad = (dot_nt(low[at, :], obuf[slot]) * slope).astype(BF)
-            u = dot_nt(grad, fbuf[slot])
-            if begin:
-                acc[at, :] = mlp
-                back[at, :] = u
-            else:
-                acc[at, :] += mlp
-                back[at, :] += u
-
-    @pl.when(step == 0)
-    def _():
-        body(True)
-
-    @pl.when(step > 0)
-    def _():
-        body(False)
+    def body(i, carry):
+        at = pl.ds(pl.multiple_of(i * ROWS, ROWS), ROWS)
+        act, slope = gelu_both(pbuf[slot, at, :])
+        acc[at, :] += dot(act.astype(BF), obuf[slot])
+        grad = (dot_nt(low[at, :], obuf[slot]) * slope).astype(BF)
+        back[at, :] += dot_nt(grad, fbuf[slot])
+        return carry
+
+    lax.fori_loop(0, size // ROWS, body, 0)
 
     @pl.when(step == steps - 1)
     def _():
         for c in late:
             c.wait()
-        sent = []
-        for i, at in enumerate(blocks_of(size, BLOCK)):
+        def out_copies(i):
+            at = pl.ds(pl.multiple_of(i * BLOCK, BLOCK), BLOCK)
+            return [
+                pltpu.make_async_copy(block.at[at, :], block_ref.at[at, :], wsem),
+                pltpu.make_async_copy(hidden.at[at, :], gh_ref.at[at, :], wsem),
+                pltpu.make_async_copy(gatt.at[at, :], ga_ref.at[at, :], wsem),
+            ]
+
+        def finish(i, carry):
+            at = pl.ds(pl.multiple_of(i * BLOCK, BLOCK), BLOCK)
             h = hidden[at, :]
             keep = row((BLOCK, 1)) + i * BLOCK < len_ref[0]
             block[at, :] = jnp.where(keep, h + acc[at, :], 0.0).astype(BF)
@@ -535,26 +581,24 @@
             gh = low[at, :].astype(F32) + norm_back(xhat, inv, gain_ref[...] * back[at, :])
             hidden[at, :] = gh
             gatt[at, :] = dot_nt(gh.astype(BF), wproj[...]).astype(BF)
-            here = [
-                pltpu.make_async_copy(block.at[at, :], block_ref.at[at, :], wsem),
-                pltpu.make_async_copy(hidden.at[at, :], gh_ref.at[at, :], wsem),
-                pltpu.make_async_copy(gatt.at[at, :], ga_ref.at[at, :], wsem),
-            ]
-            for c in here:
+            for c in out_copies(i):
                 c.start()
-            sent += here
-        for c in sent:
-            c.wait()
+            return carry
+
+        lax.fori_loop(0, size // BLOCK, finish, 0)
+        for i in range(size // BLOCK):
+            for c in out_copies(i):
+                c.wait()
 
 
 def fall(lengths, index, projs, col, fcs, outs, pre, hidden, cot, gain):
     size, width = cot.shape
-    units = pre.shape[1]
-    steps = units // FF_STEP
+    steps = pre.shape[0]
+    flat = [w for half in fcs + outs for w in half]
     return pl.pallas_call(
-        functools.partial(fall_kernel, len(projs), col, steps),
+        functools.partial(fall_kernel, len(projs), (len(fcs), len(outs)), col, steps),
         grid=(steps,),
-        in_specs=[SMEM, SMEM] + [ANY] * (3 * len(projs) + 3) + [whole((1, width))],
+        in_specs=[SMEM, SMEM] + [ANY] * (len(projs) + len(flat) + 3) + [whole((1, width))],
         out_specs=[ANY] * 3,
         out_shape=[
             jax.ShapeDtypeStruct((size, width), BF),
@@ -575,12 +619,13 @@
             pltpu.VMEM((size, width), BF),
             pltpu.SemaphoreType.DMA((2,)),
             pltpu.SemaphoreType.DMA((2,)),
+            pltpu.SemaphoreType.DMA((2,)),
             pltpu.SemaphoreType.DMA,
         ],
         compiler_params=params(),
         cost_estimate=CHEAP,
         name="fall",
-    )(lengths, index, *projs, *fcs, *outs, pre, hidden, cot, gain)
+    )(lengths, index, *projs, *flat, pre, hidden, cot, gain)
 
 
 def backward_kernel(
@@ -650,9 +695,10 @@
     dq_ref[...] = dq
     dv = dv_ref[...]
     narrow = narrow_ref[...]
-    part = dot_nt(upq_ref[...], dq) + dot_nt(upv_ref[...], dv)
-    gq = SCALE * dot(narrow, dq)[:8]
-    gv = SCALE * dot(narrow, dv)[:8]
+    both = jnp.concatenate([dq, dv], axis=1)
+    part = dot_nt(jnp.concatenate([upq_ref[...], upv_ref[...]], axis=1), both)
+    ups = SCALE * dot(narrow, both)[:8]
+    gq, gv = ups[:, :PAIR], ups[:, PAIR:]
     cols = pl.ds(pl.multiple_of(step * PAIR, PAIR), PAIR)
     sums_ref[8:16, cols] = jnp.where(row((8, PAIR)) < 4, gq, gv)
 
@@ -775,13 +821,22 @@
     def sibling(self, value):
         return swap(value, lambda i: i ^ 1, self.total)
 
-    def first(self, value):
-        return swap(value, lambda i: i ^ (2 if self.even(i) else 4), self.total)
-
-    def second(self, value):
-        b = swap(value, lambda i: i ^ (4 if self.even(i) else 2), self.total)
+    def first(self, value, turned=False):
+        return swap(value, lambda i: i ^ (2 if self.even(i) != turned else 4), self.total)
+
+    def second(self, value, turned=False):
+        b = swap(value, lambda i: i ^ (4 if self.even(i) != turned else 2), self.total)
         c = swap(value, lambda i: i ^ self.fsdp, self.total)
         return b, c
+
+    def all(self, own, a, b, c, turned=False):
+        found = []
+        for pair in (own, c, b, a) if turned else (own, a, b, c):
+            found += pair
+        return found
+
+    def pair(self, value):
+        return [value, self.sibling(value)]
 
     def index(self):
         here = lax.axis_index("fsdp").astype(jnp.int32)
@@ -790,22 +845,19 @@
         return jnp.stack([here ^ (m ^ s) for m in (0, a, 6, c) for s in (0, 1)])
 
 
-def all_sum(value, total):
-    if total & (total - 1):
-        return lax.psum(value, BOTH)
-    half = value.shape[0] // 2
-    odd = lax.axis_index("fsdp") % 2
-    mine = lax.dynamic_slice_in_dim(value, odd * half, half)
-    other = lax.dynamic_slice_in_dim(value, (1 - odd) * half, half)
-    mine = mine + swap(other, lambda i: i ^ 1, total)
-    bit = 2
-    while bit < total:
-        mine = mine + swap(mine, lambda i, bit=bit: i ^ bit, total)
-        bit *= 2
-    other = swap(mine, lambda i: i ^ 1, total)
-    top = jnp.where(odd == 0, mine, other)
-    low = jnp.where(odd == 0, other, mine)
-    return jnp.concatenate([top, low], axis=0)
+def sum_rounds(total):
+    bits = [1 << i for i in range(1, total.bit_length() - 1)]
+    return [[1]] + [bits[i : i + 2] for i in range(0, len(bits), 2)]
+
+
+def sum_round(value, bits, total):
+    if len(bits) == 1:
+        return value + swap(value, lambda i: i ^ bits[0], total)
+    low, high = bits
+    a = swap(value, lambda i: i ^ low, total)
+    b = swap(value, lambda i: i ^ high, total)
+    c = swap(value, lambda i: i ^ (low | high), total)
+    return (value + a) + (b + c)
 
 
 def local(
@@ -831,36 +883,41 @@
         cube = Cube(total, fsdp)
         index = cube.index()
         a0, a1, af, ao = [cube.first(w) for w in (w0, w1, w_fc, w_out)]
-        s0, s1, sf, so = [cube.sibling(w) for w in (w0, w1, w_fc, w_out)]
+        own0, own1, ownf, owno = [cube.pair(w) for w in (w0, w1, w_fc, w_out)]
         n, narrow, down, upq, upv = norm_one(*small)
         attend = functools.partial(
-            attention_forward, lengths, index, n=n, narrow=narrow, upq=upq, upv=upv
+            attention_forward, lengths, index, narrow=narrow, upq=upq, upv=upv
         )
         a0 = after(a0, n)
         b0, c0 = cube.second(a0)
-        first = [w0, s0] + [p for t in (a0, b0, c0) for p in (t, cube.sibling(t))]
-        kept = attend(first, quads=low[:1], here=0, kept=[])
+        first = cube.all(own0, *map(cube.pair, (a0, b0, c0)))
+        b1, c1 = cube.second(a1)
+        n1 = after(n, a1)
+        kept = attend(first, n=n1, quads=low[:1], here=0, kept=[])
+        kept = attend(first, n=n1, quads=low[1:], here=1, kept=kept)
         a1 = after(a1, kept[0])
-        b1, c1 = cube.second(a1)
-        kept = attend(first, quads=low[1:], here=1, kept=kept)
         b1, c1 = after(b1, kept[0]), after(c1, kept[0])
-        second = [w1, s1] + [p for t in (a1, b1, c1) for p in (t, cube.sibling(t))]
+        second = cube.all(own1, *map(cube.pair, (a1, b1, c1)))
         af = after(af, kept[0])
         bf, cf = cube.second(af)
-        kept = attend(second, quads=low, here=half, kept=kept)
+        n2 = after(n, af)
+        kept = attend(second, n=n2, quads=low, here=half, kept=kept)
+        af = after(af, kept[0])
         bf, cf = after(bf, kept[0]), after(cf, kept[0])
-        fcs = [w_fc, sf] + [p for t in (af, bf, cf) for p in (t, cube.sibling(t))]
+        fcs = [cube.all(ownf, *map(cube.pair, (af, bf, cf)))]
         ao = after(ao, kept[0])
         bo, co = cube.second(ao)
         o, qx, q, k, v = kept
-        pre, hidden = rise(index, second, col, fcs, o, x, gain_two[None], shift_two[None])
-        bo, co = after(bo, hidden), after(co, hidden)
-        outs = [w_out, so] + [p for t in (ao, bo, co) for p in (t, cube.sibling(t))]
+        o_late = after(o, ao)
+        pre, hidden = rise(index, second, col, fcs, o_late, x, gain_two[None], shift_two[None])
+        ao, bo, co = after(ao, hidden), after(bo, hidden), after(co, hidden)
+        outs = [cube.all(owno, *map(cube.pair, (ao, bo, co)))]
     else:
         index = jnp.zeros((1,), jnp.int32)
         first, second, fcs, outs = [
             [lax.all_gather(w, "fsdp", axis=0, tiled=True)] for w in (w0, w1, w_fc, w_out)
         ]
+        fcs, outs = [fcs], [outs]
         n, narrow, down, upq, upv = norm_one(*small)
         kept = attention_forward(lengths, index, first, n, narrow, upq, upv, low, 0, [])
         kept = attention_forward(lengths, index, second, n, narrow, upq, upv, low, half, kept)
@@ -872,11 +929,15 @@
     dq, dk, dv, joint, sums = attention_backward(
         lengths, qx, q, k, v, o, ga, upq, upv, narrow, n
     )
-    sums = all_sum(sums, total)
-    grad = token_gradient(
-        index, [first, second], (half, quads - half), dq, dk, dv, joint, down, gh, x,
-        gain_one[None],
-    )
+    args = (dq, dk, dv, joint, down, gh, x, gain_one[None])
+    shards, quads = [first, second], (half, quads - half)
+    if total & (total - 1):
+        sums = lax.psum(sums, BOTH)
+        grad = token_gradient(index, shards, quads, *args)
+    else:
+        for bits in sum_rounds(total):
+            sums = sum_round(sums, bits, total)
+        grad = token_gradient(index, shards, quads, *args)
     return (
         block_out.reshape(tokens.shape),
         grad.reshape(tokens.shape),

time: 240 us -> 223 us (0.929)
  waiting for transfers between devices: 34.3 us -> 21.4 us
  Pallas kernels: 164 us -> 156 us
  starting transfers between devices: 32.1 us -> 37.3 us
    ppermute x34 -> x35, waiting for transfers between devices: 34.3 us -> 21.4 us  [swap(): return lax.ppermute(value, BOTH, [(i, fn(i)) for i in range(total)])]
    pallas_call x2, Pallas kernels: 71.9 us -> 64.6 us  [the longest x1 44 us: fall(): pl.pallas_call(functools.partial(fall_kernel, len(projs), (len(fcs), len(...]
    ppermute x34 -> x35, starting transfers between devices: 32.1 us -> 37.3 us  [swap(): return lax.ppermute(value, BOTH, [(i, fn(i)) for i in range(total)])]
  transfers between devices with their start and end apart: 34 -> 35, of which waited for: 15 -> 12; matrix products, arithmetic and copies ran while one was open for 0% -> 0% of each run, Pallas kernels for 31% -> 34%
where the time goes in v4:
time: 223 us; the launch traced here: 221 us
  Pallas kernels  156 us (70%)
  starting transfers between devices  37.3 us (17%)
  waiting for transfers between devices  21.4 us (10%)
  local copies, waits for them, and re-layouts  4.09 us (2%)
    pallas_call x1, Pallas kernels, fall(): pl.pallas_call(functools.partial(fall_kernel, len(projs), (len(fcs), len(...  44 us
    ppermute x35, starting transfers between devices, swap(): return lax.ppermute(value, BOTH, [(i, fn(i)) for i in range(total)])  37.3 us
    pallas_call x1, Pallas kernels, attention_backward(): pl.pallas_call(backward_kernel, grid=(width // PAIR,), in_specs=[SMEM, pl...  35.4 us
    pallas_call x3, Pallas kernels, attention_forward(): pl.pallas_call(functools.partial(forward_kernel, len(shards), len(kept),...  34.5 us
    ppermute x35, waiting for transfers between devices, swap(): return lax.ppermute(value, BOTH, [(i, fn(i)) for i in range(total)])  21.4 us
    pallas_call x1, Pallas kernels, rise(): pl.pallas_call(functools.partial(rise_kernel, len(projs), len(fcs), col),...  20.6 us
    pallas_call x1, Pallas kernels, token_gradient(): pl.pallas_call(functools.partial(token_kernel, [len(p) for p in shards],...  14.8 us
    pallas_call x1, Pallas kernels, norm_one(): pl.pallas_call(norm_one_kernel, grid=(length // BLOCK,), in_specs=[pl.Blo...  4.53 us
  transfers between devices with their start and end apart: 35, of which 12 were waited for; matrix products, arithmetic and copies ran while one was open for 0% of the time, Pallas kernels for 34%

profile of v4, /device:TPU:1, one launch (start us, length us, event | category | flops | bytes accessed | tf_op | source)
XLA Modules:
  0.0 221.2 jit_solution(2346696804502798931)
XLA Ops:
  0.6 2.3 %repack.1 = (bf16[128,1536]{1,0:T(8,128)(2,1)}, bf16[128,2560]{1,0:T(8,128)(2,1)}) custom-call(bf16[128,3072]{1,0:T(8,128)(2,1)} %qkv_ref.1, bf16[128,1024]{1,0:T(8,128)(2,1)} %proj_ref.1), custom_call_target="tpu_custom_call" | custom-call | tf_op jit(solution)/shard_map/repack/pallas_call | solution.py:143
  2.9 2.0 collective-permute-start.3
  5.9 4.5 %norm_one.1 = (bf16[1024,1024]{1,0:T(8,128)(2,1)}, bf16[16,1024]{1,0:T(8,128)(2,1)}, bf16[16,1024]{1,0:T(8,128)(2,1)}, bf16[16,1024]{1,0:T(8,128)(2,1)}, bf16[16,1024]{1,0:T(8,128)(2,1)}) custom-call(bf16[1024,1024]{1,0:T(8,128)(2,1)} %bitcast.22, f32[1,1024]{1,0:T(1,128)} %bitcast.31, f32[1,1024]{1,0:T(1,128)} %bitcast.33, f32[4,1024]{1,0:T(4,128)} %bitcast.27, ...), custom_call_target="tpu_custom_call" | custom-call | tf_op jit(solution)/shard_map/norm_one/pallas_call | solution.py:110
  10.5 3.5 %collective-permute-done.3.refs_2_ = bf16[128,1536]{1,0:T(8,128)(2,1)S(1)} collective-permute-done((bf16[128,1536]{1,0:T(8,128)(2,1)}, bf16[128,1536]{1,0:T(8,128)(2,1)S(1)}, u32[]{:S(2)}, u32[]{:S(2)}) %collective-permute-start.3) | collective-permute-done | bytes 393248 | tf_op jit(solution)/shard_map/ppermute | solution.py:807
  14.0 1.2 collective-permute-start.7
  15.2 1.2 collective-permute-start.5
  16.5 1.2 collective-permute-start.15
  17.7 3.5 %collective-permute-start.4 = (bf16[128,1536]{1,0:T(8,128)(2,1)S(1)}, bf16[128,1536]{1,0:T(8,128)(2,1)}, u32[]{:S(2)}, u32[]{:S(2)}) collective-permute-start(bf16[128,1536]{1,0:T(8,128)(2,1)S(1)} %collective-permute-done.3.refs_2_), channel_id=1, source_target_pairs={{0,1},{1,0},{2,3},{3,2},{4,5},{5,4},{6,7},{7,6},{8,9},{9,8},{10,11... | collective-permute-start | bytes 1179656 | tf_op jit(solution)/shard_map/ppermute | solution.py:807
  21.2 1.3 collective-permute-done.7.refs_6_
  22.5 3.1 %collective-permute-start.8 = (bf16[128,1536]{1,0:T(8,128)(2,1)}, bf16[128,1536]{1,0:T(8,128)(2,1)}, u32[]{:S(2)}, u32[]{:S(2)}) collective-permute-start(bf16[128,1536]{1,0:T(8,128)(2,1)} %collective-permute-done.7.refs_6_), channel_id=1, source_target_pairs={{0,1},{1,0},{2,3},{3,2},{4,5},{5,4},{6,7},{7,6},{8,9},{9,8},{10,11... | collective-permute-start | bytes 1179656 | tf_op jit(solution)/shard_map/ppermute | solution.py:807
  25.6 1.2 collective-permute-start.6
  30.5 3.0 %collective-permute-start = (bf16[128,2560]{1,0:T(8,128)(2,1)S(1)}, bf16[128,2560]{1,0:T(8,128)(2,1)S(1)}, u32[]{:S(2)}, u32[]{:S(2)}) collective-permute-start(bf16[128,2560]{1,0:T(8,128)(2,1)S(1)} %copy-done), channel_id=1, source_target_pairs={{0,1},{1,0},{2,3},{3,2},{4,5},{5,4},{6,7},{7,6},{8,9},{9,8},{10,11... | collective-permute-start | bytes 1966088 | tf_op jit(solution)/shard_map/ppermute | solution.py:807
  33.5 1.3 collective-permute-start.12
  34.7 9.6 %attention_forward.3 = (bf16[1024,1024]{1,0:T(8,128)(2,1)}, bf16[2048,1024]{1,0:T(8,128)(2,1)}, bf16[1024,1024]{1,0:T(8,128)(2,1)}, bf16[1024,1024]{1,0:T(8,128)(2,1)}, bf16[1024,1024]{1,0:T(8,128)(2,1)}) custom-call(s32[1]{0:T(128)S(6)} %copy.41.len_ref, s32[8]{0:T(128)} %stack.35.index_ref, bf16[128,1536]{1,0:T(8,128)(2,1)} %get-tuple-element.54.refs_0_, ...), custom_call_target="tpu_custom_call" | custom-call | flops 1000 | bytes 1000 | tf_op jit(solution)/shard_map/attention_forward/pallas_call | solution.py:288
  44.3 9.7 %attention_forward.4 = (bf16[1024,1024]{1,0:T(8,128)(2,1)}, bf16[2048,1024]{1,0:T(8,128)(2,1)}, bf16[1024,1024]{1,0:T(8,128)(2,1)}, bf16[1024,1024]{1,0:T(8,128)(2,1)}, bf16[1024,1024]{1,0:T(8,128)(2,1)}) custom-call(s32[1]{0:T(128)S(6)} %copy.41.len_ref, ...), custom_call_target="tpu_custom_call", output_to_operand_aliasing={{0}: (10, {}), {1}: (11, {}), {2}: (12, {}), {3}: (13, {}),... | custom-call | flops 1000 | bytes 1000 | tf_op jit(solution)/shard_map/attention_forward/pallas_call | solution.py:288
  57.5 3.1 %collective-permute-done.13.refs_7_.refs_15_ = bf16[128,2560]{1,0:T(8,128)(2,1)S(1)} collective-permute-done((bf16[128,2560]{1,0:T(8,128)(2,1)S(1)}, bf16[128,2560]{1,0:T(8,128)(2,1)S(1)}, u32[]{:S(2)}, u32[]{:S(2)}) %collective-permute-start.13) | collective-permute-done | bytes 655392 | tf_op jit(solution)/shard_map/ppermute | solution.py:807
  61.6 15.2 %attention_forward.5 = (bf16[1024,1024]{1,0:T(8,128)(2,1)}, bf16[2048,1024]{1,0:T(8,128)(2,1)}, bf16[1024,1024]{1,0:T(8,128)(2,1)}, bf16[1024,1024]{1,0:T(8,128)(2,1)}, bf16[1024,1024]{1,0:T(8,128)(2,1)}) custom-call(s32[1]{0:T(128)S(6)} %copy.41.len_ref, ...), custom_call_target="tpu_custom_call", output_to_operand_aliasing={{0}: (10, {}), {1}: (11, {}), {2}: (12, {}), {3}: (13, {}),... | custom-call | flops 1000 | bytes 1000 | tf_op jit(solution)/shard_map/attention_forward/pallas_call | solution.py:288
  77.2 2.1 collective-permute-done.19.refs_14_
  80.7 1.3 collective-permute-start.26
  82.0 1.2 collective-permute-start.24
  85.5 20.6 %rise.1 = (f32[4,1024,1024]{2,1,0:T(8,128)}, f32[1024,1024]{1,0:T(8,128)}) custom-call(s32[8]{0:T(128)} %stack.35.index_ref, bf16[128,2560]{1,0:T(8,128)(2,1)} %get-tuple-element.53.refs_0_.refs_8_, bf16[128,2560]{1,0:T(8,128)(2,1)} %copy-done.3, bf16[128,2560]{1,0:T(8,128)(2,1)} %copy-done.1, bf16[128,2560]{1,0:T(8,128)(2,1)} %copy-done.5, ...), custom_call_target="tpu_custom_call" | custom-call | flops 1000 | bytes 1000 | tf_op jit(solution)/shard_map/rise/pallas_call | solution.py:450
  106.4 1.4 collective-permute-start.23
  108.3 3.4 %collective-permute-done.23.refs_19_ = bf16[512,1024]{1,0:T(8,128)(2,1)S(1)} collective-permute-done((bf16[512,1024]{1,0:T(8,128)(2,1)}, bf16[512,1024]{1,0:T(8,128)(2,1)S(1)}, u32[]{:S(2)}, u32[]{:S(2)}) %collective-permute-start.23) | collective-permute-done | bytes 1048608 | tf_op jit(solution)/shard_map/ppermute | solution.py:807
  111.7 1.3 collective-permute-done.27.refs_23_
  114.0 44.0 %fall.1 = (bf16[1024,1024]{1,0:T(8,128)(2,1)}, f32[1024,1024]{1,0:T(8,128)}, bf16[1024,1024]{1,0:T(8,128)(2,1)}) custom-call(s32[1]{0:T(128)S(6)} %copy.41.len_ref, s32[8]{0:T(128)} %stack.35.index_ref, bf16[128,2560]{1,0:T(8,128)(2,1)} %get-tuple-element.53.refs_0_.refs_8_, bf16[128,2560]{1,0:T(8,128)(2,1)} %copy-done.3, bf16[128,2560]{1,0:T(8,128)(2,1)} %copy-done.1, ...), custom_call_target="tpu_custom_call" | custom-call | flops 1000 | bytes 1000 | tf_op jit(solution)/shard_map/fall/pallas_call | solution.py:598
  158.0 35.4 %attention_backward.1 = (bf16[1024,1024]{1,0:T(8,128)(2,1)}, bf16[1024,1024]{1,0:T(8,128)(2,1)}, bf16[1024,1024]{1,0:T(8,128)(2,1)}, bf16[16,1024]{1,0:T(8,128)(2,1)}, f32[16,1024]{1,0:T(8,128)}) custom-call(s32[1]{0:T(128)S(6)} %copy.41.len_ref, bf16[2048,1024]{1,0:T(8,128)(2,1)} %get-tuple-element.88.qx_ref, bf16[1024,1024]{1,0:T(8,128)(2,1)} %get-tuple-element.89.q_ref, ...), custom_call_target="tpu_custom_call" | custom-call | flops 1000 | bytes 1000 | tf_op jit(solution)/shard_map/attention_backward/pallas_call | solution.py:724
  195.8 1.3 collective-permute-start.31
  197.3 1.2 collective-permute-start.29
  198.5 1.4 collective-permute-done.31
  199.9 2.2 collective-permute-done.30
  202.2 2.3 %collective-permute-start.34 = (f32[16,1024]{1,0:T(8,128)S(1)}, f32[16,1024]{1,0:T(8,128)S(1)}, u32[]{:S(2)}, u32[]{:S(2)}) collective-permute-start(f32[16,1024]{1,0:T(8,128)S(1)} %add_add_fusion.1), channel_id=1, source_target_pairs={{0,24},{1,25},{2,26},{3,27},{4,28},{5,29},{6,30},{7,31},{8,16},{9,... | collective-permute-start | bytes 196616 | tf_op jit(solution)/shard_map/ppermute | solution.py:807
  205.8 14.8 %token_gradient.1 = bf16[1024,1024]{1,0:T(8,128)(2,1)} custom-call(s32[8]{0:T(128)} %stack.35.index_ref, bf16[128,1536]{1,0:T(8,128)(2,1)} %get-tuple-element.54.refs_0_, bf16[128,1536]{1,0:T(8,128)(2,1)} %copy-done.13, bf16[128,1536]{1,0:T(8,128)(2,1)} %copy-done.12, bf16[128,1536]{1,0:T(8,128)(2,1)} %collective-permute-done.4.refs_3_, ...), custom_call_target="tpu_custom_call" | custom-call | flops 1000 | bytes 1000 | tf_op jit(solution)/shard_map/token_gradient/pallas_call | solution.py:783
  (90 shorter events, 18.8 us)
Async XLA Ops:
  2.9 11.1 %collective-permute-start.3 = (bf16[128,1536]{1,0:T(8,128)(2,1)}, bf16[128,1536]{1,0:T(8,128)(2,1)S(1)}, u32[]{:S(2)}, u32[]{:S(2)}) collective-permute-start(bf16[128,1536]{1,0:T(8,128)(2,1)} %get-tuple-element.54.refs_0_), channel_id=1, source_target_pairs={{0,2},{1,3},{2,0},{3,1},{4,6},{5,7},{6,4},{7,5},{8,12},{9,13},{10,... | collective-permute-start | bytes 1179656 | tf_op jit(solution)/shard_map/ppermute | solution.py:807
  5.0 23.1 %collective-permute-start.1 = (bf16[128,2560]{1,0:T(8,128)(2,1)}, bf16[128,2560]{1,0:T(8,128)(2,1)S(1)}, u32[]{:S(2)}, u32[]{:S(2)}) collective-permute-start(bf16[128,2560]{1,0:T(8,128)(2,1)} %get-tuple-element.53.refs_0_.refs_8_), channel_id=1, source_target_pairs={{0,2},{1,3},{2,0},{3,1},{4,6},{5,7},{6,4},{7,5},{8,12},{9,13},{10,... | collective-permute-start | bytes 1966088 | tf_op jit(solution)/shard_map/ppermute | solution.py:807
  5.0 12.7 %collective-permute-start.2 = (bf16[128,1536]{1,0:T(8,128)(2,1)}, bf16[128,1536]{1,0:T(8,128)(2,1)S(1)}, u32[]{:S(2)}, u32[]{:S(2)}) collective-permute-start(bf16[128,1536]{1,0:T(8,128)(2,1)} %get-tuple-element.54.refs_0_), channel_id=1, source_target_pairs={{0,1},{1,0},{2,3},{3,2},{4,5},{5,4},{6,7},{7,6},{8,9},{9,8},{10,11... | collective-permute-start | bytes 1179656 | tf_op jit(solution)/shard_map/ppermute | solution.py:807
  14.0 8.5 %collective-permute-start.7 = (bf16[128,1536]{1,0:T(8,128)(2,1)S(1)}, bf16[128,1536]{1,0:T(8,128)(2,1)}, u32[]{:S(2)}, u32[]{:S(2)}) collective-permute-start(bf16[128,1536]{1,0:T(8,128)(2,1)S(1)} %collective-permute-done.3.refs_2_), channel_id=1, source_target_pairs={{0,8},{1,9},{2,10},{3,11},{4,12},{5,13},{6,14},{7,15},{8,0},{9,1},... | collective-permute-start | bytes 1179656 | tf_op jit(solution)/shard_map/ppermute | solution.py:807
  15.2 10.4 %collective-permute-start.5 = (bf16[128,1536]{1,0:T(8,128)(2,1)S(1)}, bf16[128,1536]{1,0:T(8,128)(2,1)}, u32[]{:S(2)}, u32[]{:S(2)}) collective-permute-start(bf16[128,1536]{1,0:T(8,128)(2,1)S(1)} %collective-permute-done.3.refs_2_), channel_id=1, source_target_pairs={{0,4},{1,5},{2,6},{3,7},{4,0},{5,1},{6,2},{7,3},{8,10},{9,11},{10,... | collective-permute-start | bytes 1179656 | tf_op jit(solution)/shard_map/ppermute | solution.py:807
  16.5 38.1 %collective-permute-start.15 = (bf16[128,4096]{1,0:T(8,128)(2,1)S(1)}, bf16[128,4096]{1,0:T(8,128)(2,1)}, u32[]{:S(2)}, u32[]{:S(2)}) collective-permute-start(bf16[128,4096]{1,0:T(8,128)(2,1)S(1)} %copy-done.8), channel_id=1, source_target_pairs={{0,2},{1,3},{2,0},{3,1},{4,6},{5,7},{6,4},{7,5},{8,12},{9,13},{10,... | collective-permute-start | bytes 3145736 | tf_op jit(solution)/shard_map/ppermute | solution.py:807
  17.7 12.8 %collective-permute-start.4 = (bf16[128,1536]{1,0:T(8,128)(2,1)S(1)}, bf16[128,1536]{1,0:T(8,128)(2,1)}, u32[]{:S(2)}, u32[]{:S(2)}) collective-permute-start(bf16[128,1536]{1,0:T(8,128)(2,1)S(1)} %collective-permute-done.3.refs_2_), channel_id=1, source_target_pairs={{0,1},{1,0},{2,3},{3,2},{4,5},{5,4},{6,7},{7,6},{8,9},{9,8},{10,11... | collective-permute-start | bytes 1179656 | tf_op jit(solution)/shard_map/ppermute | solution.py:807
  22.5 10.9 %collective-permute-start.8 = (bf16[128,1536]{1,0:T(8,128)(2,1)}, bf16[128,1536]{1,0:T(8,128)(2,1)}, u32[]{:S(2)}, u32[]{:S(2)}) collective-permute-start(bf16[128,1536]{1,0:T(8,128)(2,1)} %collective-permute-done.7.refs_6_), channel_id=1, source_target_pairs={{0,1},{1,0},{2,3},{3,2},{4,5},{5,4},{6,7},{7,6},{8,9},{9,8},{10,11... | collective-permute-start | bytes 1179656 | tf_op jit(solution)/shard_map/ppermute | solution.py:807
  25.6 9.1 %collective-permute-start.6 = (bf16[128,1536]{1,0:T(8,128)(2,1)}, bf16[128,1536]{1,0:T(8,128)(2,1)}, u32[]{:S(2)}, u32[]{:S(2)}) collective-permute-start(bf16[128,1536]{1,0:T(8,128)(2,1)} %collective-permute-done.5.refs_4_), channel_id=1, source_target_pairs={{0,1},{1,0},{2,3},{3,2},{4,5},{5,4},{6,7},{7,6},{8,9},{9,8},{10,11... | collective-permute-start | bytes 1179656 | tf_op jit(solution)/shard_map/ppermute | solution.py:807
  28.0 26.4 %collective-permute-start.10 = (bf16[128,2560]{1,0:T(8,128)(2,1)S(1)}, bf16[128,2560]{1,0:T(8,128)(2,1)S(1)}, u32[]{:S(2)}, u32[]{:S(2)}) collective-permute-start(bf16[128,2560]{1,0:T(8,128)(2,1)S(1)} %collective-permute-done.1.refs_2_.refs_10_), channel_id=1, source_target_pairs={{0,4},{1,5},{2,6},{3,7},{4,0},{5,1},{6,2},{7,3},{8,10},{9,11},{10,... | collective-permute-start | bytes 1966088 | tf_op jit(solution)/shard_map/ppermute | solution.py:807
  30.5 24.3 %collective-permute-start = (bf16[128,2560]{1,0:T(8,128)(2,1)S(1)}, bf16[128,2560]{1,0:T(8,128)(2,1)S(1)}, u32[]{:S(2)}, u32[]{:S(2)}) collective-permute-start(bf16[128,2560]{1,0:T(8,128)(2,1)S(1)} %copy-done), channel_id=1, source_target_pairs={{0,1},{1,0},{2,3},{3,2},{4,5},{5,4},{6,7},{7,6},{8,9},{9,8},{10,11... | collective-permute-start | bytes 1966088 | tf_op jit(solution)/shard_map/ppermute | solution.py:807
  33.5 22.5 %collective-permute-start.12 = (bf16[128,2560]{1,0:T(8,128)(2,1)S(1)}, bf16[128,2560]{1,0:T(8,128)(2,1)S(1)}, u32[]{:S(2)}, u32[]{:S(2)}) collective-permute-start(bf16[128,2560]{1,0:T(8,128)(2,1)S(1)} %collective-permute-done.1.refs_2_.refs_10_), channel_id=1, source_target_pairs={{0,8},{1,9},{2,10},{3,11},{4,12},{5,13},{6,14},{7,15},{8,0},{9,1},... | collective-permute-start | bytes 1966088 | tf_op jit(solution)/shard_map/ppermute | solution.py:807
  54.6 24.7 %collective-permute-start.19 = (bf16[128,4096]{1,0:T(8,128)(2,1)}, bf16[128,4096]{1,0:T(8,128)(2,1)}, u32[]{:S(2)}, u32[]{:S(2)}) collective-permute-start(bf16[128,4096]{1,0:T(8,128)(2,1)} %collective-permute-done.15.refs_10_), channel_id=1, source_target_pairs={{0,8},{1,9},{2,10},{3,11},{4,12},{5,13},{6,14},{7,15},{8,0},{9,1},... | collective-permute-start | bytes 3145736 | tf_op jit(solution)/shard_map/ppermute | solution.py:807
  54.8 25.7 %collective-permute-start.17 = (bf16[128,4096]{1,0:T(8,128)(2,1)}, bf16[128,4096]{1,0:T(8,128)(2,1)}, u32[]{:S(2)}, u32[]{:S(2)}) collective-permute-start(bf16[128,4096]{1,0:T(8,128)(2,1)} %collective-permute-done.15.refs_10_), channel_id=1, source_target_pairs={{0,4},{1,5},{2,6},{3,7},{4,0},{5,1},{6,2},{7,3},{8,10},{9,11},{10,... | collective-permute-start | bytes 3145736 | tf_op jit(solution)/shard_map/ppermute | solution.py:807
  56.0 24.8 %collective-permute-start.22 = (bf16[512,1024]{1,0:T(8,128)(2,1)}, bf16[512,1024]{1,0:T(8,128)(2,1)}, u32[]{:S(2)}, u32[]{:S(2)}) collective-permute-start(bf16[512,1024]{1,0:T(8,128)(2,1)} %refs_16_.1), channel_id=1, source_target_pairs={{0,2},{1,3},{2,0},{3,1},{4,6},{5,7},{6,4},{7,5},{8,12},{9,13},{10,... | collective-permute-start | bytes 3145736 | tf_op jit(solution)/shard_map/ppermute | solution.py:807
  56.3 25.7 %collective-permute-start.14 = (bf16[128,4096]{1,0:T(8,128)(2,1)S(1)}, bf16[128,4096]{1,0:T(8,128)(2,1)}, u32[]{:S(2)}, u32[]{:S(2)}) collective-permute-start(bf16[128,4096]{1,0:T(8,128)(2,1)S(1)} %copy-done.8), channel_id=1, source_target_pairs={{0,1},{1,0},{2,3},{3,2},{4,5},{5,4},{6,7},{7,6},{8,9},{9,8},{10,11... | collective-permute-start | bytes 3145736 | tf_op jit(solution)/shard_map/ppermute | solution.py:807
  57.5 3.2 %collective-permute-start.13 = (bf16[128,2560]{1,0:T(8,128)(2,1)S(1)}, bf16[128,2560]{1,0:T(8,128)(2,1)S(1)}, u32[]{:S(2)}, u32[]{:S(2)}) collective-permute-start(bf16[128,2560]{1,0:T(8,128)(2,1)S(1)} %collective-permute-done.12.refs_6_.refs_14_), channel_id=1, source_target_pairs={{0,1},{1,0},{2,3},{3,2},{4,5},{5,4},{6,7},{7,6},{8,9},{9,8},{10,11... | collective-permute-start | bytes 1966088 | tf_op jit(solution)/shard_map/ppermute | solution.py:807
  76.8 6.4 %collective-permute-start.16 = (bf16[128,4096]{1,0:T(8,128)(2,1)}, bf16[128,4096]{1,0:T(8,128)(2,1)S(1)}, u32[]{:S(2)}, u32[]{:S(2)}) collective-permute-start(bf16[128,4096]{1,0:T(8,128)(2,1)} %collective-permute-done.15.refs_10_), channel_id=1, source_target_pairs={{0,1},{1,0},{2,3},{3,2},{4,5},{5,4},{6,7},{7,6},{8,9},{9,8},{10,11... | collective-permute-start | bytes 3145736 | tf_op jit(solution)/shard_map/ppermute | solution.py:807
  79.3 4.7 %collective-permute-start.20 = (bf16[128,4096]{1,0:T(8,128)(2,1)}, bf16[128,4096]{1,0:T(8,128)(2,1)S(1)}, u32[]{:S(2)}, u32[]{:S(2)}) collective-permute-start(bf16[128,4096]{1,0:T(8,128)(2,1)} %collective-permute-done.19.refs_14_), channel_id=1, source_target_pairs={{0,1},{1,0},{2,3},{3,2},{4,5},{5,4},{6,7},{7,6},{8,9},{9,8},{10,11... | collective-permute-start | bytes 3145736 | tf_op jit(solution)/shard_map/ppermute | solution.py:807
  80.5 4.0 %collective-permute-start.18 = (bf16[128,4096]{1,0:T(8,128)(2,1)}, bf16[128,4096]{1,0:T(8,128)(2,1)S(1)}, u32[]{:S(2)}, u32[]{:S(2)}) collective-permute-start(bf16[128,4096]{1,0:T(8,128)(2,1)} %collective-permute-done.17.refs_12_), channel_id=1, source_target_pairs={{0,1},{1,0},{2,3},{3,2},{4,5},{5,4},{6,7},{7,6},{8,9},{9,8},{10,11... | collective-permute-start | bytes 3145736 | tf_op jit(solution)/shard_map/ppermute | solution.py:807
  80.7 25.4 %collective-permute-start.26 = (bf16[512,1024]{1,0:T(8,128)(2,1)}, bf16[512,1024]{1,0:T(8,128)(2,1)S(1)}, u32[]{:S(2)}, u32[]{:S(2)}) collective-permute-start(bf16[512,1024]{1,0:T(8,128)(2,1)} %collective-permute-done.22.refs_18_), channel_id=1, source_target_pairs={{0,8},{1,9},{2,10},{3,11},{4,12},{5,13},{6,14},{7,15},{8,0},{9,1},... | collective-permute-start | bytes 3145736 | tf_op jit(solution)/shard_map/ppermute | solution.py:807
  82.0 24.4 %collective-permute-start.24 = (bf16[512,1024]{1,0:T(8,128)(2,1)}, bf16[512,1024]{1,0:T(8,128)(2,1)S(1)}, u32[]{:S(2)}, u32[]{:S(2)}) collective-permute-start(bf16[512,1024]{1,0:T(8,128)(2,1)} %collective-permute-done.22.refs_18_), channel_id=1, source_target_pairs={{0,4},{1,5},{2,6},{3,7},{4,0},{5,1},{6,2},{7,3},{8,10},{9,11},{10,... | collective-permute-start | bytes 3145736 | tf_op jit(solution)/shard_map/ppermute | solution.py:807
  83.2 25.1 %collective-permute-start.21 = (bf16[512,1024]{1,0:T(8,128)(2,1)}, bf16[512,1024]{1,0:T(8,128)(2,1)}, u32[]{:S(2)}, u32[]{:S(2)}) collective-permute-start(bf16[512,1024]{1,0:T(8,128)(2,1)} %refs_16_.1), channel_id=1, source_target_pairs={{0,1},{1,0},{2,3},{3,2},{4,5},{5,4},{6,7},{7,6},{8,9},{9,8},{10,11... | collective-permute-start | bytes 3145736 | tf_op jit(solution)/shard_map/ppermute | solution.py:807
  106.4 5.4 %collective-permute-start.23 = (bf16[512,1024]{1,0:T(8,128)(2,1)}, bf16[512,1024]{1,0:T(8,128)(2,1)S(1)}, u32[]{:S(2)}, u32[]{:S(2)}) collective-permute-start(bf16[512,1024]{1,0:T(8,128)(2,1)} %collective-permute-done.22.refs_18_), channel_id=1, source_target_pairs={{0,1},{1,0},{2,3},{3,2},{4,5},{5,4},{6,7},{7,6},{8,9},{9,8},{10,11... | collective-permute-start | bytes 3145736 | tf_op jit(solution)/shard_map/ppermute | solution.py:807
  107.8 4.0 %collective-permute-start.25 = (bf16[512,1024]{1,0:T(8,128)(2,1)S(1)}, bf16[512,1024]{1,0:T(8,128)(2,1)S(1)}, u32[]{:S(2)}, u32[]{:S(2)}) collective-permute-start(bf16[512,1024]{1,0:T(8,128)(2,1)S(1)} %collective-permute-done.24.refs_20_), channel_id=1, source_target_pairs={{0,1},{1,0},{2,3},{3,2},{4,5},{5,4},{6,7},{7,6},{8,9},{9,8},{10,11... | collective-permute-start | bytes 3145736 | tf_op jit(solution)/shard_map/ppermute | solution.py:807
  107.8 5.3 %collective-permute-start.27 = (bf16[512,1024]{1,0:T(8,128)(2,1)S(1)}, bf16[512,1024]{1,0:T(8,128)(2,1)S(1)}, u32[]{:S(2)}, u32[]{:S(2)}) collective-permute-start(bf16[512,1024]{1,0:T(8,128)(2,1)S(1)} %collective-permute-done.26.refs_22_), channel_id=1, source_target_pairs={{0,1},{1,0},{2,3},{3,2},{4,5},{5,4},{6,7},{7,6},{8,9},{9,8},{10,11... | collective-permute-start | bytes 3145736 | tf_op jit(solution)/shard_map/ppermute | solution.py:807
  195.8 4.1 %collective-permute-start.31 = (f32[16,1024]{1,0:T(8,128)S(1)}, f32[16,1024]{1,0:T(8,128)S(1)}, u32[]{:S(2)}, u32[]{:S(2)}) collective-permute-start(f32[16,1024]{1,0:T(8,128)S(1)} %add.30), channel_id=1, source_target_pairs={{0,6},{1,7},{2,4},{3,5},{4,2},{5,3},{6,0},{7,1},{8,14},{9,15},{10,... | collective-permute-start | bytes 196616 | tf_op jit(solution)/shard_map/ppermute | solution.py:807
  197.1 5.0 %collective-permute-start.30 = (f32[16,1024]{1,0:T(8,128)S(1)}, f32[16,1024]{1,0:T(8,128)S(1)}, u32[]{:S(2)}, u32[]{:S(2)}) collective-permute-start(f32[16,1024]{1,0:T(8,128)S(1)} %add.30), channel_id=1, source_target_pairs={{0,4},{1,5},{2,6},{3,7},{4,0},{5,1},{6,2},{7,3},{8,12},{9,13},{10,... | collective-permute-start | bytes 196616 | tf_op jit(solution)/shard_map/ppermute | solution.py:807
  197.3 4.8 %collective-permute-start.29 = (f32[16,1024]{1,0:T(8,128)S(1)}, f32[16,1024]{1,0:T(8,128)S(1)}, u32[]{:S(2)}, u32[]{:S(2)}) collective-permute-start(f32[16,1024]{1,0:T(8,128)S(1)} %add.30), channel_id=1, source_target_pairs={{0,2},{1,3},{2,0},{3,1},{4,6},{5,7},{6,4},{7,5},{8,10},{9,11},{10,... | collective-permute-start | bytes 196616 | tf_op jit(solution)/shard_map/ppermute | solution.py:807
  202.2 18.4 %collective-permute-start.34 = (f32[16,1024]{1,0:T(8,128)S(1)}, f32[16,1024]{1,0:T(8,128)S(1)}, u32[]{:S(2)}, u32[]{:S(2)}) collective-permute-start(f32[16,1024]{1,0:T(8,128)S(1)} %add_add_fusion.1), channel_id=1, source_target_pairs={{0,24},{1,25},{2,26},{3,27},{4,28},{5,29},{6,30},{7,31},{8,16},{9,... | collective-permute-start | bytes 196616 | tf_op jit(solution)/shard_map/ppermute | solution.py:807
  204.5 16.1 %collective-permute-start.33 = (f32[16,1024]{1,0:T(8,128)S(1)}, f32[16,1024]{1,0:T(8,128)S(1)}, u32[]{:S(2)}, u32[]{:S(2)}) collective-permute-start(f32[16,1024]{1,0:T(8,128)S(1)} %add_add_fusion.1), channel_id=1, source_target_pairs={{0,16},{1,17},{2,18},{3,19},{4,20},{5,21},{6,22},{7,23},{8,24},{9,... | collective-permute-start | bytes 196616 | tf_op jit(solution)/shard_map/ppermute | solution.py:807
  204.6 16.0 %collective-permute-start.32 = (f32[16,1024]{1,0:T(8,128)S(1)}, f32[16,1024]{1,0:T(8,128)S(1)}, u32[]{:S(2)}, u32[]{:S(2)}) collective-permute-start(f32[16,1024]{1,0:T(8,128)S(1)} %add_add_fusion.1), channel_id=1, source_target_pairs={{0,8},{1,9},{2,10},{3,11},{4,12},{5,13},{6,14},{7,15},{8,0},{9,1},... | collective-permute-start | bytes 196616 | tf_op jit(solution)/shard_map/ppermute | solution.py:807
  (22 other events, 152.1 us)

commit v5 on v4

--- a/solution.py
+++ b/solution.py
@@ -479,7 +479,7 @@
     fcs, refs = split_list(refs, count, halves[0])
     outs, refs = split_list(refs, count, halves[1])
     (pre_ref, hidden_ref, cot_ref, gain_ref, block_ref, gh_ref, ga_ref,
-     wproj, fbuf, obuf, pbuf, hidden, cbuf, low, acc, back, block, gatt, sem, fsem, lsem, wsem) = refs
+     wproj, fbuf, obuf, pbuf, hidden, cbuf, low, acc, back, block, gatt, grads, sem, fsem, lsem, wsem) = refs
     step = pl.program_id(0)
     size, width = low.shape
     slot = lax.rem(step, 2)
@@ -552,10 +552,10 @@
 
     def body(i, carry):
         at = pl.ds(pl.multiple_of(i * ROWS, ROWS), ROWS)
+        down = dot_nt(low[at, :], obuf[slot])
         act, slope = gelu_both(pbuf[slot, at, :])
         acc[at, :] += dot(act.astype(BF), obuf[slot])
-        grad = (dot_nt(low[at, :], obuf[slot]) * slope).astype(BF)
-        back[at, :] += dot_nt(grad, fbuf[slot])
+        back[at, :] += dot_nt((down * slope).astype(BF), fbuf[slot])
         return carry
 
     lax.fori_loop(0, size // ROWS, body, 0)
@@ -572,7 +572,7 @@
                 pltpu.make_async_copy(gatt.at[at, :], ga_ref.at[at, :], wsem),
             ]
 
-        def finish(i, carry):
+        def grad(i):
             at = pl.ds(pl.multiple_of(i * BLOCK, BLOCK), BLOCK)
             h = hidden[at, :]
             keep = row((BLOCK, 1)) + i * BLOCK < len_ref[0]
@@ -580,13 +580,29 @@
             xhat, inv = norm_stats(h)
             gh = low[at, :].astype(F32) + norm_back(xhat, inv, gain_ref[...] * back[at, :])
             hidden[at, :] = gh
-            gatt[at, :] = dot_nt(gh.astype(BF), wproj[...]).astype(BF)
+            return gh.astype(BF)
+
+        def product(i, gh):
+            at = pl.ds(pl.multiple_of(i * BLOCK, BLOCK), BLOCK)
+            gatt[at, :] = dot_nt(gh, wproj[...]).astype(BF)
             for c in out_copies(i):
                 c.start()
+
+        def finish(i, carry):
+            last = grads[...]
+            at = pl.ds(pl.multiple_of((i - 1) * BLOCK, BLOCK), BLOCK)
+            made = dot_nt(last, wproj[...]).astype(BF)
+            grads[...] = grad(i)
+            gatt[at, :] = made
+            for c in out_copies(i - 1):
+                c.start()
             return carry
 
-        lax.fori_loop(0, size // BLOCK, finish, 0)
-        for i in range(size // BLOCK):
+        blocks = size // BLOCK
+        grads[...] = grad(0)
+        lax.fori_loop(1, blocks, finish, 0)
+        product(blocks - 1, grads[...])
+        for i in range(blocks):
             for c in out_copies(i):
                 c.wait()
 
@@ -617,6 +633,7 @@
             pltpu.VMEM((size, width), F32),
             pltpu.VMEM((size, width), BF),
             pltpu.VMEM((size, width), BF),
+            pltpu.VMEM((BLOCK, width), BF),
             pltpu.SemaphoreType.DMA((2,)),
             pltpu.SemaphoreType.DMA((2,)),
             pltpu.SemaphoreType.DMA((2,)),
@@ -747,51 +764,69 @@
     for count in counts:
         shards.append(refs[:count])
         refs = refs[count:]
-    (dq_ref, dk_ref, dv_ref, joint_ref, down_ref, gh_ref, x_ref, gain_ref, o_ref, wbuf, sem) = refs
+    (dq_ref, dk_ref, dv_ref, joint_ref, down_ref, gh_ref, x_ref, gain_ref, o_ref,
+     wbuf, made, sem) = refs
     step = pl.program_id(0)
+    last = pl.num_programs(0) - 1
     pieces = [(j, q) for j in range(len(counts)) for q in range(quads[j])]
 
     def copies(s):
         j, q = pieces[s]
         return qkv_copies(index_ref, shards[j], wbuf.at[s], sem.at[s], q)
 
+    def product(first):
+        total = dot_tn(joint_ref[...], down_ref[...])
+        for s in range(len(pieces)):
+            if first:
+                for c in copies(s):
+                    c.wait()
+            cols = slice(s * QUAD, (s + 1) * QUAD)
+            g = jnp.concatenate([ref[:, cols] for ref in (dq_ref, dk_ref, dv_ref)], axis=1)
+            total = total + dot_nt(g, wbuf[s])
+        return total
+
+    def finish(total):
+        xhat, inv = norm_stats(x_ref[...].astype(F32))
+        o_ref[...] = (gh_ref[...] + norm_back(xhat, inv, gain_ref[...] * total)).astype(BF)
+
     @pl.when(step == 0)
     def _():
         for s in range(len(pieces)):
             for c in copies(s):
                 c.start()
-
-    total = dot_tn(joint_ref[...], down_ref[...])
-    for s in range(len(pieces)):
-
-        @pl.when(step == 0)
-        def _(s=s):
-            for c in copies(s):
-                c.wait()
-
-        cols = slice(s * QUAD, (s + 1) * QUAD)
-        g = jnp.concatenate([ref[:, cols] for ref in (dq_ref, dk_ref, dv_ref)], axis=1)
-        total = total + dot_nt(g, wbuf[s])
-    xhat, inv = norm_stats(x_ref[...].astype(F32))
-    o_ref[...] = (gh_ref[...] + norm_back(xhat, inv, gain_ref[...] * total)).astype(BF)
+        made[...] = product(True)
+
+    @pl.when((step > 0) & (step < last))
+    def _():
+        held = made[...]
+        total = product(False)
+        finish(held)
+        made[...] = total
+
+    @pl.when(step == last)
+    def _():
+        finish(made[...])
 
 
 def token_gradient(index, shards, quads, dq, dk, dv, joint, down, gh, x, gain):
     size, width = x.shape
     flat = [s for part in shards for s in part]
-    block = pl.BlockSpec((BLOCK, width), lambda i: (i, 0))
+    blocks = size // BLOCK
+    ahead = pl.BlockSpec((BLOCK, width), lambda i: (jnp.minimum(i, blocks - 1), 0))
+    behind = pl.BlockSpec((BLOCK, width), lambda i: (jnp.maximum(i - 1, 0), 0))
+    narrow = pl.BlockSpec((PAD, BLOCK), lambda i: (0, jnp.minimum(i, blocks - 1)))
     return pl.pallas_call(
         functools.partial(token_kernel, [len(p) for p in shards], quads),
-        grid=(size // BLOCK,),
+        grid=(blocks + 1,),
         in_specs=[SMEM]
         + [ANY] * len(flat)
-        + [block] * 3
-        + [pl.BlockSpec((PAD, BLOCK), lambda i: (0, i)), whole((PAD, width))]
-        + [block, block, whole((1, width))],
-        out_specs=block,
+        + [ahead] * 3
+        + [narrow, whole((PAD, width)), behind, behind, whole((1, width))],
+        out_specs=behind,
         out_shape=jax.ShapeDtypeStruct((size, width), BF),
         scratch_shapes=[
             pltpu.VMEM((sum(quads), width, 3 * QUAD), BF),
+            pltpu.VMEM((BLOCK, width), F32),
             pltpu.SemaphoreType.DMA((sum(quads),)),
         ],
         compiler_params=params(),
@@ -901,17 +936,18 @@
         af = after(af, kept[0])
         bf, cf = cube.second(af)
         n2 = after(n, af)
+        pair_af = cube.pair(af)
         kept = attend(second, n=n2, quads=low, here=half, kept=kept)
-        af = after(af, kept[0])
         bf, cf = after(bf, kept[0]), after(cf, kept[0])
-        fcs = [cube.all(ownf, *map(cube.pair, (af, bf, cf)))]
+        fcs = [cube.all(ownf, pair_af, *map(cube.pair, (bf, cf)))]
         ao = after(ao, kept[0])
         bo, co = cube.second(ao)
         o, qx, q, k, v = kept
         o_late = after(o, ao)
+        pair_ao = cube.pair(ao)
         pre, hidden = rise(index, second, col, fcs, o_late, x, gain_two[None], shift_two[None])
-        ao, bo, co = after(ao, hidden), after(bo, hidden), after(co, hidden)
-        outs = [cube.all(owno, *map(cube.pair, (ao, bo, co)))]
+        bo, co = after(bo, hidden), after(co, hidden)
+        outs = [cube.all(owno, pair_ao, *map(cube.pair, (bo, co)))]
     else:
         index = jnp.zeros((1,), jnp.int32)
         first, second, fcs, outs = [

time: 223 us -> 220 us (0.987)
  no operation moved by 1% of the time
where the time goes in v5:
time: 220 us; the launch traced here: 218 us
  Pallas kernels  154 us (70%)
  starting transfers between devices  36.8 us (17%)
  waiting for transfers between devices  20.8 us (9%)
  local copies, waits for them, and re-layouts  3.74 us (2%)
    pallas_call x1, Pallas kernels, fall(): pl.pallas_call(functools.partial(fall_kernel, len(projs), (len(fcs), len(...  42.6 us
    ppermute x35, starting transfers between devices, swap(): return lax.ppermute(value, BOTH, [(i, fn(i)) for i in range(total)])  36.8 us
    pallas_call x1, Pallas kernels, attention_backward(): pl.pallas_call(backward_kernel, grid=(width // PAIR,), in_specs=[SMEM, pl...  35.4 us
    pallas_call x3, Pallas kernels, attention_forward(): pl.pallas_call(functools.partial(forward_kernel, len(shards), len(kept),...  34.5 us
    ppermute x35, waiting for transfers between devices, swap(): return lax.ppermute(value, BOTH, [(i, fn(i)) for i in range(total)])  20.8 us
    pallas_call x1, Pallas kernels, rise(): pl.pallas_call(functools.partial(rise_kernel, len(projs), len(fcs), col),...  20.6 us
    pallas_call x1, Pallas kernels, token_gradient(): pl.pallas_call(functools.partial(token_kernel, [len(p) for p in shards],...  14.2 us
    pallas_call x1, Pallas kernels, norm_one(): pl.pallas_call(norm_one_kernel, grid=(length // BLOCK,), in_specs=[pl.Blo...  4.53 us
  transfers between devices with their start and end apart: 35, of which 12 were waited for; matrix products, arithmetic and copies ran while one was open for 0% of the time, Pallas kernels for 34%

profile of v5, /device:TPU:1, one launch (start us, length us, event | category | flops | bytes accessed | tf_op | source)
XLA Modules:
  0.0 217.9 jit_solution(11451581931593159570)
XLA Ops:
  0.6 2.3 %repack.1 = (bf16[128,1536]{1,0:T(8,128)(2,1)}, bf16[128,2560]{1,0:T(8,128)(2,1)}) custom-call(bf16[128,3072]{1,0:T(8,128)(2,1)} %qkv_ref.1, bf16[128,1024]{1,0:T(8,128)(2,1)} %proj_ref.1), custom_call_target="tpu_custom_call" | custom-call | tf_op jit(solution)/shard_map/repack/pallas_call | solution.py:143
  2.9 2.0 collective-permute-start.3
  5.9 4.5 %norm_one.1 = (bf16[1024,1024]{1,0:T(8,128)(2,1)}, bf16[16,1024]{1,0:T(8,128)(2,1)}, bf16[16,1024]{1,0:T(8,128)(2,1)}, bf16[16,1024]{1,0:T(8,128)(2,1)}, bf16[16,1024]{1,0:T(8,128)(2,1)}) custom-call(bf16[1024,1024]{1,0:T(8,128)(2,1)} %bitcast.22, f32[1,1024]{1,0:T(1,128)} %bitcast.31, f32[1,1024]{1,0:T(1,128)} %bitcast.33, f32[4,1024]{1,0:T(4,128)} %bitcast.27, ...), custom_call_target="tpu_custom_call" | custom-call | tf_op jit(solution)/shard_map/norm_one/pallas_call | solution.py:110
  10.5 3.5 %collective-permute-done.3.refs_2_ = bf16[128,1536]{1,0:T(8,128)(2,1)S(1)} collective-permute-done((bf16[128,1536]{1,0:T(8,128)(2,1)}, bf16[128,1536]{1,0:T(8,128)(2,1)S(1)}, u32[]{:S(2)}, u32[]{:S(2)}) %collective-permute-start.3) | collective-permute-done | bytes 393248 | tf_op jit(solution)/shard_map/ppermute | solution.py:842
  14.0 1.2 collective-permute-start.7
  15.2 1.2 collective-permute-start.5
  16.5 1.2 collective-permute-start.15
  17.7 3.5 %collective-permute-start.4 = (bf16[128,1536]{1,0:T(8,128)(2,1)S(1)}, bf16[128,1536]{1,0:T(8,128)(2,1)}, u32[]{:S(2)}, u32[]{:S(2)}) collective-permute-start(bf16[128,1536]{1,0:T(8,128)(2,1)S(1)} %collective-permute-done.3.refs_2_), channel_id=1, source_target_pairs={{0,1},{1,0},{2,3},{3,2},{4,5},{5,4},{6,7},{7,6},{8,9},{9,8},{10,11... | collective-permute-start | bytes 1179656 | tf_op jit(solution)/shard_map/ppermute | solution.py:842
  21.2 1.3 collective-permute-done.7.refs_6_
  22.5 3.1 %collective-permute-start.8 = (bf16[128,1536]{1,0:T(8,128)(2,1)}, bf16[128,1536]{1,0:T(8,128)(2,1)}, u32[]{:S(2)}, u32[]{:S(2)}) collective-permute-start(bf16[128,1536]{1,0:T(8,128)(2,1)} %collective-permute-done.7.refs_6_), channel_id=1, source_target_pairs={{0,1},{1,0},{2,3},{3,2},{4,5},{5,4},{6,7},{7,6},{8,9},{9,8},{10,11... | collective-permute-start | bytes 1179656 | tf_op jit(solution)/shard_map/ppermute | solution.py:842
  25.6 1.2 collective-permute-start.6
  30.5 3.0 %collective-permute-start = (bf16[128,2560]{1,0:T(8,128)(2,1)S(1)}, bf16[128,2560]{1,0:T(8,128)(2,1)S(1)}, u32[]{:S(2)}, u32[]{:S(2)}) collective-permute-start(bf16[128,2560]{1,0:T(8,128)(2,1)S(1)} %copy-done), channel_id=1, source_target_pairs={{0,1},{1,0},{2,3},{3,2},{4,5},{5,4},{6,7},{7,6},{8,9},{9,8},{10,11... | collective-permute-start | bytes 1966088 | tf_op jit(solution)/shard_map/ppermute | solution.py:842
  33.5 1.3 collective-permute-start.12
  34.8 9.6 %attention_forward.3 = (bf16[1024,1024]{1,0:T(8,128)(2,1)}, bf16[2048,1024]{1,0:T(8,128)(2,1)}, bf16[1024,1024]{1,0:T(8,128)(2,1)}, bf16[1024,1024]{1,0:T(8,128)(2,1)}, bf16[1024,1024]{1,0:T(8,128)(2,1)}) custom-call(s32[1]{0:T(128)S(6)} %copy.41.len_ref, s32[8]{0:T(128)} %stack.35.index_ref, bf16[128,1536]{1,0:T(8,128)(2,1)} %get-tuple-element.52.refs_0_, ...), custom_call_target="tpu_custom_call" | custom-call | flops 1000 | bytes 1000 | tf_op jit(solution)/shard_map/attention_forward/pallas_call | solution.py:288
  44.4 9.7 %attention_forward.4 = (bf16[1024,1024]{1,0:T(8,128)(2,1)}, bf16[2048,1024]{1,0:T(8,128)(2,1)}, bf16[1024,1024]{1,0:T(8,128)(2,1)}, bf16[1024,1024]{1,0:T(8,128)(2,1)}, bf16[1024,1024]{1,0:T(8,128)(2,1)}) custom-call(s32[1]{0:T(128)S(6)} %copy.41.len_ref, ...), custom_call_target="tpu_custom_call", output_to_operand_aliasing={{0}: (10, {}), {1}: (11, {}), {2}: (12, {}), {3}: (13, {}),... | custom-call | flops 1000 | bytes 1000 | tf_op jit(solution)/shard_map/attention_forward/pallas_call | solution.py:288
  57.6 3.1 %collective-permute-done.13.refs_7_.refs_15_ = bf16[128,2560]{1,0:T(8,128)(2,1)S(1)} collective-permute-done((bf16[128,2560]{1,0:T(8,128)(2,1)S(1)}, bf16[128,2560]{1,0:T(8,128)(2,1)S(1)}, u32[]{:S(2)}, u32[]{:S(2)}) %collective-permute-start.13) | collective-permute-done | bytes 655392 | tf_op jit(solution)/shard_map/ppermute | solution.py:842
  61.6 15.2 %attention_forward.5 = (bf16[1024,1024]{1,0:T(8,128)(2,1)}, bf16[2048,1024]{1,0:T(8,128)(2,1)}, bf16[1024,1024]{1,0:T(8,128)(2,1)}, bf16[1024,1024]{1,0:T(8,128)(2,1)}, bf16[1024,1024]{1,0:T(8,128)(2,1)}) custom-call(s32[1]{0:T(128)S(6)} %copy.41.len_ref, ...), custom_call_target="tpu_custom_call", output_to_operand_aliasing={{0}: (10, {}), {1}: (11, {}), {2}: (12, {}), {3}: (13, {}),... | custom-call | flops 1000 | bytes 1000 | tf_op jit(solution)/shard_map/attention_forward/pallas_call | solution.py:288
  76.8 2.5 %collective-permute-done.19.refs_14_ = bf16[128,4096]{1,0:T(8,128)(2,1)} collective-permute-done((bf16[128,4096]{1,0:T(8,128)(2,1)}, bf16[128,4096]{1,0:T(8,128)(2,1)}, u32[]{:S(2)}, u32[]{:S(2)}) %collective-permute-start.19) | collective-permute-done | bytes 1048608 | tf_op jit(solution)/shard_map/ppermute | solution.py:842
  80.8 1.3 collective-permute-start.26
  82.0 1.2 collective-permute-start.24
  85.6 20.6 %rise.1 = (f32[4,1024,1024]{2,1,0:T(8,128)}, f32[1024,1024]{1,0:T(8,128)}) custom-call(s32[8]{0:T(128)} %stack.35.index_ref, bf16[128,2560]{1,0:T(8,128)(2,1)} %get-tuple-element.51.refs_0_.refs_8_, bf16[128,2560]{1,0:T(8,128)(2,1)} %copy-done.3, bf16[128,2560]{1,0:T(8,128)(2,1)} %copy-done.1, bf16[128,2560]{1,0:T(8,128)(2,1)} %copy-done.5, ...), custom_call_target="tpu_custom_call" | custom-call | flops 1000 | bytes 1000 | tf_op jit(solution)/shard_map/rise/pallas_call | solution.py:450
  106.4 1.4 collective-permute-start.25
  107.8 2.3 %collective-permute-done.25.refs_21_ = bf16[512,1024]{1,0:T(8,128)(2,1)S(1)} collective-permute-done((bf16[512,1024]{1,0:T(8,128)(2,1)S(1)}, bf16[512,1024]{1,0:T(8,128)(2,1)S(1)}, u32[]{:S(2)}, u32[]{:S(2)}) %collective-permute-start.25) | collective-permute-done | bytes 1048608 | tf_op jit(solution)/shard_map/ppermute | solution.py:842
  110.1 1.5 collective-permute-done.27.refs_23_
  112.6 42.6 %fall.1 = (bf16[1024,1024]{1,0:T(8,128)(2,1)}, f32[1024,1024]{1,0:T(8,128)}, bf16[1024,1024]{1,0:T(8,128)(2,1)}) custom-call(s32[1]{0:T(128)S(6)} %copy.41.len_ref, s32[8]{0:T(128)} %stack.35.index_ref, bf16[128,2560]{1,0:T(8,128)(2,1)} %get-tuple-element.51.refs_0_.refs_8_, bf16[128,2560]{1,0:T(8,128)(2,1)} %copy-done.3, bf16[128,2560]{1,0:T(8,128)(2,1)} %copy-done.1, ...), custom_call_target="tpu_custom_call" | custom-call | flops 1000 | bytes 1000 | tf_op jit(solution)/shard_map/fall/pallas_call | solution.py:614
  155.2 35.4 %attention_backward.1 = (bf16[1024,1024]{1,0:T(8,128)(2,1)}, bf16[1024,1024]{1,0:T(8,128)(2,1)}, bf16[1024,1024]{1,0:T(8,128)(2,1)}, bf16[16,1024]{1,0:T(8,128)(2,1)}, f32[16,1024]{1,0:T(8,128)}) custom-call(s32[1]{0:T(128)S(6)} %copy.41.len_ref, bf16[2048,1024]{1,0:T(8,128)(2,1)} %get-tuple-element.84.qx_ref, bf16[1024,1024]{1,0:T(8,128)(2,1)} %get-tuple-element.85.q_ref, ...), custom_call_target="tpu_custom_call" | custom-call | flops 1000 | bytes 1000 | tf_op jit(solution)/shard_map/attention_backward/pallas_call | solution.py:741
  193.0 1.3 collective-permute-start.31
  194.5 1.2 collective-permute-start.29
  195.7 1.4 collective-permute-done.31
  197.1 2.2 %collective-permute-done.30 = f32[16,1024]{1,0:T(8,128)S(1)} collective-permute-done((f32[16,1024]{1,0:T(8,128)S(1)}, f32[16,1024]{1,0:T(8,128)S(1)}, u32[]{:S(2)}, u32[]{:S(2)}) %collective-permute-start.30) | collective-permute-done | bytes 65568 | tf_op jit(solution)/shard_map/ppermute | solution.py:842
  199.3 2.3 %collective-permute-start.34 = (f32[16,1024]{1,0:T(8,128)S(1)}, f32[16,1024]{1,0:T(8,128)S(1)}, u32[]{:S(2)}, u32[]{:S(2)}) collective-permute-start(f32[16,1024]{1,0:T(8,128)S(1)} %add_add_fusion.1), channel_id=1, source_target_pairs={{0,24},{1,25},{2,26},{3,27},{4,28},{5,29},{6,30},{7,31},{8,16},{9,... | collective-permute-start | bytes 196616 | tf_op jit(solution)/shard_map/ppermute | solution.py:842
  203.0 14.2 %token_gradient.1 = bf16[1024,1024]{1,0:T(8,128)(2,1)} custom-call(s32[8]{0:T(128)} %stack.35.index_ref, bf16[128,1536]{1,0:T(8,128)(2,1)} %get-tuple-element.52.refs_0_, bf16[128,1536]{1,0:T(8,128)(2,1)} %copy-done.12, bf16[128,1536]{1,0:T(8,128)(2,1)} %copy-done.11, bf16[128,1536]{1,0:T(8,128)(2,1)} %collective-permute-done.4.refs_3_, ...), custom_call_target="tpu_custom_call" | custom-call | flops 1000 | bytes 1000 | tf_op jit(solution)/shard_map/token_gradient/pallas_call | solution.py:818
  (88 shorter events, 17.8 us)
Async XLA Ops:
  2.9 11.1 %collective-permute-start.3 = (bf16[128,1536]{1,0:T(8,128)(2,1)}, bf16[128,1536]{1,0:T(8,128)(2,1)S(1)}, u32[]{:S(2)}, u32[]{:S(2)}) collective-permute-start(bf16[128,1536]{1,0:T(8,128)(2,1)} %get-tuple-element.52.refs_0_), channel_id=1, source_target_pairs={{0,2},{1,3},{2,0},{3,1},{4,6},{5,7},{6,4},{7,5},{8,12},{9,13},{10,... | collective-permute-start | bytes 1179656 | tf_op jit(solution)/shard_map/ppermute | solution.py:842
  5.0 23.1 %collective-permute-start.1 = (bf16[128,2560]{1,0:T(8,128)(2,1)}, bf16[128,2560]{1,0:T(8,128)(2,1)S(1)}, u32[]{:S(2)}, u32[]{:S(2)}) collective-permute-start(bf16[128,2560]{1,0:T(8,128)(2,1)} %get-tuple-element.51.refs_0_.refs_8_), channel_id=1, source_target_pairs={{0,2},{1,3},{2,0},{3,1},{4,6},{5,7},{6,4},{7,5},{8,12},{9,13},{10,... | collective-permute-start | bytes 1966088 | tf_op jit(solution)/shard_map/ppermute | solution.py:842
  5.0 12.7 %collective-permute-start.2 = (bf16[128,1536]{1,0:T(8,128)(2,1)}, bf16[128,1536]{1,0:T(8,128)(2,1)S(1)}, u32[]{:S(2)}, u32[]{:S(2)}) collective-permute-start(bf16[128,1536]{1,0:T(8,128)(2,1)} %get-tuple-element.52.refs_0_), channel_id=1, source_target_pairs={{0,1},{1,0},{2,3},{3,2},{4,5},{5,4},{6,7},{7,6},{8,9},{9,8},{10,11... | collective-permute-start | bytes 1179656 | tf_op jit(solution)/shard_map/ppermute | solution.py:842
  14.0 8.5 %collective-permute-start.7 = (bf16[128,1536]{1,0:T(8,128)(2,1)S(1)}, bf16[128,1536]{1,0:T(8,128)(2,1)}, u32[]{:S(2)}, u32[]{:S(2)}) collective-permute-start(bf16[128,1536]{1,0:T(8,128)(2,1)S(1)} %collective-permute-done.3.refs_2_), channel_id=1, source_target_pairs={{0,8},{1,9},{2,10},{3,11},{4,12},{5,13},{6,14},{7,15},{8,0},{9,1},... | collective-permute-start | bytes 1179656 | tf_op jit(solution)/shard_map/ppermute | solution.py:842
  15.2 10.4 %collective-permute-start.5 = (bf16[128,1536]{1,0:T(8,128)(2,1)S(1)}, bf16[128,1536]{1,0:T(8,128)(2,1)}, u32[]{:S(2)}, u32[]{:S(2)}) collective-permute-start(bf16[128,1536]{1,0:T(8,128)(2,1)S(1)} %collective-permute-done.3.refs_2_), channel_id=1, source_target_pairs={{0,4},{1,5},{2,6},{3,7},{4,0},{5,1},{6,2},{7,3},{8,10},{9,11},{10,... | collective-permute-start | bytes 1179656 | tf_op jit(solution)/shard_map/ppermute | solution.py:842
  16.5 38.2 %collective-permute-start.15 = (bf16[128,4096]{1,0:T(8,128)(2,1)S(1)}, bf16[128,4096]{1,0:T(8,128)(2,1)}, u32[]{:S(2)}, u32[]{:S(2)}) collective-permute-start(bf16[128,4096]{1,0:T(8,128)(2,1)S(1)} %copy-done.8), channel_id=1, source_target_pairs={{0,2},{1,3},{2,0},{3,1},{4,6},{5,7},{6,4},{7,5},{8,12},{9,13},{10,... | collective-permute-start | bytes 3145736 | tf_op jit(solution)/shard_map/ppermute | solution.py:842
  17.7 12.8 %collective-permute-start.4 = (bf16[128,1536]{1,0:T(8,128)(2,1)S(1)}, bf16[128,1536]{1,0:T(8,128)(2,1)}, u32[]{:S(2)}, u32[]{:S(2)}) collective-permute-start(bf16[128,1536]{1,0:T(8,128)(2,1)S(1)} %collective-permute-done.3.refs_2_), channel_id=1, source_target_pairs={{0,1},{1,0},{2,3},{3,2},{4,5},{5,4},{6,7},{7,6},{8,9},{9,8},{10,11... | collective-permute-start | bytes 1179656 | tf_op jit(solution)/shard_map/ppermute | solution.py:842
  22.5 10.9 %collective-permute-start.8 = (bf16[128,1536]{1,0:T(8,128)(2,1)}, bf16[128,1536]{1,0:T(8,128)(2,1)}, u32[]{:S(2)}, u32[]{:S(2)}) collective-permute-start(bf16[128,1536]{1,0:T(8,128)(2,1)} %collective-permute-done.7.refs_6_), channel_id=1, source_target_pairs={{0,1},{1,0},{2,3},{3,2},{4,5},{5,4},{6,7},{7,6},{8,9},{9,8},{10,11... | collective-permute-start | bytes 1179656 | tf_op jit(solution)/shard_map/ppermute | solution.py:842
  25.6 9.1 %collective-permute-start.6 = (bf16[128,1536]{1,0:T(8,128)(2,1)}, bf16[128,1536]{1,0:T(8,128)(2,1)}, u32[]{:S(2)}, u32[]{:S(2)}) collective-permute-start(bf16[128,1536]{1,0:T(8,128)(2,1)} %collective-permute-done.5.refs_4_), channel_id=1, source_target_pairs={{0,1},{1,0},{2,3},{3,2},{4,5},{5,4},{6,7},{7,6},{8,9},{9,8},{10,11... | collective-permute-start | bytes 1179656 | tf_op jit(solution)/shard_map/ppermute | solution.py:842
  28.1 26.4 %collective-permute-start.10 = (bf16[128,2560]{1,0:T(8,128)(2,1)S(1)}, bf16[128,2560]{1,0:T(8,128)(2,1)S(1)}, u32[]{:S(2)}, u32[]{:S(2)}) collective-permute-start(bf16[128,2560]{1,0:T(8,128)(2,1)S(1)} %collective-permute-done.1.refs_2_.refs_10_), channel_id=1, source_target_pairs={{0,4},{1,5},{2,6},{3,7},{4,0},{5,1},{6,2},{7,3},{8,10},{9,11},{10,... | collective-permute-start | bytes 1966088 | tf_op jit(solution)/shard_map/ppermute | solution.py:842
  30.5 24.4 %collective-permute-start = (bf16[128,2560]{1,0:T(8,128)(2,1)S(1)}, bf16[128,2560]{1,0:T(8,128)(2,1)S(1)}, u32[]{:S(2)}, u32[]{:S(2)}) collective-permute-start(bf16[128,2560]{1,0:T(8,128)(2,1)S(1)} %copy-done), channel_id=1, source_target_pairs={{0,1},{1,0},{2,3},{3,2},{4,5},{5,4},{6,7},{7,6},{8,9},{9,8},{10,11... | collective-permute-start | bytes 1966088 | tf_op jit(solution)/shard_map/ppermute | solution.py:842
  33.5 22.5 %collective-permute-start.12 = (bf16[128,2560]{1,0:T(8,128)(2,1)S(1)}, bf16[128,2560]{1,0:T(8,128)(2,1)S(1)}, u32[]{:S(2)}, u32[]{:S(2)}) collective-permute-start(bf16[128,2560]{1,0:T(8,128)(2,1)S(1)} %collective-permute-done.1.refs_2_.refs_10_), channel_id=1, source_target_pairs={{0,8},{1,9},{2,10},{3,11},{4,12},{5,13},{6,14},{7,15},{8,0},{9,1},... | collective-permute-start | bytes 1966088 | tf_op jit(solution)/shard_map/ppermute | solution.py:842
  54.7 24.7 %collective-permute-start.19 = (bf16[128,4096]{1,0:T(8,128)(2,1)}, bf16[128,4096]{1,0:T(8,128)(2,1)}, u32[]{:S(2)}, u32[]{:S(2)}) collective-permute-start(bf16[128,4096]{1,0:T(8,128)(2,1)} %collective-permute-done.15.refs_10_), channel_id=1, source_target_pairs={{0,8},{1,9},{2,10},{3,11},{4,12},{5,13},{6,14},{7,15},{8,0},{9,1},... | collective-permute-start | bytes 3145736 | tf_op jit(solution)/shard_map/ppermute | solution.py:842
  54.9 25.7 %collective-permute-start.17 = (bf16[128,4096]{1,0:T(8,128)(2,1)}, bf16[128,4096]{1,0:T(8,128)(2,1)}, u32[]{:S(2)}, u32[]{:S(2)}) collective-permute-start(bf16[128,4096]{1,0:T(8,128)(2,1)} %collective-permute-done.15.refs_10_), channel_id=1, source_target_pairs={{0,4},{1,5},{2,6},{3,7},{4,0},{5,1},{6,2},{7,3},{8,10},{9,11},{10,... | collective-permute-start | bytes 3145736 | tf_op jit(solution)/shard_map/ppermute | solution.py:842
  56.0 24.8 %collective-permute-start.22 = (bf16[512,1024]{1,0:T(8,128)(2,1)}, bf16[512,1024]{1,0:T(8,128)(2,1)}, u32[]{:S(2)}, u32[]{:S(2)}) collective-permute-start(bf16[512,1024]{1,0:T(8,128)(2,1)} %refs_16_.1), channel_id=1, source_target_pairs={{0,2},{1,3},{2,0},{3,1},{4,6},{5,7},{6,4},{7,5},{8,12},{9,13},{10,... | collective-permute-start | bytes 3145736 | tf_op jit(solution)/shard_map/ppermute | solution.py:842
  56.3 25.7 %collective-permute-start.14 = (bf16[128,4096]{1,0:T(8,128)(2,1)S(1)}, bf16[128,4096]{1,0:T(8,128)(2,1)}, u32[]{:S(2)}, u32[]{:S(2)}) collective-permute-start(bf16[128,4096]{1,0:T(8,128)(2,1)S(1)} %copy-done.8), channel_id=1, source_target_pairs={{0,1},{1,0},{2,3},{3,2},{4,5},{5,4},{6,7},{7,6},{8,9},{9,8},{10,11... | collective-permute-start | bytes 3145736 | tf_op jit(solution)/shard_map/ppermute | solution.py:842
  57.5 3.2 %collective-permute-start.13 = (bf16[128,2560]{1,0:T(8,128)(2,1)S(1)}, bf16[128,2560]{1,0:T(8,128)(2,1)S(1)}, u32[]{:S(2)}, u32[]{:S(2)}) collective-permute-start(bf16[128,2560]{1,0:T(8,128)(2,1)S(1)} %collective-permute-done.12.refs_6_.refs_14_), channel_id=1, source_target_pairs={{0,1},{1,0},{2,3},{3,2},{4,5},{5,4},{6,7},{7,6},{8,9},{9,8},{10,11... | collective-permute-start | bytes 1966088 | tf_op jit(solution)/shard_map/ppermute | solution.py:842
  60.7 22.6 %collective-permute-start.16 = (bf16[128,4096]{1,0:T(8,128)(2,1)}, bf16[128,4096]{1,0:T(8,128)(2,1)}, u32[]{:S(2)}, u32[]{:S(2)}) collective-permute-start(bf16[128,4096]{1,0:T(8,128)(2,1)} %collective-permute-done.15.refs_10_), channel_id=1, source_target_pairs={{0,1},{1,0},{2,3},{3,2},{4,5},{5,4},{6,7},{7,6},{8,9},{9,8},{10,11... | collective-permute-start | bytes 3145736 | tf_op jit(solution)/shard_map/ppermute | solution.py:842
  79.4 4.7 %collective-permute-start.20 = (bf16[128,4096]{1,0:T(8,128)(2,1)}, bf16[128,4096]{1,0:T(8,128)(2,1)S(1)}, u32[]{:S(2)}, u32[]{:S(2)}) collective-permute-start(bf16[128,4096]{1,0:T(8,128)(2,1)} %collective-permute-done.19.refs_14_), channel_id=1, source_target_pairs={{0,1},{1,0},{2,3},{3,2},{4,5},{5,4},{6,7},{7,6},{8,9},{9,8},{10,11... | collective-permute-start | bytes 3145736 | tf_op jit(solution)/shard_map/ppermute | solution.py:842
  80.6 4.0 %collective-permute-start.18 = (bf16[128,4096]{1,0:T(8,128)(2,1)}, bf16[128,4096]{1,0:T(8,128)(2,1)S(1)}, u32[]{:S(2)}, u32[]{:S(2)}) collective-permute-start(bf16[128,4096]{1,0:T(8,128)(2,1)} %collective-permute-done.17.refs_12_), channel_id=1, source_target_pairs={{0,1},{1,0},{2,3},{3,2},{4,5},{5,4},{6,7},{7,6},{8,9},{9,8},{10,11... | collective-permute-start | bytes 3145736 | tf_op jit(solution)/shard_map/ppermute | solution.py:842
  80.8 25.4 %collective-permute-start.26 = (bf16[512,1024]{1,0:T(8,128)(2,1)}, bf16[512,1024]{1,0:T(8,128)(2,1)S(1)}, u32[]{:S(2)}, u32[]{:S(2)}) collective-permute-start(bf16[512,1024]{1,0:T(8,128)(2,1)} %collective-permute-done.22.refs_18_), channel_id=1, source_target_pairs={{0,8},{1,9},{2,10},{3,11},{4,12},{5,13},{6,14},{7,15},{8,0},{9,1},... | collective-permute-start | bytes 3145736 | tf_op jit(solution)/shard_map/ppermute | solution.py:842
  82.0 24.4 %collective-permute-start.24 = (bf16[512,1024]{1,0:T(8,128)(2,1)}, bf16[512,1024]{1,0:T(8,128)(2,1)S(1)}, u32[]{:S(2)}, u32[]{:S(2)}) collective-permute-start(bf16[512,1024]{1,0:T(8,128)(2,1)} %collective-permute-done.22.refs_18_), channel_id=1, source_target_pairs={{0,4},{1,5},{2,6},{3,7},{4,0},{5,1},{6,2},{7,3},{8,10},{9,11},{10,... | collective-permute-start | bytes 3145736 | tf_op jit(solution)/shard_map/ppermute | solution.py:842
  83.3 24.5 %collective-permute-start.21 = (bf16[512,1024]{1,0:T(8,128)(2,1)}, bf16[512,1024]{1,0:T(8,128)(2,1)S(1)}, u32[]{:S(2)}, u32[]{:S(2)}) collective-permute-start(bf16[512,1024]{1,0:T(8,128)(2,1)} %refs_16_.1), channel_id=1, source_target_pairs={{0,1},{1,0},{2,3},{3,2},{4,5},{5,4},{6,7},{7,6},{8,9},{9,8},{10,11... | collective-permute-start | bytes 3145736 | tf_op jit(solution)/shard_map/ppermute | solution.py:842
  84.1 23.7 %collective-permute-start.23 = (bf16[512,1024]{1,0:T(8,128)(2,1)}, bf16[512,1024]{1,0:T(8,128)(2,1)}, u32[]{:S(2)}, u32[]{:S(2)}) collective-permute-start(bf16[512,1024]{1,0:T(8,128)(2,1)} %collective-permute-done.22.refs_18_), channel_id=1, source_target_pairs={{0,1},{1,0},{2,3},{3,2},{4,5},{5,4},{6,7},{7,6},{8,9},{9,8},{10,11... | collective-permute-start | bytes 3145736 | tf_op jit(solution)/shard_map/ppermute | solution.py:842
  106.4 3.7 %collective-permute-start.25 = (bf16[512,1024]{1,0:T(8,128)(2,1)S(1)}, bf16[512,1024]{1,0:T(8,128)(2,1)S(1)}, u32[]{:S(2)}, u32[]{:S(2)}) collective-permute-start(bf16[512,1024]{1,0:T(8,128)(2,1)S(1)} %collective-permute-done.24.refs_20_), channel_id=1, source_target_pairs={{0,1},{1,0},{2,3},{3,2},{4,5},{5,4},{6,7},{7,6},{8,9},{9,8},{10,11... | collective-permute-start | bytes 3145736 | tf_op jit(solution)/shard_map/ppermute | solution.py:842
  107.8 3.8 %collective-permute-start.27 = (bf16[512,1024]{1,0:T(8,128)(2,1)S(1)}, bf16[512,1024]{1,0:T(8,128)(2,1)S(1)}, u32[]{:S(2)}, u32[]{:S(2)}) collective-permute-start(bf16[512,1024]{1,0:T(8,128)(2,1)S(1)} %collective-permute-done.26.refs_22_), channel_id=1, source_target_pairs={{0,1},{1,0},{2,3},{3,2},{4,5},{5,4},{6,7},{7,6},{8,9},{9,8},{10,11... | collective-permute-start | bytes 3145736 | tf_op jit(solution)/shard_map/ppermute | solution.py:842
  193.0 4.1 %collective-permute-start.31 = (f32[16,1024]{1,0:T(8,128)S(1)}, f32[16,1024]{1,0:T(8,128)S(1)}, u32[]{:S(2)}, u32[]{:S(2)}) collective-permute-start(f32[16,1024]{1,0:T(8,128)S(1)} %add.30), channel_id=1, source_target_pairs={{0,6},{1,7},{2,4},{3,5},{4,2},{5,3},{6,0},{7,1},{8,14},{9,15},{10,... | collective-permute-start | bytes 196616 | tf_op jit(solution)/shard_map/ppermute | solution.py:842
  194.3 5.0 %collective-permute-start.30 = (f32[16,1024]{1,0:T(8,128)S(1)}, f32[16,1024]{1,0:T(8,128)S(1)}, u32[]{:S(2)}, u32[]{:S(2)}) collective-permute-start(f32[16,1024]{1,0:T(8,128)S(1)} %add.30), channel_id=1, source_target_pairs={{0,4},{1,5},{2,6},{3,7},{4,0},{5,1},{6,2},{7,3},{8,12},{9,13},{10,... | collective-permute-start | bytes 196616 | tf_op jit(solution)/shard_map/ppermute | solution.py:842
  194.5 4.8 %collective-permute-start.29 = (f32[16,1024]{1,0:T(8,128)S(1)}, f32[16,1024]{1,0:T(8,128)S(1)}, u32[]{:S(2)}, u32[]{:S(2)}) collective-permute-start(f32[16,1024]{1,0:T(8,128)S(1)} %add.30), channel_id=1, source_target_pairs={{0,2},{1,3},{2,0},{3,1},{4,6},{5,7},{6,4},{7,5},{8,10},{9,11},{10,... | collective-permute-start | bytes 196616 | tf_op jit(solution)/shard_map/ppermute | solution.py:842
  199.3 17.9 %collective-permute-start.34 = (f32[16,1024]{1,0:T(8,128)S(1)}, f32[16,1024]{1,0:T(8,128)S(1)}, u32[]{:S(2)}, u32[]{:S(2)}) collective-permute-start(f32[16,1024]{1,0:T(8,128)S(1)} %add_add_fusion.1), channel_id=1, source_target_pairs={{0,24},{1,25},{2,26},{3,27},{4,28},{5,29},{6,30},{7,31},{8,16},{9,... | collective-permute-start | bytes 196616 | tf_op jit(solution)/shard_map/ppermute | solution.py:842
  201.6 15.6 %collective-permute-start.33 = (f32[16,1024]{1,0:T(8,128)S(1)}, f32[16,1024]{1,0:T(8,128)S(1)}, u32[]{:S(2)}, u32[]{:S(2)}) collective-permute-start(f32[16,1024]{1,0:T(8,128)S(1)} %add_add_fusion.1), channel_id=1, source_target_pairs={{0,16},{1,17},{2,18},{3,19},{4,20},{5,21},{6,22},{7,23},{8,24},{9,... | collective-permute-start | bytes 196616 | tf_op jit(solution)/shard_map/ppermute | solution.py:842
  201.8 15.4 %collective-permute-start.32 = (f32[16,1024]{1,0:T(8,128)S(1)}, f32[16,1024]{1,0:T(8,128)S(1)}, u32[]{:S(2)}, u32[]{:S(2)}) collective-permute-start(f32[16,1024]{1,0:T(8,128)S(1)} %add_add_fusion.1), channel_id=1, source_target_pairs={{0,8},{1,9},{2,10},{3,11},{4,12},{5,13},{6,14},{7,15},{8,0},{9,1},... | collective-permute-start | bytes 196616 | tf_op jit(solution)/shard_map/ppermute | solution.py:842
  (21 other events, 152.4 us)
